TPU v7x, 32 devices: a whole 2x2x4 slice. The times are simulated.
32 devices in a mesh: dp: 16 (over z, x, core), tensor: 2 (over y).
Axes of the slice: x: 2, y: 2, z: 4, core: 2. Of those that a mesh axis runs over, the one named last changes fastest.
Arguments:
- frames: bfloat16 [19200, 512], P('dp', 'tensor'), may hold values from -6 to 6
- resets: int32 [19200], P('dp'), may hold values 0 or 1
- first_gain: float32 [512], replicated, may hold values from 0.5 to 1.5
- first_shift: float32 [512], replicated, may hold values from -1 to 1
- qkv_weight: bfloat16 [3, 512, 512], P(None, None, 'tensor'), may hold values from -0.375 to 0.375
- out_weight: bfloat16 [512, 512], P('tensor'), may hold values from -0.75 to 0.75
- out_bias: float32 [512], replicated, may hold values from -1 to 1
- second_gain: float32 [512], replicated, may hold values from 0.5 to 1.5
- second_shift: float32 [512], replicated, may hold values from -1 to 1
- up_weight: bfloat16 [512, 2048], P(None, 'tensor'), may hold values from -0.25 to 0.25
- up_bias: float32 [2048], P('tensor'), may hold values from -1 to 1
- down_weight: bfloat16 [2048, 512], P('tensor'), may hold values from -0.125 to 0.125
- down_bias: float32 [512], replicated, may hold values from -1 to 1
- prior_gain: float32 [512], replicated, may hold values from 0.5 to 1.5
- prior_shift: float32 [512], replicated, may hold values from -1 to 1
- prior_weight: bfloat16 [512, 1024], P(None, 'tensor'), may hold values from -0.25 to 0.25
- prior_bias: float32 [1024], P('tensor'), may hold values from -2.5 to 2.5
- out_cotangent: bfloat16 [19200, 512], P('dp', 'tensor'), may hold values from -6 to 6
- logit_cotangent: bfloat16 [19200, 1024], P('dp', 'tensor'), may hold values from -6 to 6
Outputs:
- block_out: bfloat16 [19200, 512], P('dp', 'tensor')
- logits: float32 [19200, 1024], P('dp', 'tensor')
- grad_frames: float32 [19200, 512], P('dp', 'tensor')
- grad_first_gain: float32 [512], replicated
- grad_first_shift: float32 [512], replicated
- grad_qkv: float32 [3, 512, 512], P(None, None, 'tensor')
- grad_out_weight: float32 [512, 512], P('tensor')
- grad_out_bias: float32 [512], replicated
- grad_second_gain: float32 [512], replicated
- grad_second_shift: float32 [512], replicated
- grad_up_weight: float32 [512, 2048], P(None, 'tensor')
- grad_up_bias: float32 [2048], P('tensor')
- grad_down_weight: float32 [2048, 512], P('tensor')
- grad_down_bias: float32 [512], replicated
- grad_prior_gain: float32 [512], replicated
- grad_prior_shift: float32 [512], replicated
- grad_prior_weight: float32 [512, 1024], P(None, 'tensor')
- grad_prior_bias: float32 [1024], P('tensor')
All inputs are finite; a program needn't handle non-finite values. No bound on the sum of `resets` on one device may be relied on, other than what follows from the above.
Results may differ from a plain program's by a relative error of at most 0.012.
The roundings to bfloat16 on the way count: a program that leaves them out, or rounds other values in their place, can miss the bound.
Values may be sent and summed in bfloat16 or wider, within the bound.
No kernel may reach another device: no remote copies, remote signals or barrier semaphores. Data moves between devices by JAX's collectives and lax.ppermute only.
A program may use at most 128 MiB of HBM per device.

v0:
```python
import jax
import jax.numpy as jnp
from jax import lax
from jax.sharding import PartitionSpec as P

HEAD_DIM = 64
SEQ_LEN = 50


EPS = 1e-05
NEG = -1e30


def own_part(value, size, axis_dim):
    return lax.dynamic_slice_in_dim(value, lax.axis_index("tensor") * size, size, axis_dim)


def row_norm(full):
    centre = full - jnp.mean(full, axis=-1, keepdims=True)
    factor = lax.rsqrt(jnp.mean(centre * centre, axis=-1, keepdims=True) + EPS)
    return (centre * factor, factor)


def norm_finish(grad_part, unit_part, factor, scaled, first_sum, second_sum, width):
    result = factor * (
        scaled - (first_sum / width)[:, None] - unit_part * (second_sum / width)[:, None]
    )
    return (result, jnp.sum(grad_part * unit_part, axis=0), jnp.sum(grad_part, axis=0))


def norm_back(grad_half, unit_half, factor, gain_half, width):
    scaled = grad_half * gain_half
    first_sum = jnp.sum(scaled, axis=-1)
    second_sum = jnp.sum(scaled * unit_half, axis=-1)
    first_sum, second_sum = lax.psum((first_sum, second_sum), "tensor")
    return norm_finish(grad_half, unit_half, factor, scaled, first_sum, second_sum, width)


def smooth(value):
    return jax.nn.gelu(value, approximate=True)


def episode_mask(resets):
    rows = resets.shape[0]
    places = jnp.arange(rows, dtype=jnp.int32)
    starts = jnp.where((places % SEQ_LEN == 0) | (resets == 1), 1, 0).astype(jnp.int32)
    labels = jnp.cumsum(starts).reshape(rows // SEQ_LEN, SEQ_LEN)
    inside = jnp.arange(SEQ_LEN, dtype=jnp.int32)
    causal = inside[:, None] >= inside[None, :]
    return (labels[:, :, None] == labels[:, None, :]) & causal[None]


def scores_of(queries, keys, allowed):
    raw = jnp.einsum(
        "sqhd,skhd->shqk", queries, keys, preferred_element_type=jnp.float32
    ) * HEAD_DIM ** (-0.5)
    return jnp.where(allowed[:, None], raw, NEG)


def attend_forward(queries, keys, values, allowed):
    scores = scores_of(queries, keys, allowed)
    top = jnp.max(scores, axis=-1, keepdims=True)
    expo = jnp.exp(scores - top)
    total = jnp.sum(expo, axis=-1, keepdims=True)
    logsum = top + jnp.log(total)
    weights = (expo / total).astype(jnp.bfloat16)
    mixed = jnp.einsum("shqk,skhd->sqhd", weights, values, preferred_element_type=jnp.float32)
    return (mixed, logsum)


def attend_backward(queries, keys, values, allowed, logsum, mixed_grad):
    factor = HEAD_DIM ** (-0.5)
    again = jnp.exp(scores_of(queries, keys, allowed) - logsum)
    weight_grad = jnp.einsum(
        "sqhd,skhd->shqk", mixed_grad, values, preferred_element_type=jnp.float32
    )
    inner = jnp.sum(again * weight_grad, axis=-1, keepdims=True)
    score_grad = (again * (weight_grad - inner)).astype(jnp.bfloat16)
    query_grad = (
        jnp.einsum("shqk,skhd->sqhd", score_grad, keys, preferred_element_type=jnp.float32) * factor
    )
    key_grad = (
        jnp.einsum("shqk,sqhd->skhd", score_grad, queries, preferred_element_type=jnp.float32)
        * factor
    )
    value_grad = jnp.einsum(
        "shqk,sqhd->skhd",
        again.astype(jnp.bfloat16),
        mixed_grad,
        preferred_element_type=jnp.float32,
    )
    return (query_grad, key_grad, value_grad)


def local(
    frames,
    resets,
    first_gain,
    first_shift,
    qkv_weight,
    out_weight,
    out_bias,
    second_gain,
    second_shift,
    up_weight,
    up_bias,
    down_weight,
    down_bias,
    prior_gain,
    prior_shift,
    prior_weight,
    prior_bias,
    out_cotangent,
    logit_cotangent,
):
    rows, half = frames.shape
    width = first_gain.shape[0]
    sequences = rows // SEQ_LEN
    heads_here = qkv_weight.shape[2] // HEAD_DIM
    allowed = episode_mask(resets)
    whole = lax.all_gather(frames, "tensor", axis=1, tiled=True)
    unit_one, scale_one = row_norm(whole.astype(jnp.float32))
    first = (unit_one * first_gain + first_shift).astype(jnp.bfloat16)
    triple = jnp.einsum(
        "rd,cde->cre", first, qkv_weight, preferred_element_type=jnp.float32
    ).astype(jnp.bfloat16)
    queries = triple[0].reshape(sequences, SEQ_LEN, heads_here, HEAD_DIM)
    keys = triple[1].reshape(sequences, SEQ_LEN, heads_here, HEAD_DIM)
    values = triple[2].reshape(sequences, SEQ_LEN, heads_here, HEAD_DIM)
    mixed, logsum = attend_forward(queries, keys, values, allowed)
    mixed = mixed.reshape(rows, half).astype(jnp.bfloat16)
    attn_terms = jnp.dot(mixed, out_weight, preferred_element_type=jnp.float32)
    attended = lax.psum_scatter(attn_terms, "tensor", scatter_dimension=1, tiled=True)
    middle = frames.astype(jnp.float32) + attended + own_part(out_bias, half, 0)
    middle_whole = lax.all_gather(middle, "tensor", axis=1, tiled=True)
    unit_two, scale_two = row_norm(middle_whole)
    second = (unit_two * second_gain + second_shift).astype(jnp.bfloat16)
    hidden = jnp.dot(second, up_weight, preferred_element_type=jnp.float32) + up_bias
    activated = smooth(hidden).astype(jnp.bfloat16)
    down_terms = jnp.dot(activated, down_weight, preferred_element_type=jnp.float32)
    ending = (
        middle
        + lax.psum_scatter(down_terms, "tensor", scatter_dimension=1, tiled=True)
        + own_part(down_bias, half, 0)
    )
    ending_whole = lax.all_gather(ending, "tensor", axis=1, tiled=True)
    unit_three, scale_three = row_norm(ending_whole)
    prior_in = (unit_three * prior_gain + prior_shift).astype(jnp.bfloat16)
    logits = jnp.dot(prior_in, prior_weight, preferred_element_type=jnp.float32) + prior_bias
    grad_prior_weight = jnp.einsum(
        "rd,re->de", prior_in, logit_cotangent, preferred_element_type=jnp.float32
    )
    grad_prior_bias = jnp.sum(logit_cotangent.astype(jnp.float32), axis=0)
    prior_terms = jnp.einsum(
        "re,de->rd", logit_cotangent, prior_weight, preferred_element_type=jnp.float32
    )
    prior_back = lax.psum_scatter(prior_terms, "tensor", scatter_dimension=1, tiled=True)
    back_three, gain_three, shift_three = norm_back(
        prior_back, own_part(unit_three, half, 1), scale_three, own_part(prior_gain, half, 0), width
    )
    grad_ending = out_cotangent.astype(jnp.float32) + back_three
    ending_grad = lax.all_gather(grad_ending.astype(jnp.bfloat16), "tensor", axis=1, tiled=True)
    grad_down_weight = jnp.einsum(
        "rf,rd->fd", activated, ending_grad, preferred_element_type=jnp.float32
    )
    act_grad = jnp.einsum("rd,fd->rf", ending_grad, down_weight, preferred_element_type=jnp.float32)
    gelu_value, gelu_pull = jax.vjp(smooth, hidden)
    hidden_grad = gelu_pull(act_grad)[0].astype(jnp.bfloat16)
    grad_up_bias = jnp.sum(hidden_grad.astype(jnp.float32), axis=0)
    grad_up_weight = jnp.einsum(
        "rd,rf->df", second, hidden_grad, preferred_element_type=jnp.float32
    )
    up_terms = jnp.einsum("rf,df->rd", hidden_grad, up_weight, preferred_element_type=jnp.float32)
    up_back = lax.psum_scatter(up_terms, "tensor", scatter_dimension=1, tiled=True)
    back_two, gain_two, shift_two = norm_back(
        up_back, own_part(unit_two, half, 1), scale_two, own_part(second_gain, half, 0), width
    )
    grad_middle = grad_ending + back_two
    middle_grad = lax.all_gather(grad_middle.astype(jnp.bfloat16), "tensor", axis=1, tiled=True)
    grad_out_weight = jnp.einsum(
        "rh,rd->hd", mixed, middle_grad, preferred_element_type=jnp.float32
    )
    mixed_grad = jnp.einsum(
        "rd,hd->rh", middle_grad, out_weight, preferred_element_type=jnp.float32
    )
    mixed_grad = mixed_grad.astype(jnp.bfloat16).reshape(sequences, SEQ_LEN, heads_here, HEAD_DIM)
    query_grad, key_grad, value_grad = attend_backward(
        queries, keys, values, allowed, logsum, mixed_grad
    )
    triple_grad = (
        jnp.stack([query_grad, key_grad, value_grad]).reshape(3, rows, half).astype(jnp.bfloat16)
    )
    grad_qkv = jnp.einsum("rd,cre->cde", first, triple_grad, preferred_element_type=jnp.float32)
    first_terms = jnp.einsum(
        "cre,cde->rd", triple_grad, qkv_weight, preferred_element_type=jnp.float32
    )
    first_back = lax.psum_scatter(first_terms, "tensor", scatter_dimension=1, tiled=True)
    back_one, gain_one, shift_one = norm_back(
        first_back, own_part(unit_one, half, 1), scale_one, own_part(first_gain, half, 0), width
    )
    grad_frames = grad_middle + back_one
    halves = jnp.stack(
        [
            gain_one,
            shift_one,
            jnp.sum(grad_middle, axis=0),
            gain_two,
            shift_two,
            jnp.sum(grad_ending, axis=0),
            gain_three,
            shift_three,
        ]
    )
    carried = lax.dynamic_update_slice_in_dim(
        jnp.zeros((8, width), jnp.float32), halves, lax.axis_index("tensor") * half, 1
    )
    totals = lax.psum(
        (
            grad_qkv,
            grad_out_weight,
            grad_up_weight,
            grad_up_bias,
            grad_down_weight,
            grad_prior_weight,
            grad_prior_bias,
            carried,
        ),
        "dp",
    )
    vectors = lax.psum(totals[7], "tensor")
    return (
        ending.astype(jnp.bfloat16),
        logits,
        grad_frames,
        vectors[0],
        vectors[1],
        totals[0],
        totals[1],
        vectors[2],
        vectors[3],
        vectors[4],
        totals[2],
        totals[3],
        totals[4],
        vectors[5],
        vectors[6],
        vectors[7],
        totals[5],
        totals[6],
    )


def solution(mesh):
    placed = (
        P("dp", "tensor"),
        P("dp"),
        P(),
        P(),
        P(None, None, "tensor"),
        P("tensor", None),
        P(),
        P(),
        P(),
        P(None, "tensor"),
        P("tensor"),
        P("tensor", None),
        P(),
        P(),
        P(),
        P(None, "tensor"),
        P("tensor"),
        P("dp", "tensor"),
        P("dp", "tensor"),
    )
    return jax.shard_map(
        local,
        mesh=mesh,
        in_specs=placed,
        out_specs=(
            P("dp", "tensor"),
            P("dp", "tensor"),
            P("dp", "tensor"),
            P(),
            P(),
            P(None, None, "tensor"),
            P("tensor", None),
            P(),
            P(),
            P(),
            P(None, "tensor"),
            P("tensor"),
            P("tensor", None),
            P(),
            P(),
            P(),
            P(None, "tensor"),
            P("tensor"),
        ),
        check_vma=False,
    )
```

profile of v0, /device:TPU:0, one launch (start us, length us, event | category | flops | bytes accessed | tf_op | source)
XLA Modules:
  0.0 692.6 jit_solution(2680352516006282227)
XLA Ops:
  10.4 25.3 %all-gather.6.cloned.1.call-done = bf16[1200,512]{1,0:T(8,128)(2,1)} async-done(((bf16[1200,256]{1,0:T(8,128)(2,1)}), bf16[1200,512]{1,0:T(8,128)(2,1)}) %all-gather.6.cloned.1.call-update) | async-done | bytes 1228816 | tf_op jit(solution)/shard_map/all_gather | solution.py:121
  35.6 1.6 convert_reduce_fusion.1
  38.0 1.4 fusion.7
  39.4 1.1 fusion.45
  41.1 2.5 reshape_squeeze.11
  43.5 3.3 reshape_squeeze.9
  46.8 1.9 fusion.47
  49.6 1.4 copy-done.20
  53.3 1.9 fusion.48
  55.4 35.8 %reduce-scatter.6.cloned.1.call-done = f32[1200,256]{1,0:T(8,128)} async-done(((f32[1200,512]{1,0:T(8,128)}), f32[1200,256]{1,0:T(8,128)}) %reduce-scatter.6.cloned.1.call-update) | async-done | bytes 1228816 | tf_op jit(solution)/shard_map/reduce_scatter | solution.py:133
  91.2 2.5 add_add_fusion.1
  94.0 37.1 %all-gather.8.cloned.1.call-done = f32[1200,512]{1,0:T(8,128)} async-done(((f32[1200,256]{1,0:T(8,128)}), f32[1200,512]{1,0:T(8,128)}) %all-gather.8.cloned.1.call-update) | async-done | bytes 2457616 | tf_op jit(solution)/shard_map/all_gather | solution.py:135
  131.1 2.1 reduce_sum.219
  135.7 4.2 multiply_convert_fusion
  139.9 1.5 copy-done.74
  141.4 2.9 fusion.49
  145.0 35.2 %reduce-scatter.8.cloned.1.call-done = f32[1200,256]{1,0:T(8,128)} async-done(((f32[1200,512]{1,0:T(8,128)}), f32[1200,256]{1,0:T(8,128)}) %reduce-scatter.8.cloned.1.call-update) | async-done | bytes 1228816 | tf_op jit(solution)/shard_map/reduce_scatter | solution.py:143
  180.2 3.1 fusion.44
  183.4 3.7 fusion.50
  187.8 32.8 %all-gather.10.cloned.1.call-done = f32[1200,512]{1,0:T(8,128)} async-done(((f32[1200,256]{1,0:T(8,128)}), f32[1200,512]{1,0:T(8,128)}) %all-gather.10.cloned.1.call-update) | async-done | bytes 2457616 | tf_op jit(solution)/shard_map/all_gather | solution.py:146
  220.6 1.9 reduce_sum.221
  222.6 2.3 multiply_reduce_fusion.1
  225.0 1.8 subtract_multiply_fusion
  226.8 31.7 %reduce-scatter.10.cloned.1.call-done = f32[1200,256]{1,0:T(8,128)} async-done(((f32[1200,512]{1,0:T(8,128)}), f32[1200,256]{1,0:T(8,128)}) %reduce-scatter.10.cloned.1.call-update) | async-done | bytes 1228816 | tf_op jit(solution)/shard_map/reduce_scatter | solution.py:157
  258.6 2.7 multiply_reduce_fusion.3
  261.3 6.9 all-reduce.5
  268.2 2.9 fusion.42
  273.4 24.3 %all-gather.12.cloned.1.call-done = bf16[1200,512]{1,0:T(8,128)(2,1)} async-done(((bf16[1200,256]{1,0:T(8,128)(2,1)}), bf16[1200,512]{1,0:T(8,128)(2,1)}) %all-gather.12.cloned.1.call-update) | async-done | bytes 1228816 | tf_op jit(solution)/shard_map/all_gather | solution.py:162
  297.7 7.8 %convert_reduce_fusion = (f32[1024]{0:T(1024)}, bf16[1200,1024]{1,0:T(8,128)(2,1)S(1)}) fusion(f32[1200,1024]{1,0:T(8,128)} %get-tuple-element.101, bf16[1200,512]{1,0:T(8,128)(2,1)} %all-gather.12.cloned.1.call-done, bf16[1024,512]{1,0:T(8,128)(2,1)} %param.30), kind=kOutput, calls=%fused_computation.9 | convolution fusion | flops 1285323776 | bytes 9654272 | tf_op jit(solution)/shard_map/rd,fd->rf/dot_general | solution.py:166
  305.5 1.4 copy-done.26
  307.0 2.9 fusion.51
  310.8 35.1 %reduce-scatter.12.cloned.1.call-done = f32[1200,256]{1,0:T(8,128)} async-done(((f32[1200,512]{1,0:T(8,128)}), f32[1200,256]{1,0:T(8,128)}) %reduce-scatter.12.cloned.1.call-update) | async-done | bytes 1228816 | tf_op jit(solution)/shard_map/reduce_scatter | solution.py:174
  345.9 2.4 multiply_reduce_fusion.4
  348.3 6.9 %all-reduce.4 = (f32[1200]{0:T(1024)S(1)}, f32[1200]{0:T(1024)S(1)}) all-reduce(f32[1200]{0:T(1024)S(1)} %get-tuple-element.57, f32[1200]{0:T(1024)S(1)} %get-tuple-element.61), channel_id=1, replica_groups=mesh['dp'=16,'tensor'=2] {'tensor'}, use_global_device_ids=true, to_apply=%region_21.22 | all-reduce | flops 2400 | bytes 19200 | tf_op jit(solution)/shard_map/psum | solution.py:35
  355.2 2.8 fusion.43
  358.0 1.0 copy-done.10
  360.3 4.0 fusion.31
  364.4 2.9 fusion.53
  367.3 2.9 fusion.30
  370.2 14.4 %all-gather.14.cloned.1.call-done = bf16[1200,512]{1,0:T(8,128)(2,1)} async-done(((bf16[1200,256]{1,0:T(8,128)(2,1)}), bf16[1200,512]{1,0:T(8,128)(2,1)}) %all-gather.14.cloned.1.call-update) | async-done | bytes 1228816 | tf_op jit(solution)/shard_map/all_gather | solution.py:179
  384.6 1.8 convolution_convert_fusion.1
  386.4 1.5 reshape.149
  387.9 2.3 fusion.14
  390.2 1.2 multiply_reduce_fusion
  395.0 1.5 copy.61
  396.5 2.5 stack.41
  399.0 1.5 copy.59
  400.5 2.9 stack.40
  406.2 1.4 fusion.52
  407.7 2.5 convolution_bitcast_fusion.1
  410.3 1.4 copy-done.36
  411.7 3.8 convolution_bitcast_fusion
  415.5 1.6 copy-done.22
  417.4 1.8 fusion.8
  420.0 2.2 convolution_add_fusion.1
  422.2 144.4 %all-reduce.8.cloned.1.call-done = (f32[3,512,256]{1,2,0:T(8,128)}, f32[256,512]{1,0:T(8,128)}, f32[512,1024]{1,0:T(8,128)}, f32[1024,512]{1,0:T(8,128)}, f32[512,512]{1,0:T(8,128)}) async-done(((f32[3,512,256]{1,2,0:T(8,128)}, f32[256,512]{1,0:T(8,128)}, f32[512,1024]{1,0:T(8,128)}, f32[1024,512]{1,0:T(8,128)}, f32[512,512]{1,0:T(8,128)}), (f32[3,512,256]{1,2,0:T(8,128)}, f32[256,512]{1,0:T(8,128)}, ...) | async-done | bytes 7340048 | tf_op jit(solution)/shard_map/psum | solution.py:217
  566.7 3.1 copy.62
  569.8 35.0 %reduce-scatter.14.cloned.1.call-done = f32[1200,256]{1,0:T(8,128)} async-done(((f32[1200,512]{1,0:T(8,128)}), f32[1200,256]{1,0:T(8,128)}) %reduce-scatter.14.cloned.1.call-update) | async-done | bytes 1228816 | tf_op jit(solution)/shard_map/reduce_scatter | solution.py:197
  604.8 2.3 multiply_reduce_fusion.5
  607.3 61.2 %all-reduce.1 = (f32[8,512]{1,0:T(8,128)S(1)}, f32[1024]{0:T(1024)}, f32[512]{0:T(512)}) all-reduce(f32[8,512]{1,0:T(8,128)S(1)} %constant_dynamic-update-slice_fusion.3, f32[1024]{0:T(1024)S(1)} %copy-done.56, f32[512]{0:T(512)S(1)} %convert_reduce_fusion.2), channel_id=1, replica_groups=mesh['dp'=16,'tensor'=2] {'dp'}, use_global_device_ids=true, to_apply=%region_36.37 | all-reduce | flops 5632 | bytes 45056 | tf_op jit(solution)/shard_map/psum | solution.py:217
  668.5 7.3 %all-reduce.3 = (f32[1200]{0:T(1024)S(1)}, f32[1200]{0:T(1024)S(1)}, f32[8,512]{1,0:T(8,128)S(1)}) all-reduce(f32[1200]{0:T(1024)S(1)} %get-tuple-element.59, f32[1200]{0:T(1024)S(1)} %get-tuple-element.60, f32[8,512]{1,0:T(8,128)S(1)} %get-tuple-element.66), channel_id=1, replica_groups=mesh['dp'=16,'tensor'=2] {'tensor'}, use_global_device_ids=true, to_apply=%region_27.28 | all-reduce | flops 6496 | bytes 51968 | tf_op jit(solution)/shard_map/psum | solution.py:35
  676.5 3.0 multiply_add_fusion
  680.3 1.3 copy.98
  682.6 1.3 copy.99
  (220 shorter events, 27.6 us)
Async XLA Ops:
  7.2 128.4 %copy-start = (bf16[512,1024]{1,0:T(8,128)(2,1)S(1)}, bf16[512,1024]{1,0:T(8,128)(2,1)}, u32[]{:S(2)}) copy-start(bf16[512,1024]{1,0:T(8,128)(2,1)} %param.28) | copy-start | bytes 3145732
  7.2 30.8 %copy-start.60 = (f32[512]{0:T(512)S(1)}, f32[512]{0:T(512)}, u32[]{:S(2)}) copy-start(f32[512]{0:T(512)} %param.21) | copy-start | bytes 6148
  7.2 30.8 %copy-start.69 = (f32[512]{0:T(512)S(1)}, f32[512]{0:T(512)}, u32[]{:S(2)}) copy-start(f32[512]{0:T(512)} %param.22) | copy-start | bytes 6148
  7.2 30.8 %copy-start.67 = (bf16[3,512,256]{2,1,0:T(8,128)(2,1)S(1)}, bf16[3,512,256]{2,1,0:T(8,128)(2,1)}, u32[]{:S(2)}) copy-start(bf16[3,512,256]{2,1,0:T(8,128)(2,1)} %param.23) | copy-start | bytes 2359300
  7.2 28.4 %all-gather.6.cloned.1.call-start = ((), (), s32[]{:S(2)}) async-start(), calls=%async_computation.5 | async-start | bytes 1843200 | tf_op jit(solution)/shard_map/all_gather | solution.py:121
  8.0 83.3 %reduce-scatter.6.cloned.1.call-start = ((), (), s32[]{:S(2)}) async-start(), calls=%async_computation.6 | async-start | bytes 3686400 | tf_op jit(solution)/shard_map/reduce_scatter | solution.py:133
  35.6 1.7 copy-start.8
  37.3 2.1 copy-start.43
  41.0 7.7 %copy-start.16 = (bf16[24,50,4,64]{3,2,1,0:T(4,128)(2,1)}, bf16[24,50,4,64]{3,2,1,0:T(4,128)(2,1)S(1)}, u32[]{:S(2)}) copy-start(bf16[24,50,4,64]{3,2,1,0:T(4,128)(2,1)S(1)} %reshape_squeeze.10) | copy-start | bytes 1843204
  43.5 5.2 copy-start.18
  48.8 3.2 copy-start.2
  48.8 3.2 copy-start.37
  48.8 2.2 copy-start.20
  53.3 2.0 copy-start.14
  53.3 2.0 copy-start.58
  53.3 37.9 %copy-start.28 = (bf16[1200,256]{1,0:T(8,128)(2,1)S(1)}, bf16[1200,256]{1,0:T(8,128)(2,1)}, u32[]{:S(2)}) copy-start(bf16[1200,256]{1,0:T(8,128)(2,1)} %param.19) | copy-start | bytes 1843204
  55.3 75.8 %all-gather.8.cloned.1.call-start = ((), (), s32[]{:S(2)}) async-start(), calls=%async_computation.7 | async-start | bytes 3686400 | tf_op jit(solution)/shard_map/all_gather | solution.py:135
  93.8 86.5 %reduce-scatter.8.cloned.1.call-start = ((), (), s32[]{:S(2)}) async-start(), calls=%async_computation.8 | async-start | bytes 3686400 | tf_op jit(solution)/shard_map/reduce_scatter | solution.py:143
  131.1 2.4 copy-start.5
  133.2 1.8 copy-start.6
  135.7 5.7 copy-start.66
  144.3 76.4 %all-gather.10.cloned.1.call-start = ((), (), s32[]{:S(2)}) async-start(), calls=%async_computation.9 | async-start | bytes 3686400 | tf_op jit(solution)/shard_map/all_gather | solution.py:146
  183.3 75.3 %reduce-scatter.10.cloned.1.call-start = ((), (), s32[]{:S(2)}) async-start(), calls=%async_computation.10 | async-start | bytes 3686400 | tf_op jit(solution)/shard_map/reduce_scatter | solution.py:157
  187.1 110.6 %all-gather.12.cloned.1.call-start = ((), (), s32[]{:S(2)}) async-start(), calls=%async_computation.11 | async-start | bytes 1843200 | tf_op jit(solution)/shard_map/all_gather | solution.py:162
  222.6 2.4 copy-start.4
  273.1 72.8 %reduce-scatter.12.cloned.1.call-start = ((), (), s32[]{:S(2)}) async-start(), calls=%async_computation.12 | async-start | bytes 3686400 | tf_op jit(solution)/shard_map/reduce_scatter | solution.py:174
  309.9 45.3 %copy-start.46 = (f32[1200]{0:T(1024)S(1)}, f32[1200]{0:T(1024)}, u32[]{:S(2)}) copy-start(f32[1200]{0:T(1024)} %copy-done.45) | copy-start | bytes 14404
  310.0 74.6 %all-gather.14.cloned.1.call-start = ((), (), s32[]{:S(2)}) async-start(), calls=%async_computation.13 | async-start | bytes 1843200 | tf_op jit(solution)/shard_map/all_gather | solution.py:179
  358.0 2.2 copy-start.63
  358.0 2.3 copy-start.72
  360.0 206.7 %all-reduce.8.cloned.1.call-start = ((), (), s32[]{:S(2)}) async-start(), calls=%async_computation.15 | async-start | bytes 14680064 | tf_op jit(solution)/shard_map/psum | solution.py:217
  360.3 4.1 copy-start.65
  360.3 4.1 copy-start.75
  364.3 2.9 copy-start.27
  364.4 2.9 copy-start.48
  364.4 2.9 copy-start.50
  370.2 17.7 %copy-start.3 = (f32[24,4,50,50]{2,3,1,0:T(8,128)S(1)}, f32[24,4,50,50]{2,3,1,0:T(8,128)}, u32[]{:S(2)}) copy-start(f32[24,4,50,50]{2,3,1,0:T(8,128)} %copy-done.2) | copy-start | bytes 2880004
  387.9 2.3 copy-start.7
  387.9 2.3 copy-start.21
  405.0 2.6 copy-start.9
  405.1 2.6 copy-start.42
  405.1 2.6 copy-start.44
  405.1 2.6 copy-start.61
  405.1 2.6 copy-start.70
  410.2 194.6 %reduce-scatter.14.cloned.1.call-start = ((), (), s32[]{:S(2)}) async-start(), calls=%async_computation.14 | async-start | bytes 3686400 | tf_op jit(solution)/shard_map/reduce_scatter | solution.py:197
  417.3 2.4 copy-start.13
  417.3 2.7 copy-start.34
  417.3 2.7 copy-start.64
  417.3 2.6 copy-start.71
  417.4 2.6 copy-start.73
  566.7 40.5 %copy-start.51 = (f32[256]{0:T(256)S(1)}, f32[256]{0:T(256)}, u32[]{:S(2)}) copy-start(f32[256]{0:T(256)} %get-tuple-element.54) | copy-start | bytes 3076
  566.7 40.5 %copy-start.52 = (f32[256]{0:T(256)S(1)}, f32[256]{0:T(256)}, u32[]{:S(2)}) copy-start(f32[256]{0:T(256)} %get-tuple-element.63) | copy-start | bytes 3076
  566.7 40.5 %copy-start.53 = (f32[256]{0:T(256)S(1)}, f32[256]{0:T(256)}, u32[]{:S(2)}) copy-start(f32[256]{0:T(256)} %get-tuple-element.56) | copy-start | bytes 3076
  566.7 40.5 %copy-start.54 = (f32[256]{0:T(256)S(1)}, f32[256]{0:T(256)}, u32[]{:S(2)}) copy-start(f32[256]{0:T(256)} %get-tuple-element.64) | copy-start | bytes 3076
  566.7 40.5 %copy-start.55 = (f32[256]{0:T(256)S(1)}, f32[256]{0:T(256)}, u32[]{:S(2)}) copy-start(f32[256]{0:T(256)} %get-tuple-element.83) | copy-start | bytes 3076
  566.7 40.5 %copy-start.57 = (f32[256]{0:T(256)S(1)}, f32[256]{0:T(256)}, u32[]{:S(2)}) copy-start(f32[256]{0:T(256)} %get-tuple-element.81) | copy-start | bytes 3076
  566.7 40.6 %copy-start.56 = (f32[1024]{0:T(1024)S(1)}, f32[1024]{0:T(1024)}, u32[]{:S(2)}) copy-start(f32[1024]{0:T(1024)} %get-tuple-element.104) | copy-start | bytes 12292
  569.8 106.7 %copy-start.11 = (f32[1200,256]{1,0:T(8,128)S(1)}, f32[1200,256]{1,0:T(8,128)}, u32[]{:S(2)}) copy-start(f32[1200,256]{1,0:T(8,128)} %copy-done.10) | copy-start | bytes 3686404
  604.8 71.6 %copy-start.23 = (f32[1200,256]{1,0:T(8,128)S(1)}, f32[1200,256]{1,0:T(8,128)}, u32[]{:S(2)}) copy-start(f32[1200,256]{1,0:T(8,128)} %reduce-scatter.14.cloned.1.call-done) | copy-start | bytes 3686404
  676.5 3.0 copy-start.33
  676.5 3.8 copy-start.30
  680.3 2.3 copy-start.29
  682.6 2.0 copy-start.31
  682.6 2.9 copy-start.1
  (23 other events, 25.2 us)
Sparse Core Ops, SparseCore 0:
  9.6 25.9 all-gather.5
  55.4 35.7 reduce-scatter.5
  93.9 37.1 all-gather.7
  144.4 35.7 reduce-scatter.7
  183.4 37.1 all-gather.9
  222.8 35.7 reduce-scatter.9
  273.2 24.4 all-gather.11
  310.1 35.7 reduce-scatter.11
  360.1 24.4 all-gather.13
  410.3 156.2 all-reduce.7
  569.0 35.7 reduce-scatter.13
where the time goes:
time: 701 us; the launch traced here: 693 us
  waiting for transfers between devices  452 us (64%)
  blocking collectives  82.4 us (12%)
  matrix products  54.6 us (8%)
  local copies, waits for them, and re-layouts  46.7 us (7%)
  other arithmetic  40.5 us (6%)
  between operations  15.3 us (2%)
    psum x1, waiting for transfers between devices, local(): lax.psum((grad_qkv, grad_out_weight, grad_up_weight, grad_up_bias, grad_d...  144 us
    psum x1, blocking collectives, local(): lax.psum((grad_qkv, grad_out_weight, grad_up_weight, grad_up_bias, grad_d...  61.2 us
    all_gather x1, waiting for transfers between devices, local(): middle_whole = lax.all_gather(middle, 'tensor', axis=1, tiled=True)  37.1 us
    reduce_scatter x1, waiting for transfers between devices, local(): lax.psum_scatter(attn_terms, 'tensor', scatter_dimension=1, tiled=True)  35.8 us
    reduce_scatter x1, waiting for transfers between devices, local(): lax.psum_scatter(down_terms, 'tensor', scatter_dimension=1, tiled=True)  35.2 us
    reduce_scatter x1, waiting for transfers between devices, local(): lax.psum_scatter(up_terms, 'tensor', scatter_dimension=1, tiled=True)  35.1 us
    reduce_scatter x1, waiting for transfers between devices, local(): lax.psum_scatter(first_terms, 'tensor', scatter_dimension=1, tiled=True)  35 us
    all_gather x1, waiting for transfers between devices, local(): ending_whole = lax.all_gather(ending, 'tensor', axis=1, tiled=True)  32.8 us
  transfers between devices with their start and end apart: 11, of which 11 were waited for; matrix products, arithmetic and copies ran while one was open for 5% of the time, Pallas kernels for 0%

commit v1 on v0

v1 whole, which is shorter than its diff:
```python
import functools

import jax
import jax.numpy as jnp
from jax import lax
from jax.experimental import pallas as pl
from jax.experimental.pallas import tpu as pltpu
from jax.sharding import PartitionSpec as P

HEAD_DIM = 64
SEQ_LEN = 50
BLOCK = 4 * SEQ_LEN
PAD = -(-BLOCK // 16) * 16
EPS = 1e-05
NEG = -1e30
GELU_C = 0.7978845608028654
GELU_A = 0.044715
VMEM = 48 * 1024 * 1024
BF = jnp.bfloat16
F32 = jnp.float32


def mm(a, b):
    return lax.dot_general(a, b, (((1,), (0,)), ((), ())), preferred_element_type=F32)


def mm_bt(a, b):
    return lax.dot_general(a, b, (((1,), (1,)), ((), ())), preferred_element_type=F32)


def mm_at(a, b):
    return lax.dot_general(a, b, (((0,), (0,)), ((), ())), preferred_element_type=F32)


def norm_of(value):
    centre = value - jnp.mean(value, axis=-1, keepdims=True)
    factor = lax.rsqrt(jnp.mean(centre * centre, axis=-1, keepdims=True) + EPS)
    return centre * factor, factor


def norm_back(grad, unit, factor, gain):
    scaled = grad * gain
    first = jnp.mean(scaled, axis=-1, keepdims=True)
    second = jnp.mean(scaled * unit, axis=-1, keepdims=True)
    return factor * (scaled - first - unit * second)


def col_sum(value):
    return jnp.sum(value, axis=0, keepdims=True)


def whole_row(here, own, other):
    low = jnp.where(here == 0, own, other)
    high = jnp.where(here == 0, other, own)
    return jnp.concatenate([low, high], axis=1).astype(F32)


def allowed_pairs(seg):
    seg2 = jnp.concatenate([seg, seg], axis=0)
    row = lax.broadcasted_iota(jnp.int32, (2 * PAD, PAD), 0)
    row = jnp.where(row >= PAD, row - PAD, row)
    col = lax.broadcasted_iota(jnp.int32, (2 * PAD, PAD), 1)
    return (col <= row) & (col >= seg2)


def two_heads(value):
    first = lax.broadcasted_iota(jnp.int32, value.shape, 1) < HEAD_DIM
    none = jnp.zeros_like(value)
    return jnp.concatenate([jnp.where(first, value, none), jnp.where(first, none, value)], axis=0)


def one_pair(value):
    first = lax.broadcasted_iota(jnp.int32, (PAD, 2 * HEAD_DIM), 1) < HEAD_DIM
    return jnp.where(first, value[:PAD], value[PAD:])


def softmax_of(query2, key, allowed):
    scores = jnp.where(allowed, mm_bt(query2, key) * HEAD_DIM ** (-0.5), NEG)
    expo = jnp.exp(scores - jnp.max(scores, axis=-1, keepdims=True))
    return expo / jnp.sum(expo, axis=-1, keepdims=True)


def accumulate(step, ref, index, value):
    @pl.when(step == 0)
    def _():
        ref[index] = value

    @pl.when(step != 0)
    def _():
        ref[index] += value


def attend_kernel(
    s, own, other, seg, gain, shift, qkv, qkv_o, out, out_o, out_bias, gain2, shift2,
    first_ref, triple_ref, mixed_ref, middle_ref, second_ref,
):
    frames = whole_row(s[0], own[0], other[0])
    unit, _ = norm_of(frames)
    first = (unit * gain[...] + shift[...]).astype(BF)
    first_ref[0] = first
    allowed = allowed_pairs(seg[0])
    total = frames + out_bias[...]
    for half, (weight, weight_out) in enumerate(((qkv, out), (qkv_o, out_o))):
        triple = [mm(first, weight[c]).astype(BF) for c in range(3)]
        mixed = []
        for pair in range(2):
            at = slice(pair * 128, pair * 128 + 128)
            query, key, value = (item[:, at] for item in triple)
            weights = softmax_of(two_heads(query), key, allowed).astype(BF)
            mixed.append(one_pair(mm(weights, value)).astype(BF))
        mixed = jnp.concatenate(mixed, axis=1)
        for c in range(3):
            triple_ref[0, :, (half * 3 + c) * 256 : (half * 3 + c + 1) * 256] = triple[c]
        mixed_ref[0, :, half * 256 : half * 256 + 256] = mixed
        total = total + mm(mixed, weight_out[...])
    middle_ref[0] = total
    unit2, _ = norm_of(total)
    second_ref[0] = (unit2 * gain2[...] + shift2[...]).astype(BF)


def feed_kernel(
    s, second, middle, up, u0, u1, u2, u3, up_bias, down, d0, d1, d2, d3, down_bias, gain, shift,
    act_ref, slope_ref, ending_ref, prior_in_ref, block_own_ref, block_other_ref,
):
    x = second[0]
    total = middle[0] + down_bias[...]
    ups = [up[:, i * 256 : i * 256 + 256] for i in range(4)] + [u[...] for u in (u0, u1, u2, u3)]
    downs = [down[i * 256 : i * 256 + 256, :] for i in range(4)] + [d[...] for d in (d0, d1, d2, d3)]
    half = up.shape[1]
    for i in range(8):
        if i < 4:
            at = pl.ds(i * 256, 256)
        else:
            at = pl.ds(pl.multiple_of(half + (s[1] ^ (i - 4)) * 256, 256), 256)
        hidden = mm(x, ups[i]) + up_bias[:, at]
        square = hidden * hidden
        bent = jnp.tanh(GELU_C * (hidden + GELU_A * hidden * square))
        act = (0.5 * hidden * (1.0 + bent)).astype(BF)
        slope = 0.5 * (1.0 + bent) + (0.5 * GELU_C) * hidden * (1.0 - bent * bent) * (
            1.0 + (3.0 * GELU_A) * square
        )
        act_ref[0, :, at] = act
        slope_ref[0, :, at] = slope
        total = total + mm(act, downs[i])
    ending_ref[0] = total
    unit, _ = norm_of(total)
    prior_in_ref[0] = (unit * gain[...] + shift[...]).astype(BF)
    low, high = total[:, :256].astype(BF), total[:, 256:].astype(BF)
    block_own_ref[0] = jnp.where(s[0] == 0, low, high)
    block_other_ref[0] = jnp.where(s[0] == 0, high, low)


def prior_kernel(
    s, prior_in, ending, prior, p0, p1, p2, p3, bias, logit_own, logit_other, out_own, out_other, gain,
    logits_ref, logits_other_ref, grad_ending_ref, ending_grad_ref, vec_ref, bias_ref,
):
    step = pl.program_id(0)
    half = prior.shape[1]
    x = prior_in[0]
    cot = logit_own[0]
    logits_ref[0] = mm(x, prior[...]) + bias[:, :half]
    back = mm_bt(cot, prior[...])
    accumulate(step, bias_ref, (slice(None), slice(0, half)), col_sum(cot.astype(F32)))
    cot_o = logit_other[0]
    accumulate(step, bias_ref, (slice(None), slice(half, 2 * half)), col_sum(cot_o.astype(F32)))
    for j, piece in enumerate((p0, p1, p2, p3)):
        start = pl.multiple_of((s[1] ^ j) * 128, 128)
        at = pl.ds(start, 128)
        far = pl.ds(pl.multiple_of(half + start, 128), 128)
        logits_other_ref[0, :, at] = (mm(x, piece[...]) + bias[:, far]).astype(BF)
        back = back + mm_bt(logit_other[0, :, at], piece[...])
    unit, factor = norm_of(ending[0])
    grad = whole_row(s[0], out_own[0], out_other[0]) + norm_back(back, unit, factor, gain[...])
    grad_ending_ref[0] = grad
    ending_grad_ref[0] = grad.astype(BF)
    rows = jnp.concatenate([col_sum(back * unit), col_sum(back), col_sum(grad)], axis=0)
    accumulate(step, vec_ref, (slice(0, 3), slice(None)), rows)


def piece_targets(s, step, last, keep, sums, send):
    def put(h, j, rows, value):
        if j < 2:
            accumulate(step, keep, (2 * h + j, rows), value)
        else:
            accumulate(step, sums, (2 * h + j - 2, rows), value)

    def finish():
        @pl.when(step == last)
        def _():
            send[...] = sums[...].astype(BF)

    return put, finish


def late_grads_kernel(
    s, prior_in, logit_own, logit_other, act, ending_grad, keep, send, sums,
):
    step = pl.program_id(0)
    put, finish = piece_targets(s, step, pl.num_programs(0) - 1, keep, sums, send)
    x = prior_in[0]
    grad = ending_grad[0]
    half = act.shape[2] // 2
    n = x.shape[1]
    for h in range(2):
        for j in range(4):
            place = s[1] ^ j
            cot = (logit_own, logit_other)[h][0, :, pl.ds(pl.multiple_of(place * 128, 128), 128)]
            put(h, j, slice(0, n), mm_at(x, cot))
            part = act[0, :, pl.ds(pl.multiple_of(h * half + place * 256, 256), 256)]
            value = mm_at(part, grad)
            for t in range(4):
                put(h, j, slice(n + t * 256, n + t * 256 + 256), value[:, t * 128 : t * 128 + 128])
    finish()


def feed_back_kernel(
    s, ending_grad, slope, second, middle, grad_ending, up, u0, u1, u2, u3, down, d0, d1, d2, d3, gain,
    grad_middle_ref, middle_grad_ref, vec_ref, bias_ref, keep, send, sums,
):
    step = pl.program_id(0)
    put, finish = piece_targets(s, step, pl.num_programs(0) - 1, keep, sums, send)
    grad = ending_grad[0]
    x = second[0]
    half = up.shape[1]
    n = x.shape[1]
    back = jnp.zeros((PAD, n), F32)
    for h in range(2):
        for j in range(4):
            place = pl.multiple_of((s[1] ^ j) * 256, 256)
            at = pl.ds(pl.multiple_of(h * half + place, 256), 256)
            if h == 0:
                w_up, w_down = up[:, pl.ds(place, 256)], down[pl.ds(place, 256), :]
            else:
                w_up, w_down = (u0, u1, u2, u3)[j][...], (d0, d1, d2, d3)[j][...]
            low = (mm_bt(grad, w_down) * slope[0, :, at]).astype(BF)
            accumulate(step, bias_ref, (slice(None), at), col_sum(low.astype(F32)))
            value = mm_at(x, low)
            for t in range(2):
                put(h, j, slice(t * n, t * n + n), value[:, t * 128 : t * 128 + 128])
            back = back + mm_bt(low, w_up)
    finish()
    unit, factor = norm_of(middle[0])
    total = grad_ending[0] + norm_back(back, unit, factor, gain[...])
    grad_middle_ref[0] = total
    middle_grad_ref[0] = total.astype(BF)
    rows = jnp.concatenate([col_sum(back * unit), col_sum(back), col_sum(total)], axis=0)
    accumulate(step, vec_ref, (slice(0, 3), slice(None)), rows)


def attend_back_kernel(
    s, middle_grad, grad_middle, own, other, first, triple, mixed, seg, qkv, qkv_o, out, out_o, gain,
    frames_own_ref, frames_other_ref, vec_ref, keep, send, sums,
):
    step = pl.program_id(0)
    put, finish = piece_targets(s, step, pl.num_programs(0) - 1, keep, sums, send)
    grad = middle_grad[0]
    allowed = allowed_pairs(seg[0])
    factor = HEAD_DIM ** (-0.5)
    back = jnp.zeros(grad.shape, F32)
    for h, (weight, weight_out) in enumerate(((qkv, out), (qkv_o, out_o))):
        for j in range(4):
            part = middle_grad[0, :, pl.ds(pl.multiple_of((s[1] ^ j) * 128, 128), 128)]
            put(h, j, slice(0, 256), mm_at(mixed[0, :, h * 256 : h * 256 + 256], part))
        mixed_grad = mm_bt(grad, weight_out[...]).astype(BF)
        thirds = ([], [], [])
        for pair in range(2):
            at = slice(pair * 128, pair * 128 + 128)
            query, key, value = (
                triple[0, :, (h * 3 + c) * 256 + pair * 128 : (h * 3 + c) * 256 + pair * 128 + 128]
                for c in range(3)
            )
            query2 = two_heads(query)
            mixed2 = two_heads(mixed_grad[:, at])
            again = softmax_of(query2, key, allowed)
            weight_grad = mm_bt(mixed2, value)
            inner = jnp.sum(again * weight_grad, axis=-1, keepdims=True)
            score_grad = (again * (weight_grad - inner)).astype(BF)
            thirds[0].append((one_pair(mm(score_grad, key)) * factor).astype(BF))
            thirds[1].append((mm_at(score_grad, query2) * factor).astype(BF))
            thirds[2].append(mm_at(again.astype(BF), mixed2).astype(BF))
        for c in range(3):
            part = jnp.concatenate(thirds[c], axis=1)
            back = back + mm_bt(part, weight[c])
            for j in range(4):
                x = first[0, :, pl.ds(pl.multiple_of((s[1] ^ j) * 128, 128), 128)]
                value = mm_at(x, part)
                for t in range(2):
                    start = 256 + (t * 3 + c) * 128
                    put(h, j, slice(start, start + 128), value[:, t * 128 : t * 128 + 128])
    finish()
    unit, scale = norm_of(whole_row(s[0], own[0], other[0]))
    total = grad_middle[0] + norm_back(back, unit, scale, gain[...])
    low, high = total[:, :256], total[:, 256:]
    frames_own_ref[0] = jnp.where(s[0] == 0, low, high)
    frames_other_ref[0] = jnp.where(s[0] == 0, high, low).astype(BF)
    rows = jnp.concatenate([col_sum(back * unit), col_sum(back)], axis=0)
    accumulate(step, vec_ref, (slice(0, 2), slice(None)), rows)


def call(kernel, scalars, ins, outs, scratch=(), name=None, flops=0):
    steps = next(value.shape[0] for value, blocked in ins if blocked)

    def spec(shape, blocked):
        if blocked:
            return pl.BlockSpec((1,) + tuple(shape[1:]), lambda b, s: (b,) + (0,) * (len(shape) - 1))
        return pl.BlockSpec(tuple(shape), lambda b, s: (0,) * len(shape))

    moved = sum(v.size * v.dtype.itemsize for v, _ in ins) + sum(
        o.size * o.dtype.itemsize for o, _ in outs
    )
    return pl.pallas_call(
        kernel,
        grid_spec=pltpu.PrefetchScalarGridSpec(
            num_scalar_prefetch=1,
            grid=(steps,),
            in_specs=[spec(v.shape, blocked) for v, blocked in ins],
            out_specs=[spec(o.shape, blocked) for o, blocked in outs],
            scratch_shapes=list(scratch),
        ),
        out_shape=[o for o, _ in outs],
        compiler_params=pltpu.CompilerParams(vmem_limit_bytes=VMEM),
        cost_estimate=pl.CostEstimate(flops=flops, bytes_accessed=moved, transcendentals=0),
        name=name,
    )(scalars, *[v for v, _ in ins])


def swap(value, axes, sizes, mask):
    count = 1
    for size in sizes:
        count *= size
    return lax.ppermute(value, axes, [(i, i ^ mask) for i in range(count)])


class Moves:
    def __init__(self, n_dp, n_tensor):
        self.n_dp, self.n_tensor = n_dp, n_tensor
        self.dp = lax.axis_index("dp")
        self.here = lax.axis_index("tensor")

    def along(self, value, mask):
        return swap(value, "dp", (self.n_dp,), mask)

    def core(self, value):
        return self.along(value, 1)

    def side(self, value):
        return self.along(value, 2)

    def over(self, value):
        return swap(value, "tensor", (self.n_tensor,), 1)

    def cross(self, value):
        return swap(value, ("dp", "tensor"), (self.n_dp, self.n_tensor), 5)

    def groups(self):
        shift, rest = 2, self.n_dp // 4
        while rest > 1:
            size = 4 if rest % 4 == 0 else 2
            yield shift, size
            shift, rest = shift + (2 if size == 4 else 1), rest // size

    def reduce(self, keep, sent):
        total = keep + self.core(sent)
        parts = [total[i].astype(BF) for i in (1, 2, 3)]
        total = total[0] + self.side(parts[0]) + self.over(parts[1]) + self.cross(parts[2])
        for shift, size in self.groups():
            mine = (self.dp >> shift) & (size - 1)
            split = total.reshape(size, total.shape[0] // size, total.shape[1])
            total = lax.dynamic_index_in_dim(split, mine, 0, False)
            for k in range(1, size):
                part = lax.dynamic_index_in_dim(split, mine ^ k, 0, False).astype(BF)
                total = total + self.along(part, k << shift)
        return total

    def gather(self, total):
        total = total.astype(BF)
        for shift, size in reversed(list(self.groups())):
            mine = (self.dp >> shift) & (size - 1)
            parts = [total] + [self.along(total, k << shift) for k in range(1, size)]
            total = jnp.concatenate([pick(mine ^ i, parts) for i in range(size)], axis=0)
        near = self.side(total)
        far = self.core(jnp.stack([total, near]))
        parts = [total, near, far[0], far[1]]
        place = self.dp & 1, (self.dp >> 1) & 1
        place = place[0] * 2 + place[1]
        return jnp.stack([pick(place ^ i, parts) for i in range(4)])


def pick(which, parts):
    value = parts[-1]
    for i in range(len(parts) - 2, -1, -1):
        value = jnp.where(which == i, parts[i], value)
    return value


def blocks_of(value, start, count):
    rows = lax.dynamic_slice_in_dim(value, start, count, 0)
    rows = rows.reshape(count // BLOCK, BLOCK, value.shape[1])
    return jnp.pad(rows, ((0, 0), (0, PAD - BLOCK), (0, 0)))


def rows_of(here, own, other):
    cut = [v[:, :BLOCK].reshape(-1, v.shape[2]) for v in (own, other.astype(own.dtype))]
    return jnp.concatenate(
        [jnp.where(here == 0, cut[0], cut[1]), jnp.where(here == 0, cut[1], cut[0])], axis=0
    )


def episode_starts(resets):
    rows = resets.shape[0]
    inside = lax.broadcasted_iota(jnp.int32, (rows // SEQ_LEN, SEQ_LEN), 1)
    starts = jnp.where((inside == 0) | (resets.reshape(-1, SEQ_LEN) == 1), inside, 0)
    starts = lax.cummax(starts, axis=1).reshape(rows // BLOCK, BLOCK // SEQ_LEN, SEQ_LEN)
    starts = starts + SEQ_LEN * jnp.arange(BLOCK // SEQ_LEN, dtype=jnp.int32)[None, :, None]
    starts = starts.reshape(rows // BLOCK, BLOCK)
    tail = jnp.broadcast_to(jnp.arange(BLOCK, PAD, dtype=jnp.int32), (rows // BLOCK, PAD - BLOCK))
    return jnp.concatenate([starts, tail], axis=1)[:, :, None]


def local(
    n_dp, n_tensor, frames, resets, first_gain, first_shift, qkv_weight, out_weight, out_bias, second_gain,
    second_shift, up_weight, up_bias, down_weight, down_bias, prior_gain, prior_shift, prior_weight,
    prior_bias, out_cotangent, logit_cotangent,
):
    move = Moves(n_dp, n_tensor)
    here = move.here
    core, side = move.dp & 1, (move.dp >> 1) & 1
    place = core * 2 + side
    scalars = jnp.stack([here, place]).astype(jnp.int32)
    rows, half = frames.shape
    width = 2 * half
    mine = rows // 2
    blocks = mine // BLOCK
    row = lambda v: v.reshape(1, -1)

    def both(value):
        sent = blocks_of(value, (1 - here) * mine, mine)
        return blocks_of(value, here * mine, mine), move.over(sent)

    def part(value, index, size, dim):
        return lax.dynamic_slice_in_dim(value, index * size, size, dim)

    def half_pieces(value, dim):
        size = value.shape[dim] // 2
        got = move.over(part(value, core, size, dim))
        near = move.core(got)
        return jnp.concatenate(
            [jnp.where(core == 0, got, near), jnp.where(core == 0, near, got)], axis=dim
        )

    def quarter_pieces(value, dim):
        got = move.over(part(value, place, value.shape[dim] // 4, dim))
        beside = move.side(got)
        return [got, beside, move.core(got), move.core(beside)]

    qkv_other = half_pieces(qkv_weight, 2)
    frames_own, frames_other = both(frames)
    out_other = half_pieces(out_weight, 0)
    bias_other = move.over(jnp.concatenate([up_bias, prior_bias]))
    up_pieces = quarter_pieces(up_weight, 1)
    down_pieces = quarter_pieces(down_weight, 0)
    prior_pieces = quarter_pieces(prior_weight, 1)
    logit_own, logit_other = both(logit_cotangent)
    out_own, out_other_cot = both(out_cotangent)
    hidden_width = up_bias.shape[0]
    up_bias_all = row(jnp.concatenate([up_bias, bias_other[:hidden_width]]))
    prior_bias_all = row(jnp.concatenate([prior_bias, bias_other[hidden_width:]]))
    seg = lax.dynamic_slice_in_dim(episode_starts(resets), here * blocks, blocks, 0)

    def blocked(n, dtype):
        return (jax.ShapeDtypeStruct((blocks, PAD, n), dtype), True)

    def fixed(shape, dtype):
        return (jax.ShapeDtypeStruct(shape, dtype), False)

    def b(*values):
        return [(v, True) for v in values]

    def w(*values):
        return [(v, False) for v in values]

    first, triple, mixed, middle, second = call(
        attend_kernel,
        scalars,
        b(frames_own, frames_other, seg)
        + w(row(first_gain), row(first_shift), qkv_weight, qkv_other, out_weight, out_other)
        + w(row(out_bias), row(second_gain), row(second_shift)),
        [blocked(width, BF), blocked(3 * width, BF), blocked(width, BF), blocked(width, F32), blocked(width, BF)],
        name="attend",
        flops=2 * mine * width * width * 4,
    )
    act, slope, ending, prior_in, block_own, block_send = call(
        feed_kernel,
        scalars,
        b(second, middle)
        + w(up_weight, *up_pieces, up_bias_all, down_weight, *down_pieces, row(down_bias))
        + w(row(prior_gain), row(prior_shift)),
        [blocked(2 * hidden_width, BF), blocked(2 * hidden_width, F32), blocked(width, F32)]
        + [blocked(width, BF), blocked(half, BF), blocked(half, BF)],
        name="feed",
        flops=2 * mine * width * hidden_width * 4,
    )
    block_got = move.over(block_send)
    n_logits = prior_bias.shape[0]
    logits_own, logits_send, grad_ending, ending_grad, vec_three, prior_bias_sum = call(
        prior_kernel,
        scalars,
        b(prior_in, ending)
        + w(prior_weight, *prior_pieces, prior_bias_all)
        + b(logit_own, logit_other, out_own, out_other_cot)
        + w(row(prior_gain)),
        [blocked(n_logits, F32), blocked(n_logits, BF), blocked(width, F32), blocked(width, BF)]
        + [fixed((3, width), F32), fixed((1, 2 * n_logits), F32)],
        name="prior",
        flops=2 * mine * width * n_logits * 4,
    )
    logits_got = move.over(logits_send)

    def pieces(n):
        return [fixed((4, n, 128), F32), fixed((4, n, 128), BF)], [pltpu.VMEM((4, n, 128), F32)]

    n_late = width + hidden_width
    outs, scratch = pieces(n_late)
    keep, send = call(
        late_grads_kernel,
        scalars,
        b(prior_in, logit_own, logit_other, act, ending_grad),
        outs,
        scratch,
        name="late_grads",
        flops=2 * mine * width * (2 * n_logits + 2 * hidden_width),
    )
    late = move.gather(move.reduce(keep, send))
    n_up = width * hidden_width // 512
    outs, scratch = pieces(n_up)
    grad_middle, middle_grad, vec_two, up_bias_sum, keep, send = call(
        feed_back_kernel,
        scalars,
        b(ending_grad, slope, second, middle, grad_ending)
        + w(up_weight, *up_pieces, down_weight, *down_pieces, row(second_gain)),
        [blocked(width, F32), blocked(width, BF), fixed((3, width), F32), fixed((1, 2 * hidden_width), F32)] + outs,
        scratch,
        name="feed_back",
        flops=2 * mine * width * hidden_width * 6,
    )
    middle_part = move.gather(move.reduce(keep, send))
    n_early = 256 + 768
    outs, scratch = pieces(n_early)
    frames_grad, frames_send, vec_one, keep, send = call(
        attend_back_kernel,
        scalars,
        b(middle_grad, grad_middle, frames_own, frames_other, first, triple, mixed, seg)
        + w(qkv_weight, qkv_other, out_weight, out_other, row(first_gain)),
        [blocked(half, F32), blocked(half, BF), fixed((2, width), F32)] + outs,
        scratch,
        name="attend_back",
        flops=2 * mine * width * width * 8,
    )
    frames_got = move.over(frames_send)
    early = move.gather(move.reduce(keep, send))

    def in_order(value):
        n = value.shape[1] // 2
        return jnp.where(here == 0, value[0], jnp.concatenate([value[0, n:], value[0, :n]]))

    vectors = jnp.concatenate(
        [vec_one.reshape(-1), vec_two.reshape(-1), vec_three.reshape(-1)]
        + [in_order(up_bias_sum), in_order(prior_bias_sum)]
    ).reshape(-1, 128)
    vectors = vectors + move.over(vectors)
    shift = 1
    while shift < n_dp:
        vectors = vectors + move.along(vectors, shift)
        shift *= 2
    vectors = vectors.reshape(-1)
    named = vectors[: 8 * width].reshape(8, width)
    rest = vectors[8 * width :]
    up_bias_grad = lax.dynamic_slice_in_dim(rest, here * hidden_width, hidden_width, 0)
    prior_bias_grad = lax.dynamic_slice_in_dim(rest, 2 * hidden_width + here * n_logits, n_logits, 0)

    prior_grad = late[:, :width].transpose(1, 0, 2).reshape(width, n_logits).astype(F32)
    down_grad = (
        late[:, width:].reshape(4, width // 128, -1, 128).transpose(0, 2, 1, 3).reshape(hidden_width, width)
    ).astype(F32)
    up_grad = (
        middle_part.reshape(4, -1, width, 128).transpose(2, 0, 1, 3).reshape(width, hidden_width).astype(F32)
    )
    out_grad = early[:, :256].transpose(1, 0, 2).reshape(half, width).astype(F32)
    qkv_grad = (
        early[:, 256:].reshape(4, 2, 3, 128, 128).transpose(2, 0, 3, 1, 4).reshape(3, width, half).astype(F32)
    )
    return (
        rows_of(here, block_own, block_got),
        rows_of(here, logits_own, logits_got),
        rows_of(here, frames_grad, frames_got),
        named[0],
        named[1],
        qkv_grad,
        out_grad,
        named[4],
        named[2],
        named[3],
        up_grad,
        up_bias_grad,
        down_grad,
        named[7],
        named[5],
        named[6],
        prior_grad,
        prior_bias_grad,
    )


def solution(mesh):
    rows, cols = P("dp", "tensor"), P(None, "tensor")
    placed = (
        rows, P("dp"), P(), P(), P(None, None, "tensor"), P("tensor", None), P(), P(), P(), cols, P("tensor"),
        P("tensor", None), P(), P(), P(), cols, P("tensor"), rows, rows,
    )
    given = (
        rows, rows, rows, P(), P(), P(None, None, "tensor"), P("tensor", None), P(), P(), P(), cols,
        P("tensor"), P("tensor", None), P(), P(), P(), cols, P("tensor"),
    )
    return jax.shard_map(
        functools.partial(local, mesh.shape["dp"], mesh.shape["tensor"]),
        mesh=mesh,
        in_specs=placed,
        out_specs=given,
        check_vma=False,
    )
```

time: 701 us -> 327 us (0.47)
  waiting for transfers between devices: 452 us -> 98.5 us
  Pallas kernels: 0 us -> 103 us
  blocking collectives: 82.4 us -> 0 us
  starting transfers between devices: 1.09 us -> 70.6 us
  matrix products: 54.6 us -> 0 us
  other arithmetic: 40.5 us -> 17.4 us
  local copies, waits for them, and re-layouts: 46.7 us -> 32 us
  between operations: 15.3 us -> 2.15 us
    reduce_scatter x5 -> x0, waiting for transfers between devices: 173 us -> none  [the longest x1 35.8 us: local(): lax.psum_scatter(attn_terms, 'tensor', scatter_dimension=1, tiled=True)]
    psum x1 -> x0, waiting for transfers between devices: 144 us -> none  [local(): lax.psum((grad_qkv, grad_out_weight, grad_up_weight, grad_up_bias, grad_d...]
    all_gather x5 -> x0, waiting for transfers between devices: 134 us -> none  [the longest x1 37.1 us: local(): middle_whole = lax.all_gather(middle, 'tensor', axis=1, tiled=True)]
    pallas_call x0 -> x6, Pallas kernels: none -> 103 us  [call(): pl.pallas_call(kernel, grid_spec=pltpu.PrefetchScalarGridSpec(num_scalar_...]
    ppermute x0 -> x64, waiting for transfers between devices: none -> 98.5 us  [swap(): return lax.ppermute(value, axes, [(i, i ^ mask) for i in range(count)])]
    psum x4 -> x0, blocking collectives: 82.4 us -> none  [the longest x1 61.2 us: local(): lax.psum((grad_qkv, grad_out_weight, grad_up_weight, grad_up_bias, grad_d...]
    ppermute x0 -> x64, starting transfers between devices: none -> 70.6 us  [swap(): return lax.ppermute(value, axes, [(i, i ^ mask) for i in range(count)])]
    dot_general x21 -> x0, matrix products: 54.6 us -> none  [the longest x1 7.84 us: local(): jnp.einsum('rd,fd->rf', ending_grad, down_weight, preferred_element_type=...]
  transfers between devices with their start and end apart: 11 -> 64, of which waited for: 11 -> 27; matrix products, arithmetic and copies ran while one was open for 5% -> 11% of each run, Pallas kernels for 0% -> 12%
where the time goes in v1:
time: 327 us; the launch traced here: 324 us
  Pallas kernels  103 us (31%)
  waiting for transfers between devices  98.5 us (30%)
  starting transfers between devices  70.6 us (22%)
  local copies, waits for them, and re-layouts  32 us (10%)
  other arithmetic  17.4 us (5%)
    pallas_call x6, Pallas kernels, call(): pl.pallas_call(kernel, grid_spec=pltpu.PrefetchScalarGridSpec(num_scalar_...  103 us
    ppermute x64, waiting for transfers between devices, swap(): return lax.ppermute(value, axes, [(i, i ^ mask) for i in range(count)])  98.5 us
    ppermute x64, starting transfers between devices, swap(): return lax.ppermute(value, axes, [(i, i ^ mask) for i in range(count)])  70.6 us
    unnamed x141, local copies, waits for them, and re-layouts  9.55 us
    dynamic_slice x5, local copies, waits for them, and re-layouts, part(): return lax.dynamic_slice_in_dim(value, index * size, size, dim)  7.45 us
  transfers between devices with their start and end apart: 64, of which 27 were waited for; matrix products, arithmetic and copies ran while one was open for 11% of the time, Pallas kernels for 12%

profile of v1, /device:TPU:0, one launch (start us, length us, event | category | flops | bytes accessed | tf_op | source)
XLA Modules:
  0.0 324.1 jit_solution(2553476992538295620)
XLA Ops:
  0.7 1.9 constant_dynamic-slice_fusion.8
  2.6 3.0 collective-permute-start.1
  5.5 1.6 constant_dynamic-slice_fusion.7
  7.1 1.7 constant_dynamic-slice_fusion.5
  8.8 2.0 collective-permute-start.10
  10.8 1.7 constant_dynamic-slice_fusion.6
  12.5 2.1 collective-permute-start.9
  15.4 2.1 constant_dynamic-slice_fusion
  20.4 8.7 %collective-permute-done.9 = f32[1536]{0:T(1024)S(1)} collective-permute-done((f32[1536]{0:T(1024)S(1)}, f32[1536]{0:T(1024)S(1)}, u32[]{:S(2)}, u32[]{:S(2)}) %collective-permute-start.9) | collective-permute-done | bytes 6176 | tf_op jit(solution)/shard_map/ppermute | solution.py:331
  29.1 1.7 collective-permute-start.15
  31.4 2.6 collective-permute-done.15.p0
  34.1 1.7 collective-permute-start
  35.8 1.5 collective-permute-start.16
  37.8 1.5 collective-permute-start.6
  39.5 2.8 collective-permute-done.16.p1
  43.4 3.7 %collective-permute-done.11.d1 = bf16[256,512]{1,0:T(8,128)(2,1)S(1)} collective-permute-done((bf16[256,512]{1,0:T(8,128)(2,1)S(1)}, bf16[256,512]{1,0:T(8,128)(2,1)S(1)}, u32[]{:S(2)}, u32[]{:S(2)}) %collective-permute-start.11) | collective-permute-done | bytes 262176 | tf_op jit(solution)/shard_map/ppermute | solution.py:331
  47.2 2.8 collective-permute-done.6.u1
  52.4 9.8 %attend.1 = (bf16[3,208,512]{2,1,0:T(8,128)(2,1)S(1)}, bf16[3,208,1536]{2,1,0:T(8,128)(2,1)}, bf16[3,208,512]{2,1,0:T(8,128)(2,1)S(1)}, f32[3,208,512]{2,1,0:T(8,128)}, bf16[3,208,512]{2,1,0:T(8,128)(2,1)S(1)}) custom-call(s32[2]{0:T(128)S(1)} %pad_add_fusion.s, bf16[3,208,256]{2,1,0:T(8,128)(2,1)S(1)} %pad.20.own, ...), custom_call_target="tpu_custom_call" | custom-call | flops 1258291200 | bytes 7860672 | tf_op jit(solution)/shard_map/attend/pallas_call | solution.py:311
  63.7 8.5 %feed.1 = (bf16[3,208,2048]{2,1,0:T(8,128)(2,1)}, f32[3,208,2048]{2,1,0:T(8,128)}, f32[3,208,512]{2,1,0:T(8,128)}, bf16[3,208,512]{2,1,0:T(8,128)(2,1)S(1)}, bf1...) custom-call(s32[2]{0:T(128)S(1)} %pad_add_fusion.s, bf16[3,208,512]{2,1,0:T(8,128)(2,1)S(1)} %get-tuple-element.48.second, ...), custom_call_target="tpu_custom_call" | custom-call | flops 2516582400 | bytes 16349184 | tf_op jit(solution)/shard_map/feed/pallas_call | solution.py:311
  73.0 6.4 %prior.2 = (f32[3,208,512]{2,1,0:T(8,128)S(1)}, bf16[3,208,512]{2,1,0:T(8,128)(2,1)S(1)}, f32[3,208,512]{2,1,0:T(8,128)}, bf16[3,208,512]{2,1,0:T(8,128)(2,1)S(1...) custom-call(s32[2]{0:T(128)S(1)} %pad_add_fusion.s, bf16[3,208,512]{2,1,0:T(8,128)(2,1)S(1)} %get-tuple-element.52.prior_in, ...), custom_call_target="tpu_custom_call" | custom-call | flops 1258291200 | bytes 8732672 | tf_op jit(solution)/shard_map/prior/pallas_call | solution.py:311
  80.2 23.4 %feed_back.1 = (f32[3,208,512]{2,1,0:T(8,128)}, bf16[3,208,512]{2,1,0:T(8,128)(2,1)S(1)}, f32[3,512]{1,0:T(4,128)S(1)}, f32[1,2048]{1,0:T(1,128)S(1)}, f32[4,102...) custom-call(s32[2]{0:T(128)S(1)} %pad_add_fusion.s, bf16[3,208,512]{2,1,0:T(8,128)(2,1)S(1)} %get-tuple-element.56.ending_grad, ...), custom_call_target="tpu_custom_call" | custom-call | flops 3774873600 | bytes 18219008 | tf_op jit(solution)/shard_map/feed_back/pallas_call | solution.py:311
  104.6 35.5 %attend_back.1 = (f32[3,208,256]{2,1,0:T(8,128)S(1)}, bf16[3,208,256]{2,1,0:T(8,128)(2,1)S(1)}, f32[2,512]{1,0:T(2,128)S(1)}, f32[4,1024,128]{2,1,0:T(8,128)}, bf16[4,1024,128]{2,1,0:T(8,128)(2,1)}) custom-call(s32[2]{0:T(128)S(1)} %pad_add_fusion.s, bf16[3,208,512]{2,1,0:T(8,128)(2,1)S(1)} %get-tuple-element.59.middle_grad, ...), custom_call_target="tpu_custom_call" | custom-call | flops 2516582400 | bytes 11960768 | tf_op jit(solution)/shard_map/attend_back/pallas_call | solution.py:311
  141.0 1.5 collective-permute-start.23
  142.5 2.4 collective-permute-done.23
  147.6 2.5 collective-permute-done.25
  151.5 2.4 collective-permute-done.26
  153.9 2.5 collective-permute-start.27
  158.6 20.0 %late_grads.1 = (f32[4,1536,128]{2,1,0:T(8,128)}, bf16[4,1536,128]{2,1,0:T(8,128)(2,1)S(1)}) custom-call(s32[2]{0:T(128)S(1)} %pad_add_fusion.s, bf16[3,208,512]{2,1,0:T(8,128)(2,1)S(1)} %copy-done.2, bf16[3,208,512]{2,1,0:T(8,128)(2,1)S(1)} %pad.22.logit_own, bf16[3,208,512]{2,1,0:T(8,128)(2,1)S(1)} %collective-permute-done.19.logit_other, ...), custom_call_target="tpu_custom_call" | custom-call | flops 1887436800 | bytes 9830400 | tf_op jit(solution)/shard_map/late_grads/pallas_call | solution.py:311
  179.3 1.5 collective-permute-start.22
  183.2 6.4 %collective-permute-done.22 = bf16[3,208,256]{2,1,0:T(8,128)(2,1)S(1)} collective-permute-done((bf16[3,208,256]{2,1,0:T(8,128)(2,1)S(1)}, bf16[3,208,256]{2,1,0:T(8,128)(2,1)S(1)}, u32[]{:S(2)}, u32[]{:S(2)}) %collective-permute-start.22) | collective-permute-done | bytes 319520 | tf_op jit(solution)/shard_map/ppermute | solution.py:331
  189.6 1.5 collective-permute-start.21
  191.3 5.2 %collective-permute-done.14 = bf16[3,208,256]{2,1,0:T(8,128)(2,1)S(1)} collective-permute-done((bf16[3,208,256]{2,1,0:T(8,128)(2,1)S(1)}, bf16[3,208,256]{2,1,0:T(8,128)(2,1)S(1)}, u32[]{:S(2)}, u32[]{:S(2)}) %collective-permute-start.14) | collective-permute-done | bytes 319520 | tf_op jit(solution)/shard_map/ppermute | solution.py:331
  198.5 11.2 %collective-permute-done.21 = bf16[3,208,512]{2,1,0:T(8,128)(2,1)S(1)} collective-permute-done((bf16[3,208,512]{2,1,0:T(8,128)(2,1)S(1)}, bf16[3,208,512]{2,1,0:T(8,128)(2,1)S(1)}, u32[]{:S(2)}, u32[]{:S(2)}) %collective-permute-start.21) | collective-permute-done | bytes 639008 | tf_op jit(solution)/shard_map/ppermute | solution.py:331
  210.1 1.7 pad_maximum_fusion
  212.9 1.6 collective-permute-start.41
  214.5 1.5 collective-permute-start.42
  216.8 1.6 collective-permute-start.29
  218.4 3.8 %collective-permute-done.41 = bf16[1024,128]{1,0:T(8,128)(2,1)S(1)} collective-permute-done((bf16[1024,128]{1,0:T(8,128)(2,1)S(1)}, bf16[1024,128]{1,0:T(8,128)(2,1)S(1)}, u32[]{:S(2)}, u32[]{:S(2)}) %collective-permute-start.41) | collective-permute-done | bytes 262176 | tf_op jit(solution)/shard_map/ppermute | solution.py:331
  222.2 1.5 collective-permute-start.30
  223.7 4.3 %collective-permute-done.42 = bf16[1024,128]{1,0:T(8,128)(2,1)S(1)} collective-permute-done((bf16[1024,128]{1,0:T(8,128)(2,1)S(1)}, bf16[1024,128]{1,0:T(8,128)(2,1)S(1)}, u32[]{:S(2)}, u32[]{:S(2)}) %collective-permute-start.42) | collective-permute-done | bytes 262176 | tf_op jit(solution)/shard_map/ppermute | solution.py:331
  228.9 1.6 collective-permute-start.44
  230.6 2.9 collective-permute-done.29
  233.9 5.0 %collective-permute-done.30 = bf16[1024,128]{1,0:T(8,128)(2,1)S(1)} collective-permute-done((bf16[1024,128]{1,0:T(8,128)(2,1)S(1)}, bf16[1024,128]{1,0:T(8,128)(2,1)S(1)}, u32[]{:S(2)}, u32[]{:S(2)}) %collective-permute-start.30) | collective-permute-done | bytes 262176 | tf_op jit(solution)/shard_map/ppermute | solution.py:331
  240.7 2.8 collective-permute-start.33
  248.0 1.8 collective-permute-done.33
  249.8 2.5 collective-permute-start.49
  252.7 1.6 collective-permute-start.36
  254.7 2.6 collective-permute-start.37
  258.2 1.8 collective-permute-start.54
  261.9 1.8 collective-permute-start.38
  263.7 6.2 %collective-permute-done.53 = bf16[1536,128]{1,0:T(8,128)(2,1)S(1)} collective-permute-done((bf16[1536,128]{1,0:T(8,128)(2,1)S(1)}, bf16[1536,128]{1,0:T(8,128)(2,1)S(1)}, u32[]{:S(2)}, u32[]{:S(2)}) %collective-permute-start.53) | collective-permute-done | bytes 393248 | tf_op jit(solution)/shard_map/ppermute | solution.py:331
  270.0 7.1 %collective-permute-done.55 = bf16[1536,128]{1,0:T(8,128)(2,1)S(1)} collective-permute-done((bf16[1536,128]{1,0:T(8,128)(2,1)S(1)}, bf16[1536,128]{1,0:T(8,128)(2,1)S(1)}, u32[]{:S(2)}, u32[]{:S(2)}) %collective-permute-start.55) | collective-permute-done | bytes 393248 | tf_op jit(solution)/shard_map/ppermute | solution.py:331
  277.3 2.5 collective-permute-start.56
  280.7 1.5 collective-permute-start.58
  282.4 3.5 %collective-permute-done.57 = bf16[384,128]{1,0:T(8,128)(2,1)S(1)} collective-permute-done((bf16[384,128]{1,0:T(8,128)(2,1)S(1)}, bf16[384,128]{1,0:T(8,128)(2,1)S(1)}, u32[]{:S(2)}, u32[]{:S(2)}) %collective-permute-start.57) | collective-permute-done | bytes 98336 | tf_op jit(solution)/shard_map/ppermute | solution.py:331
  285.9 2.2 collective-permute-done.58
  289.5 3.1 collective-permute-start.61
  293.5 3.0 collective-permute-done.60
  296.6 3.4 %collective-permute-start.62 = (bf16[1536,128]{1,0:T(8,128)(2,1)S(1)}, bf16[1536,128]{1,0:T(8,128)(2,1)S(1)}, u32[]{:S(2)}, u32[]{:S(2)}) collective-permute-start(bf16[1536,128]{1,0:T(8,128)(2,1)S(1)} %get-tuple-element.129), channel_id=1, source_target_pairs={{0,4},{2,6},{4,0},{6,2},{8,12},{10,14},{12,8},{14,10},{16,20},{18,... | collective-permute-start | bytes 1179656 | tf_op jit(solution)/shard_map/ppermute | solution.py:331
  301.6 4.2 %collective-permute-done.62 = bf16[1536,128]{1,0:T(8,128)(2,1)S(1)} collective-permute-done((bf16[1536,128]{1,0:T(8,128)(2,1)S(1)}, bf16[1536,128]{1,0:T(8,128)(2,1)S(1)}, u32[]{:S(2)}, u32[]{:S(2)}) %collective-permute-start.62) | collective-permute-done | bytes 393248 | tf_op jit(solution)/shard_map/ppermute | solution.py:331
  308.2 2.9 reshape.260
  315.4 2.4 reshape.258
  317.8 1.7 copy_bitcast_fusion.3
  322.3 1.5 copy.63
  (314 shorter events, 52.7 us)
Async XLA Ops:
  2.6 28.3 %collective-permute-start.1 = (bf16[3,512,128]{2,1,0:T(8,128)(2,1)}, bf16[3,512,128]{2,1,0:T(8,128)(2,1)}, u32[]{:S(2)}, u32[]{:S(2)}) collective-permute-start(bf16[3,512,128]{2,1,0:T(8,128)(2,1)} %constant_dynamic-slice_fusion.8), channel_id=1, source_target_pairs={{0,1},{1,0},{2,3},{3,2},{4,5},{5,4},{6,7},{7,6},{8,9},{9,8},{10,11... | collective-permute-start | bytes 1179656 | tf_op jit(solution)/shard_map/ppermute | solution.py:331
  7.1 23.7 %collective-permute-start.3 = (bf16[128,512]{1,0:T(8,128)(2,1)}, bf16[128,512]{1,0:T(8,128)(2,1)S(1)}, u32[]{:S(2)}, u32[]{:S(2)}) collective-permute-start(bf16[128,512]{1,0:T(8,128)(2,1)} %constant_dynamic-slice_fusion.7), channel_id=1, source_target_pairs={{0,1},{1,0},{2,3},{3,2},{4,5},{5,4},{6,7},{7,6},{8,9},{9,8},{10,11... | collective-permute-start | bytes 393224 | tf_op jit(solution)/shard_map/ppermute | solution.py:331
  8.8 28.5 %collective-permute-start.10 = (bf16[256,512]{1,0:T(8,128)(2,1)}, bf16[256,512]{1,0:T(8,128)(2,1)S(1)}, u32[]{:S(2)}, u32[]{:S(2)}) collective-permute-start(bf16[256,512]{1,0:T(8,128)(2,1)} %constant_dynamic-slice_fusion.5), channel_id=1, source_target_pairs={{0,1},{1,0},{2,3},{3,2},{4,5},{5,4},{6,7},{7,6},{8,9},{9,8},{10,11... | collective-permute-start | bytes 786440 | tf_op jit(solution)/shard_map/ppermute | solution.py:331
  12.5 25.4 %collective-permute-start.5 = (bf16[512,256]{1,0:T(8,128)(2,1)}, bf16[512,256]{1,0:T(8,128)(2,1)S(1)}, u32[]{:S(2)}, u32[]{:S(2)}) collective-permute-start(bf16[512,256]{1,0:T(8,128)(2,1)} %constant_dynamic-slice_fusion.6), channel_id=1, source_target_pairs={{0,1},{1,0},{2,3},{3,2},{4,5},{5,4},{6,7},{7,6},{8,9},{9,8},{10,11... | collective-permute-start | bytes 786440 | tf_op jit(solution)/shard_map/ppermute | solution.py:331
  12.5 16.6 %collective-permute-start.9 = (f32[1536]{0:T(1024)S(1)}, f32[1536]{0:T(1024)S(1)}, u32[]{:S(2)}, u32[]{:S(2)}) collective-permute-start(f32[1536]{0:T(1024)S(1)} %pad_maximum_fusion.13), channel_id=1, source_target_pairs={{0,1},{1,0},{2,3},{3,2},{4,5},{5,4},{6,7},{7,6},{8,9},{9,8},{10,11... | collective-permute-start | bytes 18440 | tf_op jit(solution)/shard_map/ppermute | solution.py:331
  29.1 5.0 %collective-permute-start.15 = (bf16[512,128]{1,0:T(8,128)(2,1)S(1)}, bf16[512,128]{1,0:T(8,128)(2,1)S(1)}, u32[]{:S(2)}, u32[]{:S(2)}) collective-permute-start(bf16[512,128]{1,0:T(8,128)(2,1)S(1)} %copy-done.63), channel_id=1, source_target_pairs={{0,1},{1,0},{2,3},{3,2},{4,5},{5,4},{6,7},{7,6},{8,9},{9,8},{10,11... | collective-permute-start | bytes 393224 | tf_op jit(solution)/shard_map/ppermute | solution.py:331
  30.8 5.0 %collective-permute-start.4 = (bf16[128,512]{1,0:T(8,128)(2,1)S(1)}, bf16[128,512]{1,0:T(8,128)(2,1)S(1)}, u32[]{:S(2)}, u32[]{:S(2)}) collective-permute-start(bf16[128,512]{1,0:T(8,128)(2,1)S(1)} %collective-permute-done.3), channel_id=1, source_target_pairs={{0,2},{2,0},{4,6},{6,4},{8,10},{10,8},{12,14},{14,12},{16,18},{18,... | collective-permute-start | bytes 393224 | tf_op jit(solution)/shard_map/ppermute | solution.py:331
  30.9 19.1 %collective-permute-start.2 = (bf16[3,512,128]{2,1,0:T(8,128)(2,1)}, bf16[3,512,128]{2,1,0:T(8,128)(2,1)S(1)}, u32[]{:S(2)}, u32[]{:S(2)}) collective-permute-start(bf16[3,512,128]{2,1,0:T(8,128)(2,1)} %collective-permute-done.1), channel_id=1, source_target_pairs={{0,2},{2,0},{4,6},{6,4},{8,10},{10,8},{12,14},{14,12},{16,18},{18,... | collective-permute-start | bytes 1179656 | tf_op jit(solution)/shard_map/ppermute | solution.py:331
  34.1 9.4 %collective-permute-start = (bf16[3,208,256]{2,1,0:T(8,128)(2,1)S(1)}, bf16[3,208,256]{2,1,0:T(8,128)(2,1)S(1)}, u32[]{:S(2)}, u32[]{:S(2)}) collective-permute-start(bf16[3,208,256]{2,1,0:T(8,128)(2,1)S(1)} %copy-done.62), channel_id=1, source_target_pairs={{0,1},{1,0},{2,3},{3,2},{4,5},{5,4},{6,7},{7,6},{8,9},{9,8},{10,11... | collective-permute-start | bytes 958472 | tf_op jit(solution)/shard_map/ppermute | solution.py:331
  35.8 6.4 %collective-permute-start.16 = (bf16[512,128]{1,0:T(8,128)(2,1)S(1)}, bf16[512,128]{1,0:T(8,128)(2,1)S(1)}, u32[]{:S(2)}, u32[]{:S(2)}) collective-permute-start(bf16[512,128]{1,0:T(8,128)(2,1)S(1)} %collective-permute-done.15.p0), channel_id=1, source_target_pairs={{0,4},{2,6},{4,0},{6,2},{8,12},{10,14},{12,8},{14,10},{16,20},{18,... | collective-permute-start | bytes 393224 | tf_op jit(solution)/shard_map/ppermute | solution.py:331
  37.3 9.9 %collective-permute-start.11 = (bf16[256,512]{1,0:T(8,128)(2,1)S(1)}, bf16[256,512]{1,0:T(8,128)(2,1)S(1)}, u32[]{:S(2)}, u32[]{:S(2)}) collective-permute-start(bf16[256,512]{1,0:T(8,128)(2,1)S(1)} %collective-permute-done.10.d0), channel_id=1, source_target_pairs={{0,4},{2,6},{4,0},{6,2},{8,12},{10,14},{12,8},{14,10},{16,20},{18,... | collective-permute-start | bytes 786440 | tf_op jit(solution)/shard_map/ppermute | solution.py:331
  37.8 12.1 %collective-permute-start.6 = (bf16[512,256]{1,0:T(8,128)(2,1)S(1)}, bf16[512,256]{1,0:T(8,128)(2,1)S(1)}, u32[]{:S(2)}, u32[]{:S(2)}) collective-permute-start(bf16[512,256]{1,0:T(8,128)(2,1)S(1)} %collective-permute-done.5.u0), channel_id=1, source_target_pairs={{0,4},{2,6},{4,0},{6,2},{8,12},{10,14},{12,8},{14,10},{16,20},{18,... | collective-permute-start | bytes 786440 | tf_op jit(solution)/shard_map/ppermute | solution.py:331
  42.2 30.7 %collective-permute-start.19 = (bf16[3,208,512]{2,1,0:T(8,128)(2,1)S(1)}, bf16[3,208,512]{2,1,0:T(8,128)(2,1)S(1)}, u32[]{:S(2)}, u32[]{:S(2)}) collective-permute-start(bf16[3,208,512]{2,1,0:T(8,128)(2,1)S(1)} %pad.23), channel_id=1, source_target_pairs={{0,1},{1,0},{2,3},{3,2},{4,5},{5,4},{6,7},{7,6},{8,9},{9,8},{10,11... | collective-permute-start | bytes 1916936 | tf_op jit(solution)/shard_map/ppermute | solution.py:331
  43.4 8.2 %collective-permute-start.12 = (bf16[256,512]{1,0:T(8,128)(2,1)S(1)}, bf16[256,512]{1,0:T(8,128)(2,1)S(1)}, u32[]{:S(2)}, u32[]{:S(2)}) collective-permute-start(bf16[256,512]{1,0:T(8,128)(2,1)S(1)} %collective-permute-done.10.d0), channel_id=1, source_target_pairs={{0,2},{2,0},{4,6},{6,4},{8,10},{10,8},{12,14},{14,12},{16,18},{18,... | collective-permute-start | bytes 786440 | tf_op jit(solution)/shard_map/ppermute | solution.py:331
  47.2 16.0 %collective-permute-start.7 = (bf16[512,256]{1,0:T(8,128)(2,1)S(1)}, bf16[512,256]{1,0:T(8,128)(2,1)S(1)}, u32[]{:S(2)}, u32[]{:S(2)}) collective-permute-start(bf16[512,256]{1,0:T(8,128)(2,1)S(1)} %collective-permute-done.5.u0), channel_id=1, source_target_pairs={{0,2},{2,0},{4,6},{6,4},{8,10},{10,8},{12,14},{14,12},{16,18},{18,... | collective-permute-start | bytes 786440 | tf_op jit(solution)/shard_map/ppermute | solution.py:331
  50.0 13.2 %collective-permute-start.13 = (bf16[256,512]{1,0:T(8,128)(2,1)S(1)}, bf16[256,512]{1,0:T(8,128)(2,1)S(1)}, u32[]{:S(2)}, u32[]{:S(2)}) collective-permute-start(bf16[256,512]{1,0:T(8,128)(2,1)S(1)} %collective-permute-done.11.d1), channel_id=1, source_target_pairs={{0,2},{2,0},{4,6},{6,4},{8,10},{10,8},{12,14},{14,12},{16,18},{18,... | collective-permute-start | bytes 786440 | tf_op jit(solution)/shard_map/ppermute | solution.py:331
  50.0 13.7 %collective-permute-start.8 = (bf16[512,256]{1,0:T(8,128)(2,1)S(1)}, bf16[512,256]{1,0:T(8,128)(2,1)S(1)}, u32[]{:S(2)}, u32[]{:S(2)}) collective-permute-start(bf16[512,256]{1,0:T(8,128)(2,1)S(1)} %collective-permute-done.6.u1), channel_id=1, source_target_pairs={{0,2},{2,0},{4,6},{6,4},{8,10},{10,8},{12,14},{14,12},{16,18},{18,... | collective-permute-start | bytes 786440 | tf_op jit(solution)/shard_map/ppermute | solution.py:331
  51.7 21.2 %collective-permute-start.20 = (bf16[3,208,256]{2,1,0:T(8,128)(2,1)S(1)}, bf16[3,208,256]{2,1,0:T(8,128)(2,1)S(1)}, u32[]{:S(2)}, u32[]{:S(2)}) collective-permute-start(bf16[3,208,256]{2,1,0:T(8,128)(2,1)S(1)} %pad.25), channel_id=1, source_target_pairs={{0,1},{1,0},{2,3},{3,2},{4,5},{5,4},{6,7},{7,6},{8,9},{9,8},{10,11... | collective-permute-start | bytes 958472 | tf_op jit(solution)/shard_map/ppermute | solution.py:331
  63.1 9.8 %collective-permute-start.17 = (bf16[512,128]{1,0:T(8,128)(2,1)S(1)}, bf16[512,128]{1,0:T(8,128)(2,1)S(1)}, u32[]{:S(2)}, u32[]{:S(2)}) collective-permute-start(bf16[512,128]{1,0:T(8,128)(2,1)S(1)} %collective-permute-done.15.p0), channel_id=1, source_target_pairs={{0,2},{2,0},{4,6},{6,4},{8,10},{10,8},{12,14},{14,12},{16,18},{18,... | collective-permute-start | bytes 393224 | tf_op jit(solution)/shard_map/ppermute | solution.py:331
  63.1 9.8 %collective-permute-start.18 = (bf16[512,128]{1,0:T(8,128)(2,1)S(1)}, bf16[512,128]{1,0:T(8,128)(2,1)S(1)}, u32[]{:S(2)}, u32[]{:S(2)}) collective-permute-start(bf16[512,128]{1,0:T(8,128)(2,1)S(1)} %collective-permute-done.16.p1), channel_id=1, source_target_pairs={{0,2},{2,0},{4,6},{6,4},{8,10},{10,8},{12,14},{14,12},{16,18},{18,... | collective-permute-start | bytes 393224 | tf_op jit(solution)/shard_map/ppermute | solution.py:331
  141.0 3.9 %collective-permute-start.23 = (f32[56,128]{1,0:T(8,128)S(1)}, f32[56,128]{1,0:T(8,128)S(1)}, u32[]{:S(2)}, u32[]{:S(2)}) collective-permute-start(f32[56,128]{1,0:T(8,128)S(1)} %bitcast.309), channel_id=1, source_target_pairs={{0,1},{1,0},{2,3},{3,2},{4,5},{5,4},{6,7},{7,6},{8,9},{9,8},{10,11... | collective-permute-start | bytes 86024 | tf_op jit(solution)/shard_map/ppermute | solution.py:331
  144.9 1.2 collective-permute-start.24
  146.1 3.9 %collective-permute-start.25 = (f32[56,128]{1,0:T(8,128)S(1)}, f32[56,128]{1,0:T(8,128)S(1)}, u32[]{:S(2)}, u32[]{:S(2)}) collective-permute-start(f32[56,128]{1,0:T(8,128)S(1)} %fusion.59), channel_id=1, source_target_pairs={{0,4},{2,6},{4,0},{6,2},{8,12},{10,14},{12,8},{14,10},{16,20},{18,... | collective-permute-start | bytes 86024 | tf_op jit(solution)/shard_map/ppermute | solution.py:331
  150.0 3.9 %collective-permute-start.26 = (f32[56,128]{1,0:T(8,128)S(1)}, f32[56,128]{1,0:T(8,128)S(1)}, u32[]{:S(2)}, u32[]{:S(2)}) collective-permute-start(f32[56,128]{1,0:T(8,128)S(1)} %add.180), channel_id=1, source_target_pairs={{0,8},{2,10},{4,12},{6,14},{8,0},{10,2},{12,4},{14,6},{16,24},{18,... | collective-permute-start | bytes 86024 | tf_op jit(solution)/shard_map/ppermute | solution.py:331
  153.9 26.9 %collective-permute-start.27 = (f32[56,128]{1,0:T(8,128)S(1)}, f32[56,128]{1,0:T(8,128)S(1)}, u32[]{:S(2)}, u32[]{:S(2)}) collective-permute-start(f32[56,128]{1,0:T(8,128)S(1)} %add.181), channel_id=1, source_target_pairs={{0,16},{2,18},{4,20},{6,22},{8,24},{10,26},{12,28},{14,30},{16,0},... | collective-permute-start | bytes 86024 | tf_op jit(solution)/shard_map/ppermute | solution.py:331
  178.6 78.7 %collective-permute-start.52 = (bf16[4,1536,128]{2,1,0:T(8,128)(2,1)S(1)}, bf16[4,1536,128]{2,1,0:T(8,128)(2,1)S(1)}, u32[]{:S(2)}, u32[]{:S(2)}) collective-permute-start(bf16[4,1536,128]{2,1,0:T(8,128)(2,1)S(1)} %get-tuple-element.77), channel_id=1, source_target_pairs={{0,2},{2,0},{4,6},{6,4},{8,10},{10,8},{12,14},{14,12},{16,18},{18,... | collective-permute-start | bytes 4718600 | tf_op jit(solution)/shard_map/ppermute | solution.py:331
  178.7 33.0 %collective-permute-start.40 = (bf16[4,1024,128]{2,1,0:T(8,128)(2,1)S(1)}, bf16[4,1024,128]{2,1,0:T(8,128)(2,1)S(1)}, u32[]{:S(2)}, u32[]{:S(2)}) collective-permute-start(bf16[4,1024,128]{2,1,0:T(8,128)(2,1)S(1)} %copy-done.15), channel_id=1, source_target_pairs={{0,2},{2,0},{4,6},{6,4},{8,10},{10,8},{12,14},{14,12},{16,18},{18,... | collective-permute-start | bytes 3145736 | tf_op jit(solution)/shard_map/ppermute | solution.py:331
  179.2 37.2 %collective-permute-start.28 = (bf16[4,1024,128]{2,1,0:T(8,128)(2,1)S(1)}, bf16[4,1024,128]{2,1,0:T(8,128)(2,1)S(1)}, u32[]{:S(2)}, u32[]{:S(2)}) collective-permute-start(bf16[4,1024,128]{2,1,0:T(8,128)(2,1)S(1)} %copy-done.67), channel_id=1, source_target_pairs={{0,2},{2,0},{4,6},{6,4},{8,10},{10,8},{12,14},{14,12},{16,18},{18,... | collective-permute-start | bytes 3145736 | tf_op jit(solution)/shard_map/ppermute | solution.py:331
  179.3 10.3 %collective-permute-start.22 = (bf16[3,208,256]{2,1,0:T(8,128)(2,1)S(1)}, bf16[3,208,256]{2,1,0:T(8,128)(2,1)S(1)}, u32[]{:S(2)}, u32[]{:S(2)}) collective-permute-start(bf16[3,208,256]{2,1,0:T(8,128)(2,1)S(1)} %get-tuple-element.65), channel_id=1, source_target_pairs={{0,1},{1,0},{2,3},{3,2},{4,5},{5,4},{6,7},{7,6},{8,9},{9,8},{10,11... | collective-permute-start | bytes 958472 | tf_op jit(solution)/shard_map/ppermute | solution.py:331
  180.8 15.7 %collective-permute-start.14 = (bf16[3,208,256]{2,1,0:T(8,128)(2,1)S(1)}, bf16[3,208,256]{2,1,0:T(8,128)(2,1)S(1)}, u32[]{:S(2)}, u32[]{:S(2)}) collective-permute-start(bf16[3,208,256]{2,1,0:T(8,128)(2,1)S(1)} %copy-done.21), channel_id=1, source_target_pairs={{0,1},{1,0},{2,3},{3,2},{4,5},{5,4},{6,7},{7,6},{8,9},{9,8},{10,11... | collective-permute-start | bytes 958472 | tf_op jit(solution)/shard_map/ppermute | solution.py:331
  189.6 20.1 %collective-permute-start.21 = (bf16[3,208,512]{2,1,0:T(8,128)(2,1)S(1)}, bf16[3,208,512]{2,1,0:T(8,128)(2,1)S(1)}, u32[]{:S(2)}, u32[]{:S(2)}) collective-permute-start(bf16[3,208,512]{2,1,0:T(8,128)(2,1)S(1)} %copy-done.17), channel_id=1, source_target_pairs={{0,1},{1,0},{2,3},{3,2},{4,5},{5,4},{6,7},{7,6},{8,9},{9,8},{10,11... | collective-permute-start | bytes 1916936 | tf_op jit(solution)/shard_map/ppermute | solution.py:331
  212.9 9.3 %collective-permute-start.41 = (bf16[1024,128]{1,0:T(8,128)(2,1)S(1)}, bf16[1024,128]{1,0:T(8,128)(2,1)S(1)}, u32[]{:S(2)}, u32[]{:S(2)}) collective-permute-start(bf16[1024,128]{1,0:T(8,128)(2,1)S(1)} %get-tuple-element.99), channel_id=1, source_target_pairs={{0,4},{2,6},{4,0},{6,2},{8,12},{10,14},{12,8},{14,10},{16,20},{18,... | collective-permute-start | bytes 786440 | tf_op jit(solution)/shard_map/ppermute | solution.py:331
  214.5 13.5 %collective-permute-start.42 = (bf16[1024,128]{1,0:T(8,128)(2,1)S(1)}, bf16[1024,128]{1,0:T(8,128)(2,1)S(1)}, u32[]{:S(2)}, u32[]{:S(2)}) collective-permute-start(bf16[1024,128]{1,0:T(8,128)(2,1)S(1)} %get-tuple-element.101), channel_id=1, source_target_pairs={{0,1},{1,0},{2,3},{3,2},{4,5},{5,4},{6,7},{7,6},{8,9},{9,8},{10,11... | collective-permute-start | bytes 786440 | tf_op jit(solution)/shard_map/ppermute | solution.py:331
  216.0 12.8 %collective-permute-start.43 = (bf16[1024,128]{1,0:T(8,128)(2,1)S(1)}, bf16[1024,128]{1,0:T(8,128)(2,1)S(1)}, u32[]{:S(2)}, u32[]{:S(2)}) collective-permute-start(bf16[1024,128]{1,0:T(8,128)(2,1)S(1)} %get-tuple-element.100), channel_id=1, source_target_pairs={{0,5},{1,4},{2,7},{3,6},{4,1},{5,0},{6,3},{7,2},{8,13},{9,12},{10,... | collective-permute-start | bytes 786440 | tf_op jit(solution)/shard_map/ppermute | solution.py:331
  216.8 16.6 %collective-permute-start.29 = (bf16[1024,128]{1,0:T(8,128)(2,1)S(1)}, bf16[1024,128]{1,0:T(8,128)(2,1)S(1)}, u32[]{:S(2)}, u32[]{:S(2)}) collective-permute-start(bf16[1024,128]{1,0:T(8,128)(2,1)S(1)} %get-tuple-element.106), channel_id=1, source_target_pairs={{0,4},{2,6},{4,0},{6,2},{8,12},{10,14},{12,8},{14,10},{16,20},{18,... | collective-permute-start | bytes 786440 | tf_op jit(solution)/shard_map/ppermute | solution.py:331
  222.2 16.7 %collective-permute-start.30 = (bf16[1024,128]{1,0:T(8,128)(2,1)S(1)}, bf16[1024,128]{1,0:T(8,128)(2,1)S(1)}, u32[]{:S(2)}, u32[]{:S(2)}) collective-permute-start(bf16[1024,128]{1,0:T(8,128)(2,1)S(1)} %get-tuple-element.108), channel_id=1, source_target_pairs={{0,1},{1,0},{2,3},{3,2},{4,5},{5,4},{6,7},{7,6},{8,9},{9,8},{10,11... | collective-permute-start | bytes 786440 | tf_op jit(solution)/shard_map/ppermute | solution.py:331
  228.0 12.2 %collective-permute-start.31 = (bf16[1024,128]{1,0:T(8,128)(2,1)S(1)}, bf16[1024,128]{1,0:T(8,128)(2,1)S(1)}, u32[]{:S(2)}, u32[]{:S(2)}) collective-permute-start(bf16[1024,128]{1,0:T(8,128)(2,1)S(1)} %get-tuple-element.107), channel_id=1, source_target_pairs={{0,5},{1,4},{2,7},{3,6},{4,1},{5,0},{6,3},{7,2},{8,13},{9,12},{10,... | collective-permute-start | bytes 786440 | tf_op jit(solution)/shard_map/ppermute | solution.py:331
  228.9 11.8 %collective-permute-start.44 = (bf16[256,128]{1,0:T(8,128)(2,1)S(1)}, bf16[256,128]{1,0:T(8,128)(2,1)S(1)}, u32[]{:S(2)}, u32[]{:S(2)}) collective-permute-start(bf16[256,128]{1,0:T(8,128)(2,1)S(1)} %get-tuple-element.122), channel_id=1, source_target_pairs={{0,8},{2,10},{4,12},{6,14},{8,0},{10,2},{12,4},{14,6},{16,24},{18,... | collective-permute-start | bytes 196616 | tf_op jit(solution)/shard_map/ppermute | solution.py:331
  233.4 10.1 %collective-permute-start.45 = (bf16[256,128]{1,0:T(8,128)(2,1)S(1)}, bf16[256,128]{1,0:T(8,128)(2,1)S(1)}, u32[]{:S(2)}, u32[]{:S(2)}) collective-permute-start(bf16[256,128]{1,0:T(8,128)(2,1)S(1)} %get-tuple-element.124), channel_id=1, source_target_pairs={{0,16},{2,18},{4,20},{6,22},{8,24},{10,26},{12,28},{14,30},{16,0},... | collective-permute-start | bytes 196616 | tf_op jit(solution)/shard_map/ppermute | solution.py:331
  238.9 6.6 %collective-permute-start.46 = (bf16[256,128]{1,0:T(8,128)(2,1)S(1)}, bf16[256,128]{1,0:T(8,128)(2,1)S(1)}, u32[]{:S(2)}, u32[]{:S(2)}) collective-permute-start(bf16[256,128]{1,0:T(8,128)(2,1)S(1)} %get-tuple-element.123), channel_id=1, source_target_pairs={{0,24},{2,26},{4,28},{6,30},{8,16},{10,18},{12,20},{14,22},{16,8},... | collective-permute-start | bytes 196616 | tf_op jit(solution)/shard_map/ppermute | solution.py:331
  240.4 6.7 %collective-permute-start.32 = (bf16[256,128]{1,0:T(8,128)(2,1)S(1)}, bf16[256,128]{1,0:T(8,128)(2,1)S(1)}, u32[]{:S(2)}, u32[]{:S(2)}) collective-permute-start(bf16[256,128]{1,0:T(8,128)(2,1)S(1)} %get-tuple-element.125), channel_id=1, source_target_pairs={{0,8},{2,10},{4,12},{6,14},{8,0},{10,2},{12,4},{14,6},{16,24},{18,... | collective-permute-start | bytes 196616 | tf_op jit(solution)/shard_map/ppermute | solution.py:331
  240.7 9.1 %collective-permute-start.33 = (bf16[256,128]{1,0:T(8,128)(2,1)S(1)}, bf16[256,128]{1,0:T(8,128)(2,1)S(1)}, u32[]{:S(2)}, u32[]{:S(2)}) collective-permute-start(bf16[256,128]{1,0:T(8,128)(2,1)S(1)} %get-tuple-element.127), channel_id=1, source_target_pairs={{0,16},{2,18},{4,20},{6,22},{8,24},{10,26},{12,28},{14,30},{16,0},... | collective-permute-start | bytes 196616 | tf_op jit(solution)/shard_map/ppermute | solution.py:331
  243.5 8.8 %collective-permute-start.34 = (bf16[256,128]{1,0:T(8,128)(2,1)S(1)}, bf16[256,128]{1,0:T(8,128)(2,1)S(1)}, u32[]{:S(2)}, u32[]{:S(2)}) collective-permute-start(bf16[256,128]{1,0:T(8,128)(2,1)S(1)} %get-tuple-element.126), channel_id=1, source_target_pairs={{0,24},{2,26},{4,28},{6,30},{8,16},{10,18},{12,20},{14,22},{16,8},... | collective-permute-start | bytes 196616 | tf_op jit(solution)/shard_map/ppermute | solution.py:331
  245.6 7.1 %collective-permute-start.47 = (bf16[256,128]{1,0:T(8,128)(2,1)S(1)}, bf16[256,128]{1,0:T(8,128)(2,1)S(1)}, u32[]{:S(2)}, u32[]{:S(2)}) collective-permute-start(bf16[256,128]{1,0:T(8,128)(2,1)S(1)} %fusion.34), channel_id=1, source_target_pairs={{0,8},{2,10},{4,12},{6,14},{8,0},{10,2},{12,4},{14,6},{16,24},{18,... | collective-permute-start | bytes 196616 | tf_op jit(solution)/shard_map/ppermute | solution.py:331
  247.1 7.6 %collective-permute-start.48 = (bf16[256,128]{1,0:T(8,128)(2,1)S(1)}, bf16[256,128]{1,0:T(8,128)(2,1)S(1)}, u32[]{:S(2)}, u32[]{:S(2)}) collective-permute-start(bf16[256,128]{1,0:T(8,128)(2,1)S(1)} %fusion.34), channel_id=1, source_target_pairs={{0,16},{2,18},{4,20},{6,22},{8,24},{10,26},{12,28},{14,30},{16,0},... | collective-permute-start | bytes 196616 | tf_op jit(solution)/shard_map/ppermute | solution.py:331
  249.8 7.5 %collective-permute-start.49 = (bf16[256,128]{1,0:T(8,128)(2,1)S(1)}, bf16[256,128]{1,0:T(8,128)(2,1)S(1)}, u32[]{:S(2)}, u32[]{:S(2)}) collective-permute-start(bf16[256,128]{1,0:T(8,128)(2,1)S(1)} %fusion.34), channel_id=1, source_target_pairs={{0,24},{2,26},{4,28},{6,30},{8,16},{10,18},{12,20},{14,22},{16,8},... | collective-permute-start | bytes 196616 | tf_op jit(solution)/shard_map/ppermute | solution.py:331
  252.4 7.6 %collective-permute-start.35 = (bf16[256,128]{1,0:T(8,128)(2,1)S(1)}, bf16[256,128]{1,0:T(8,128)(2,1)S(1)}, u32[]{:S(2)}, u32[]{:S(2)}) collective-permute-start(bf16[256,128]{1,0:T(8,128)(2,1)S(1)} %fusion.37), channel_id=1, source_target_pairs={{0,8},{2,10},{4,12},{6,14},{8,0},{10,2},{12,4},{14,6},{16,24},{18,... | collective-permute-start | bytes 196616 | tf_op jit(solution)/shard_map/ppermute | solution.py:331
  252.7 8.7 %collective-permute-start.36 = (bf16[256,128]{1,0:T(8,128)(2,1)S(1)}, bf16[256,128]{1,0:T(8,128)(2,1)S(1)}, u32[]{:S(2)}, u32[]{:S(2)}) collective-permute-start(bf16[256,128]{1,0:T(8,128)(2,1)S(1)} %fusion.37), channel_id=1, source_target_pairs={{0,16},{2,18},{4,20},{6,22},{8,24},{10,26},{12,28},{14,30},{16,0},... | collective-permute-start | bytes 196616 | tf_op jit(solution)/shard_map/ppermute | solution.py:331
  254.7 7.1 %collective-permute-start.37 = (bf16[256,128]{1,0:T(8,128)(2,1)S(1)}, bf16[256,128]{1,0:T(8,128)(2,1)S(1)}, u32[]{:S(2)}, u32[]{:S(2)}) collective-permute-start(bf16[256,128]{1,0:T(8,128)(2,1)S(1)} %fusion.37), channel_id=1, source_target_pairs={{0,24},{2,26},{4,28},{6,30},{8,16},{10,18},{12,20},{14,22},{16,8},... | collective-permute-start | bytes 196616 | tf_op jit(solution)/shard_map/ppermute | solution.py:331
  257.8 12.1 %collective-permute-start.53 = (bf16[1536,128]{1,0:T(8,128)(2,1)S(1)}, bf16[1536,128]{1,0:T(8,128)(2,1)S(1)}, u32[]{:S(2)}, u32[]{:S(2)}) collective-permute-start(bf16[1536,128]{1,0:T(8,128)(2,1)S(1)} %get-tuple-element.90), channel_id=1, source_target_pairs={{0,4},{2,6},{4,0},{6,2},{8,12},{10,14},{12,8},{14,10},{16,20},{18,... | collective-permute-start | bytes 1179656 | tf_op jit(solution)/shard_map/ppermute | solution.py:331
  258.2 11.8 %collective-permute-start.54 = (bf16[1536,128]{1,0:T(8,128)(2,1)S(1)}, bf16[1536,128]{1,0:T(8,128)(2,1)S(1)}, u32[]{:S(2)}, u32[]{:S(2)}) collective-permute-start(bf16[1536,128]{1,0:T(8,128)(2,1)S(1)} %get-tuple-element.92), channel_id=1, source_target_pairs={{0,1},{1,0},{2,3},{3,2},{4,5},{5,4},{6,7},{7,6},{8,9},{9,8},{10,11... | collective-permute-start | bytes 1179656 | tf_op jit(solution)/shard_map/ppermute | solution.py:331
  259.9 17.1 %collective-permute-start.55 = (bf16[1536,128]{1,0:T(8,128)(2,1)S(1)}, bf16[1536,128]{1,0:T(8,128)(2,1)S(1)}, u32[]{:S(2)}, u32[]{:S(2)}) collective-permute-start(bf16[1536,128]{1,0:T(8,128)(2,1)S(1)} %get-tuple-element.91), channel_id=1, source_target_pairs={{0,5},{1,4},{2,7},{3,6},{4,1},{5,0},{6,3},{7,2},{8,13},{9,12},{10,... | collective-permute-start | bytes 1179656 | tf_op jit(solution)/shard_map/ppermute | solution.py:331
  261.4 20.8 %collective-permute-start.50 = (bf16[1024,128]{1,0:T(8,128)(2,1)S(1)}, bf16[1024,128]{1,0:T(8,128)(2,1)S(1)}, u32[]{:S(2)}, u32[]{:S(2)}) collective-permute-start(bf16[1024,128]{1,0:T(8,128)(2,1)S(1)} %get-tuple-element.135), channel_id=1, source_target_pairs={{0,4},{2,6},{4,0},{6,2},{8,12},{10,14},{12,8},{14,10},{16,20},{18,... | collective-permute-start | bytes 786440 | tf_op jit(solution)/shard_map/ppermute | solution.py:331
  261.9 30.7 %collective-permute-start.38 = (bf16[1024,128]{1,0:T(8,128)(2,1)S(1)}, bf16[1024,128]{1,0:T(8,128)(2,1)S(1)}, u32[]{:S(2)}, u32[]{:S(2)}) collective-permute-start(bf16[1024,128]{1,0:T(8,128)(2,1)S(1)} %get-tuple-element.141), channel_id=1, source_target_pairs={{0,4},{2,6},{4,0},{6,2},{8,12},{10,14},{12,8},{14,10},{16,20},{18,... | collective-permute-start | bytes 786440 | tf_op jit(solution)/shard_map/ppermute | solution.py:331
  277.3 5.1 %collective-permute-start.56 = (bf16[384,128]{1,0:T(8,128)(2,1)S(1)}, bf16[384,128]{1,0:T(8,128)(2,1)S(1)}, u32[]{:S(2)}, u32[]{:S(2)}) collective-permute-start(bf16[384,128]{1,0:T(8,128)(2,1)S(1)} %get-tuple-element.111), channel_id=1, source_target_pairs={{0,8},{2,10},{4,12},{6,14},{8,0},{10,2},{12,4},{14,6},{16,24},{18,... | collective-permute-start | bytes 294920 | tf_op jit(solution)/shard_map/ppermute | solution.py:331
  279.8 6.1 %collective-permute-start.57 = (bf16[384,128]{1,0:T(8,128)(2,1)S(1)}, bf16[384,128]{1,0:T(8,128)(2,1)S(1)}, u32[]{:S(2)}, u32[]{:S(2)}) collective-permute-start(bf16[384,128]{1,0:T(8,128)(2,1)S(1)} %get-tuple-element.113), channel_id=1, source_target_pairs={{0,16},{2,18},{4,20},{6,22},{8,24},{10,26},{12,28},{14,30},{16,0},... | collective-permute-start | bytes 294920 | tf_op jit(solution)/shard_map/ppermute | solution.py:331
  280.7 7.4 %collective-permute-start.58 = (bf16[384,128]{1,0:T(8,128)(2,1)S(1)}, bf16[384,128]{1,0:T(8,128)(2,1)S(1)}, u32[]{:S(2)}, u32[]{:S(2)}) collective-permute-start(bf16[384,128]{1,0:T(8,128)(2,1)S(1)} %get-tuple-element.112), channel_id=1, source_target_pairs={{0,24},{2,26},{4,28},{6,30},{8,16},{10,18},{12,20},{14,22},{16,8},... | collective-permute-start | bytes 294920 | tf_op jit(solution)/shard_map/ppermute | solution.py:331
  282.3 17.7 %collective-permute-start.51 = (bf16[2,1024,128]{2,1,0:T(8,128)(2,1)S(1)}, bf16[2,1024,128]{2,1,0:T(8,128)(2,1)S(1)}, u32[]{:S(2)}, u32[]{:S(2)}) collective-permute-start(bf16[2,1024,128]{2,1,0:T(8,128)(2,1)S(1)} %pad_maximum_fusion.8), channel_id=1, source_target_pairs={{0,2},{2,0},{4,6},{6,4},{8,10},{10,8},{12,14},{14,12},{16,18},{18,... | collective-permute-start | bytes 1572872 | tf_op jit(solution)/shard_map/ppermute | solution.py:331
  288.2 5.3 %collective-permute-start.59 = (bf16[384,128]{1,0:T(8,128)(2,1)S(1)}, bf16[384,128]{1,0:T(8,128)(2,1)S(1)}, u32[]{:S(2)}, u32[]{:S(2)}) collective-permute-start(bf16[384,128]{1,0:T(8,128)(2,1)S(1)} %fusion.31), channel_id=1, source_target_pairs={{0,8},{2,10},{4,12},{6,14},{8,0},{10,2},{12,4},{14,6},{16,24},{18,... | collective-permute-start | bytes 294920 | tf_op jit(solution)/shard_map/ppermute | solution.py:331
  288.9 7.6 %collective-permute-start.60 = (bf16[384,128]{1,0:T(8,128)(2,1)S(1)}, bf16[384,128]{1,0:T(8,128)(2,1)S(1)}, u32[]{:S(2)}, u32[]{:S(2)}) collective-permute-start(bf16[384,128]{1,0:T(8,128)(2,1)S(1)} %fusion.31), channel_id=1, source_target_pairs={{0,16},{2,18},{4,20},{6,22},{8,24},{10,26},{12,28},{14,30},{16,0},... | collective-permute-start | bytes 294920 | tf_op jit(solution)/shard_map/ppermute | solution.py:331
  289.5 7.0 %collective-permute-start.61 = (bf16[384,128]{1,0:T(8,128)(2,1)S(1)}, bf16[384,128]{1,0:T(8,128)(2,1)S(1)}, u32[]{:S(2)}, u32[]{:S(2)}) collective-permute-start(bf16[384,128]{1,0:T(8,128)(2,1)S(1)} %fusion.31), channel_id=1, source_target_pairs={{0,24},{2,26},{4,28},{6,30},{8,16},{10,18},{12,20},{14,22},{16,8},... | collective-permute-start | bytes 294920 | tf_op jit(solution)/shard_map/ppermute | solution.py:331
  293.5 17.7 %collective-permute-start.39 = (bf16[2,1024,128]{2,1,0:T(8,128)(2,1)}, bf16[2,1024,128]{2,1,0:T(8,128)(2,1)}, u32[]{:S(2)}, u32[]{:S(2)}) collective-permute-start(bf16[2,1024,128]{2,1,0:T(8,128)(2,1)} %pad_maximum_fusion.7), channel_id=1, source_target_pairs={{0,2},{2,0},{4,6},{6,4},{8,10},{10,8},{12,14},{14,12},{16,18},{18,... | collective-permute-start | bytes 1572872 | tf_op jit(solution)/shard_map/ppermute | solution.py:331
  296.6 9.1 %collective-permute-start.62 = (bf16[1536,128]{1,0:T(8,128)(2,1)S(1)}, bf16[1536,128]{1,0:T(8,128)(2,1)S(1)}, u32[]{:S(2)}, u32[]{:S(2)}) collective-permute-start(bf16[1536,128]{1,0:T(8,128)(2,1)S(1)} %get-tuple-element.129), channel_id=1, source_target_pairs={{0,4},{2,6},{4,0},{6,2},{8,12},{10,14},{12,8},{14,10},{16,20},{18,... | collective-permute-start | bytes 1179656 | tf_op jit(solution)/shard_map/ppermute | solution.py:331
  306.7 12.8 %collective-permute-start.63 = (bf16[2,1536,128]{2,1,0:T(8,128)(2,1)}, bf16[2,1536,128]{2,1,0:T(8,128)(2,1)S(1)}, u32[]{:S(2)}, u32[]{:S(2)}) collective-permute-start(bf16[2,1536,128]{2,1,0:T(8,128)(2,1)} %pad_maximum_fusion.5), channel_id=1, source_target_pairs={{0,2},{2,0},{4,6},{6,4},{8,10},{10,8},{12,14},{14,12},{16,18},{18,... | collective-permute-start | bytes 2359304 | tf_op jit(solution)/shard_map/ppermute | solution.py:331
  (68 other events, 725.8 us)

commit v2 on v1

--- a/solution.py
+++ b/solution.py
@@ -177,68 +177,96 @@
     accumulate(step, vec_ref, (slice(0, 3), slice(None)), rows)
 
 
-def piece_targets(s, step, last, keep, sums, send):
-    def put(h, j, rows, value):
-        if j < 2:
-            accumulate(step, keep, (2 * h + j, rows), value)
-        else:
-            accumulate(step, sums, (2 * h + j - 2, rows), value)
-
-    def finish():
-        @pl.when(step == last)
-        def _():
-            send[...] = sums[...].astype(BF)
-
-    return put, finish
-
-
-def late_grads_kernel(
-    s, prior_in, logit_own, logit_other, act, ending_grad, keep, send, sums,
+def piece_of(step):
+    return step // 4, step % 4
+
+
+def store_piece(step, keep, send, rows, value):
+    place = step % 4
+
+    @pl.when(place < 2)
+    def _():
+        keep[0, rows] = value
+
+    @pl.when(place >= 2)
+    def _():
+        send[0, rows] = value.astype(BF)
+
+
+def flat(ref):
+    return ref[...].reshape(-1, ref.shape[-1])
+
+
+def late_grads_kernel(s, prior_in, logit_own, logit_other, act, ending_grad, keep, send, turned):
+    step = pl.program_id(0)
+
+    @pl.when(step == 0)
+    def _():
+        turned[...] = flat(prior_in).T
+
+    cot = jnp.where(step < 4, flat(logit_own), flat(logit_other))
+    n = turned.shape[0]
+    store_piece(step, keep, send, slice(0, n), mm(turned[...], cot))
+    value = mm_at(flat(act), flat(ending_grad))
+    m = value.shape[0]
+    for t in range(value.shape[1] // 128):
+        store_piece(step, keep, send, slice(n + t * m, n + t * m + m), value[:, t * 128 : t * 128 + 128])
+
+
+def up_grads_kernel(s, second, hidden_grad, keep, send, turned):
+    step = pl.program_id(0)
+
+    @pl.when(step == 0)
+    def _():
+        turned[...] = flat(second).T
+
+    value = mm(turned[...], flat(hidden_grad))
+    n = value.shape[0]
+    for t in range(value.shape[1] // 128):
+        store_piece(step, keep, send, slice(t * n, t * n + n), value[:, t * 128 : t * 128 + 128])
+
+
+def early_grads_kernel(s, mixed, middle_grad, first, triple_grad, keep, send, turned, turned_mixed):
+    step = pl.program_id(0)
+
+    @pl.when(step == 0)
+    def _():
+        turned[...] = flat(first).T
+
+    @pl.when(step % 4 == 0)
+    def _():
+        turned_mixed[...] = flat(mixed).T
+
+    n = turned_mixed.shape[0]
+    store_piece(step, keep, send, slice(0, n), mm(turned_mixed[...], flat(middle_grad)))
+    at = pl.ds(pl.multiple_of((s[1] ^ (step % 4)) * 128, 128), 128)
+    value = mm(turned[at, :], flat(triple_grad))
+    for c in range(3):
+        for t in range(2):
+            start = n + (t * 3 + c) * 128
+            piece = value[:, c * 256 + t * 128 : c * 256 + t * 128 + 128]
+            store_piece(step, keep, send, slice(start, start + 128), piece)
+
+
+def feed_back_kernel(
+    s, ending_grad, slope, second, middle, grad_ending, up, u0, u1, u2, u3, down, d0, d1, d2, d3, gain,
+    hidden_grad_ref, grad_middle_ref, middle_grad_ref, vec_ref, bias_ref,
 ):
     step = pl.program_id(0)
-    put, finish = piece_targets(s, step, pl.num_programs(0) - 1, keep, sums, send)
-    x = prior_in[0]
     grad = ending_grad[0]
-    half = act.shape[2] // 2
-    n = x.shape[1]
-    for h in range(2):
-        for j in range(4):
-            place = s[1] ^ j
-            cot = (logit_own, logit_other)[h][0, :, pl.ds(pl.multiple_of(place * 128, 128), 128)]
-            put(h, j, slice(0, n), mm_at(x, cot))
-            part = act[0, :, pl.ds(pl.multiple_of(h * half + place * 256, 256), 256)]
-            value = mm_at(part, grad)
-            for t in range(4):
-                put(h, j, slice(n + t * 256, n + t * 256 + 256), value[:, t * 128 : t * 128 + 128])
-    finish()
-
-
-def feed_back_kernel(
-    s, ending_grad, slope, second, middle, grad_ending, up, u0, u1, u2, u3, down, d0, d1, d2, d3, gain,
-    grad_middle_ref, middle_grad_ref, vec_ref, bias_ref, keep, send, sums,
-):
-    step = pl.program_id(0)
-    put, finish = piece_targets(s, step, pl.num_programs(0) - 1, keep, sums, send)
-    grad = ending_grad[0]
-    x = second[0]
-    half = up.shape[1]
-    n = x.shape[1]
+    half, n = up.shape[1], up.shape[0]
     back = jnp.zeros((PAD, n), F32)
-    for h in range(2):
-        for j in range(4):
-            place = pl.multiple_of((s[1] ^ j) * 256, 256)
-            at = pl.ds(pl.multiple_of(h * half + place, 256), 256)
-            if h == 0:
-                w_up, w_down = up[:, pl.ds(place, 256)], down[pl.ds(place, 256), :]
-            else:
-                w_up, w_down = (u0, u1, u2, u3)[j][...], (d0, d1, d2, d3)[j][...]
-            low = (mm_bt(grad, w_down) * slope[0, :, at]).astype(BF)
-            accumulate(step, bias_ref, (slice(None), at), col_sum(low.astype(F32)))
-            value = mm_at(x, low)
-            for t in range(2):
-                put(h, j, slice(t * n, t * n + n), value[:, t * 128 : t * 128 + 128])
-            back = back + mm_bt(low, w_up)
-    finish()
+    for i in range(8):
+        if i < 4:
+            at = slice(i * 256, i * 256 + 256)
+            w_up, w_down = up[:, at], down[at, :]
+        else:
+            at = pl.ds(pl.multiple_of(half + (s[1] ^ (i - 4)) * 256, 256), 256)
+            w_up, w_down = (u0, u1, u2, u3)[i - 4][...], (d0, d1, d2, d3)[i - 4][...]
+        low = (mm_bt(grad, w_down) * slope[0, :, at]).astype(BF)
+        hidden_grad_ref[0, :, at] = low
+        accumulate(step, bias_ref, (slice(None), at), col_sum(low.astype(F32)))
+        back = back + mm_bt(low, w_up)
     unit, factor = norm_of(middle[0])
     total = grad_ending[0] + norm_back(back, unit, factor, gain[...])
     grad_middle_ref[0] = total
@@ -248,19 +276,15 @@
 
 
 def attend_back_kernel(
-    s, middle_grad, grad_middle, own, other, first, triple, mixed, seg, qkv, qkv_o, out, out_o, gain,
-    frames_own_ref, frames_other_ref, vec_ref, keep, send, sums,
+    s, middle_grad, grad_middle, own, other, triple, seg, qkv, qkv_o, out, out_o, gain,
+    triple_grad_ref, frames_own_ref, frames_other_ref, vec_ref,
 ):
     step = pl.program_id(0)
-    put, finish = piece_targets(s, step, pl.num_programs(0) - 1, keep, sums, send)
     grad = middle_grad[0]
     allowed = allowed_pairs(seg[0])
     factor = HEAD_DIM ** (-0.5)
     back = jnp.zeros(grad.shape, F32)
     for h, (weight, weight_out) in enumerate(((qkv, out), (qkv_o, out_o))):
-        for j in range(4):
-            part = middle_grad[0, :, pl.ds(pl.multiple_of((s[1] ^ j) * 128, 128), 128)]
-            put(h, j, slice(0, 256), mm_at(mixed[0, :, h * 256 : h * 256 + 256], part))
         mixed_grad = mm_bt(grad, weight_out[...]).astype(BF)
         thirds = ([], [], [])
         for pair in range(2):
@@ -280,14 +304,8 @@
             thirds[2].append(mm_at(again.astype(BF), mixed2).astype(BF))
         for c in range(3):
             part = jnp.concatenate(thirds[c], axis=1)
+            triple_grad_ref[0, :, (h * 3 + c) * 256 : (h * 3 + c) * 256 + 256] = part
             back = back + mm_bt(part, weight[c])
-            for j in range(4):
-                x = first[0, :, pl.ds(pl.multiple_of((s[1] ^ j) * 128, 128), 128)]
-                value = mm_at(x, part)
-                for t in range(2):
-                    start = 256 + (t * 3 + c) * 128
-                    put(h, j, slice(start, start + 128), value[:, t * 128 : t * 128 + 128])
-    finish()
     unit, scale = norm_of(whole_row(s[0], own[0], other[0]))
     total = grad_middle[0] + norm_back(back, unit, scale, gain[...])
     low, high = total[:, :256], total[:, 256:]
@@ -295,6 +313,34 @@
     frames_other_ref[0] = jnp.where(s[0] == 0, high, low).astype(BF)
     rows = jnp.concatenate([col_sum(back * unit), col_sum(back)], axis=0)
     accumulate(step, vec_ref, (slice(0, 2), slice(None)), rows)
+
+
+def pieces_call(kernel, scalars, ins, n, scratch, name, flops):
+    def spec(value, width, at):
+        if width is None:
+            return pl.BlockSpec(value.shape, lambda i, s: (0, 0, 0))
+        return pl.BlockSpec((*value.shape[:2], width), lambda i, s: (0, 0, at(i, s)))
+
+    moved = sum(v.size * v.dtype.itemsize for v, _, _ in ins) + 24 * n * 128
+    return pl.pallas_call(
+        kernel,
+        grid_spec=pltpu.PrefetchScalarGridSpec(
+            num_scalar_prefetch=1,
+            grid=(8,),
+            in_specs=[spec(*entry) for entry in ins],
+            out_specs=[
+                pl.BlockSpec((1, n, 128), lambda i, s: ((i // 4) * 2 + jnp.minimum(i % 4, 1), 0, 0)),
+                pl.BlockSpec(
+                    (1, n, 128), lambda i, s: (jnp.maximum((i // 4) * 2 + jnp.maximum(i % 4, 1) - 2, 0), 0, 0)
+                ),
+            ],
+            scratch_shapes=list(scratch),
+        ),
+        out_shape=[jax.ShapeDtypeStruct((4, n, 128), F32), jax.ShapeDtypeStruct((4, n, 128), BF)],
+        compiler_params=pltpu.CompilerParams(vmem_limit_bytes=VMEM),
+        cost_estimate=pl.CostEstimate(flops=flops, bytes_accessed=moved, transcendentals=0),
+        name=name,
+    )(scalars, *[v for v, _, _ in ins])
 
 
 def call(kernel, scalars, ins, outs, scratch=(), name=None, flops=0):
@@ -516,45 +562,68 @@
     )
     logits_got = move.over(logits_send)
 
-    def pieces(n):
-        return [fixed((4, n, 128), F32), fixed((4, n, 128), BF)], [pltpu.VMEM((4, n, 128), F32)]
-
+    turned = pltpu.VMEM((width, blocks * PAD), BF)
     n_late = width + hidden_width
-    outs, scratch = pieces(n_late)
-    keep, send = call(
+    keep, send = pieces_call(
         late_grads_kernel,
         scalars,
-        b(prior_in, logit_own, logit_other, act, ending_grad),
-        outs,
-        scratch,
-        name="late_grads",
-        flops=2 * mine * width * (2 * n_logits + 2 * hidden_width),
+        [
+            (prior_in, None, None),
+            (logit_own, 128, lambda i, s: s[1] ^ jnp.minimum(i, 3)),
+            (logit_other, 128, lambda i, s: s[1] ^ jnp.maximum(i - 4, 0)),
+            (act, 256, lambda i, s: (i // 4) * 4 + (s[1] ^ (i % 4))),
+            (ending_grad, None, None),
+        ],
+        n_late,
+        [turned],
+        "late_grads",
+        2 * mine * width * (2 * n_logits + 2 * hidden_width),
     )
     late = move.gather(move.reduce(keep, send))
-    n_up = width * hidden_width // 512
-    outs, scratch = pieces(n_up)
-    grad_middle, middle_grad, vec_two, up_bias_sum, keep, send = call(
+    hidden_grad, grad_middle, middle_grad, vec_two, up_bias_sum = call(
         feed_back_kernel,
         scalars,
         b(ending_grad, slope, second, middle, grad_ending)
         + w(up_weight, *up_pieces, down_weight, *down_pieces, row(second_gain)),
-        [blocked(width, F32), blocked(width, BF), fixed((3, width), F32), fixed((1, 2 * hidden_width), F32)] + outs,
-        scratch,
+        [blocked(2 * hidden_width, BF), blocked(width, F32), blocked(width, BF)]
+        + [fixed((3, width), F32), fixed((1, 2 * hidden_width), F32)],
         name="feed_back",
-        flops=2 * mine * width * hidden_width * 6,
+        flops=2 * mine * width * hidden_width * 4,
+    )
+    n_up = width * hidden_width // 512
+    keep, send = pieces_call(
+        up_grads_kernel,
+        scalars,
+        [(second, None, None), (hidden_grad, 256, lambda i, s: (i // 4) * 4 + (s[1] ^ (i % 4)))],
+        n_up,
+        [turned],
+        "up_grads",
+        2 * mine * width * hidden_width * 2,
     )
     middle_part = move.gather(move.reduce(keep, send))
+    triple_grad, frames_grad, frames_send, vec_one = call(
+        attend_back_kernel,
+        scalars,
+        b(middle_grad, grad_middle, frames_own, frames_other, triple, seg)
+        + w(qkv_weight, qkv_other, out_weight, out_other, row(first_gain)),
+        [blocked(3 * width, BF), blocked(half, F32), blocked(half, BF), fixed((2, width), F32)],
+        name="attend_back",
+        flops=2 * mine * width * width * 4,
+    )
     n_early = 256 + 768
-    outs, scratch = pieces(n_early)
-    frames_grad, frames_send, vec_one, keep, send = call(
-        attend_back_kernel,
-        scalars,
-        b(middle_grad, grad_middle, frames_own, frames_other, first, triple, mixed, seg)
-        + w(qkv_weight, qkv_other, out_weight, out_other, row(first_gain)),
-        [blocked(half, F32), blocked(half, BF), fixed((2, width), F32)] + outs,
-        scratch,
-        name="attend_back",
-        flops=2 * mine * width * width * 8,
+    keep, send = pieces_call(
+        early_grads_kernel,
+        scalars,
+        [
+            (mixed, 256, lambda i, s: i // 4),
+            (middle_grad, 128, lambda i, s: s[1] ^ (i % 4)),
+            (first, None, None),
+            (triple_grad, 768, lambda i, s: i // 4),
+        ],
+        n_early,
+        [turned, pltpu.VMEM((256, blocks * PAD), BF)],
+        "early_grads",
+        2 * mine * width * width * 4,
     )
     frames_got = move.over(frames_send)
     early = move.gather(move.reduce(keep, send))

time: 327 us -> 277 us (0.85)
  Pallas kernels: 103 us -> 78.9 us
  starting transfers between devices: 70.6 us -> 55.3 us
  waiting for transfers between devices: 98.5 us -> 84.6 us
  local copies, waits for them, and re-layouts: 32 us -> 37.5 us
    pallas_call x6 -> x5, Pallas kernels: 103 us -> 51.8 us  [call(): pl.pallas_call(kernel, grid_spec=pltpu.PrefetchScalarGridSpec(num_scalar_...]
    pallas_call x0 -> x3, Pallas kernels: none -> 27.1 us  [pieces_call(): pl.pallas_call(kernel, grid_spec=pltpu.PrefetchScalarGridSpec(num_scalar_...]
    ppermute x64, starting transfers between devices: 70.6 us -> 55.3 us  [swap(): return lax.ppermute(value, axes, [(i, i ^ mask) for i in range(count)])]
    ppermute x64, waiting for transfers between devices: 98.5 us -> 84.6 us  [swap(): return lax.ppermute(value, axes, [(i, i ^ mask) for i in range(count)])]
    unnamed x141 -> x153, local copies, waits for them, and re-layouts: 9.55 us -> 10.2 us
  transfers between devices with their start and end apart: 64 -> 64, of which waited for: 27 -> 24; matrix products, arithmetic and copies ran while one was open for 11% -> 14% of each run, Pallas kernels for 12% -> 16%
where the time goes in v2:
time: 277 us; the launch traced here: 276 us
  waiting for transfers between devices  84.6 us (31%)
  Pallas kernels  78.9 us (28%)
  starting transfers between devices  55.3 us (20%)
  local copies, waits for them, and re-layouts  37.5 us (14%)
  other arithmetic  17.8 us (6%)
    ppermute x64, waiting for transfers between devices, swap(): return lax.ppermute(value, axes, [(i, i ^ mask) for i in range(count)])  84.6 us
    ppermute x64, starting transfers between devices, swap(): return lax.ppermute(value, axes, [(i, i ^ mask) for i in range(count)])  55.3 us
    pallas_call x5, Pallas kernels, call(): pl.pallas_call(kernel, grid_spec=pltpu.PrefetchScalarGridSpec(num_scalar_...  51.8 us
    pallas_call x3, Pallas kernels, pieces_call(): pl.pallas_call(kernel, grid_spec=pltpu.PrefetchScalarGridSpec(num_scalar_...  27.1 us
    unnamed x153, local copies, waits for them, and re-layouts  10.2 us
    dynamic_slice x5, local copies, waits for them, and re-layouts, part(): return lax.dynamic_slice_in_dim(value, index * size, size, dim)  6.39 us
  transfers between devices with their start and end apart: 64, of which 24 were waited for; matrix products, arithmetic and copies ran while one was open for 14% of the time, Pallas kernels for 16%

profile of v2, /device:TPU:0, one launch (start us, length us, event | category | flops | bytes accessed | tf_op | source)
XLA Modules:
  0.0 276.2 jit_solution(17944757270401558253)
XLA Ops:
  0.7 1.4 pad_maximum_fusion.13
  2.0 3.0 %collective-permute-start.9 = (f32[1536]{0:T(1024)}, f32[1536]{0:T(1024)}, u32[]{:S(2)}, u32[]{:S(2)}) collective-permute-start(f32[1536]{0:T(1024)} %pad_maximum_fusion.13), channel_id=1, source_target_pairs={{0,1},{1,0},{2,3},{3,2},{4,5},{5,4},{6,7},{7,6},{8,9},{9,8},{10,11... | collective-permute-start | bytes 18440 | tf_op jit(solution)/shard_map/ppermute | solution.py:377
  5.0 1.6 constant_dynamic-slice_fusion.7
  6.6 1.7 constant_dynamic-slice_fusion.5
  8.3 2.0 collective-permute-start.10
  10.3 1.7 constant_dynamic-slice_fusion.6
  12.8 2.0 collective-permute-start.1
  15.5 2.2 constant_dynamic-slice_fusion.2
  17.6 2.2 constant_dynamic-slice_fusion
  25.6 7.1 %collective-permute-done.1 = bf16[3,512,128]{2,1,0:T(8,128)(2,1)} collective-permute-done((bf16[3,512,128]{2,1,0:T(8,128)(2,1)}, bf16[3,512,128]{2,1,0:T(8,128)(2,1)}, u32[]{:S(2)}, u32[]{:S(2)}) %collective-permute-start.1) | collective-permute-done | bytes 393248 | tf_op jit(solution)/shard_map/ppermute | solution.py:377
  32.7 1.5 collective-permute-done.15.p0
  34.8 1.5 collective-permute-start.16
  36.9 1.5 collective-permute-start.6
  38.5 2.8 %collective-permute-done.16.p1 = bf16[512,128]{1,0:T(8,128)(2,1)S(1)} collective-permute-done((bf16[512,128]{1,0:T(8,128)(2,1)S(1)}, bf16[512,128]{1,0:T(8,128)(2,1)S(1)}, u32[]{:S(2)}, u32[]{:S(2)}) %collective-permute-start.16) | collective-permute-done | bytes 131104 | tf_op jit(solution)/shard_map/ppermute | solution.py:377
  41.3 1.4 collective-permute-start.19
  42.7 2.0 collective-permute-done.other
  44.7 2.2 collective-permute-done.11.d1
  46.9 3.6 %collective-permute-done.6.u1 = bf16[512,256]{1,0:T(8,128)(2,1)S(1)} collective-permute-done((bf16[512,256]{1,0:T(8,128)(2,1)S(1)}, bf16[512,256]{1,0:T(8,128)(2,1)S(1)}, u32[]{:S(2)}, u32[]{:S(2)}) %collective-permute-start.6) | collective-permute-done | bytes 262176 | tf_op jit(solution)/shard_map/ppermute | solution.py:377
  52.2 1.2 collective-permute-start.20
  53.6 9.4 %attend.1 = (bf16[3,208,512]{2,1,0:T(8,128)(2,1)S(1)}, bf16[3,208,1536]{2,1,0:T(8,128)(2,1)}, bf16[3,208,512]{2,1,0:T(8,128)(2,1)S(1)}, f32[3,208,512]{2,1,0:T(8,128)}, bf16[3,208,512]{2,1,0:T(8,128)(2,1)S(1)}) custom-call(s32[2]{0:T(128)S(1)} %pad_add_fusion.s, bf16[3,208,256]{2,1,0:T(8,128)(2,1)S(1)} %pad.20.own, ...), custom_call_target="tpu_custom_call" | custom-call | flops 1258291200 | bytes 7860672 | tf_op jit(solution)/shard_map/attend/pallas_call | solution.py:357
  64.5 8.6 %feed.1 = (bf16[3,208,2048]{2,1,0:T(8,128)(2,1)}, f32[3,208,2048]{2,1,0:T(8,128)}, f32[3,208,512]{2,1,0:T(8,128)}, bf16[3,208,512]{2,1,0:T(8,128)(2,1)S(1)}, bf1...) custom-call(s32[2]{0:T(128)S(1)} %pad_add_fusion.s, bf16[3,208,512]{2,1,0:T(8,128)(2,1)S(1)} %get-tuple-element.50.second, ...), custom_call_target="tpu_custom_call" | custom-call | flops 2516582400 | bytes 16349184 | tf_op jit(solution)/shard_map/feed/pallas_call | solution.py:357
  73.9 6.6 %prior.2 = (f32[3,208,512]{2,1,0:T(8,128)S(1)}, bf16[3,208,512]{2,1,0:T(8,128)(2,1)S(1)}, f32[3,208,512]{2,1,0:T(8,128)}, bf16[3,208,512]{2,1,0:T(8,128)(2,1)S(1...) custom-call(s32[2]{0:T(128)S(1)} %pad_add_fusion.s, bf16[3,208,512]{2,1,0:T(8,128)(2,1)S(1)} %get-tuple-element.54.prior_in, ...), custom_call_target="tpu_custom_call" | custom-call | flops 1258291200 | bytes 8732672 | tf_op jit(solution)/shard_map/prior/pallas_call | solution.py:357
  80.6 14.1 %feed_back.1 = (bf16[3,208,2048]{2,1,0:T(8,128)(2,1)}, f32[3,208,512]{2,1,0:T(8,128)}, bf16[3,208,512]{2,1,0:T(8,128)(2,1)S(1)}, f32[3,512]{1,0:T(4,128)S(1)}, f32[1,2048]{1,0:T(1,128)S(1)}) custom-call(s32[2]{0:T(128)S(1)} %pad_add_fusion.s, bf16[3,208,512]{2,1,0:T(8,128)(2,1)S(1)} %get-tuple-element.58.ending_grad, ...), custom_call_target="tpu_custom_call" | custom-call | flops 2516582400 | bytes 17629184 | tf_op jit(solution)/shard_map/feed_back/pallas_call | solution.py:357
  94.7 1.5 copy-done.3
  96.3 13.1 %attend_back.1 = (bf16[3,208,1536]{2,1,0:T(8,128)(2,1)}, f32[3,208,256]{2,1,0:T(8,128)S(1)}, bf16[3,208,256]{2,1,0:T(8,128)(2,1)S(1)}, f32[2,512]{1,0:T(2,128)S(1)}) custom-call(s32[2]{0:T(128)S(1)} %pad_add_fusion.s, bf16[3,208,512]{2,1,0:T(8,128)(2,1)S(1)} %get-tuple-element.61.middle_grad, f32[3,208,512]{2,1,0:T(8,128)S(1)} %copy-done.3, ...), custom_call_target="tpu_custom_call" | custom-call | flops 1258291200 | bytes 9454016 | tf_op jit(solution)/shard_map/attend_back/pallas_call | solution.py:357
  112.0 3.0 %collective-permute-done.23 = f32[56,128]{1,0:T(8,128)S(1)} collective-permute-done((f32[56,128]{1,0:T(8,128)S(1)}, f32[56,128]{1,0:T(8,128)S(1)}, u32[]{:S(2)}, u32[]{:S(2)}) %collective-permute-start.23) | collective-permute-done | bytes 28704 | tf_op jit(solution)/shard_map/ppermute | solution.py:377
  116.2 1.6 collective-permute-start.25
  119.0 7.4 %up_grads.1 = (f32[4,1024,128]{2,1,0:T(8,128)S(1)}, bf16[4,1024,128]{2,1,0:T(8,128)(2,1)S(1)}) custom-call(s32[2]{0:T(128)S(1)} %pad_add_fusion.s, bf16[3,208,512]{2,1,0:T(8,128)(2,1)S(1)} %copy-done.8, bf16[3,208,2048]{2,1,0:T(8,128)(2,1)} %get-tuple-element.76.hidden_grad), custom_call_target="tpu_custom_call" | custom-call | flops 1258291200 | bytes 6340608 | tf_op jit(solution)/shard_map/up_grads/pallas_call | solution.py:325
  128.4 1.6 collective-permute-start.26
  131.2 8.3 %early_grads.1 = (f32[4,1024,128]{2,1,0:T(8,128)}, bf16[4,1024,128]{2,1,0:T(8,128)(2,1)S(1)}) custom-call(s32[2]{0:T(128)S(1)} %pad_add_fusion.s, bf16[3,208,512]{2,1,0:T(8,128)(2,1)S(1)} %copy-done.50, bf16[3,208,512]{2,1,0:T(8,128)(2,1)S(1)} %copy-done.10, bf16[3,208,512]{2,1,0:T(8,128)(2,1)S(1)} %copy-done.48, bf16[3,208,1536]{2,1,0:T(8,128)(2,1)S(1)} %copy-done.35), custom_call_target="tpu_custom_call" | custom-call | flops 1258291200 | bytes 6979584 | tf_op jit(solution)/shard_map/early_grads/pallas_call | solution.py:325
  139.5 2.7 collective-permute-start.27
  142.2 11.4 %late_grads.1 = (f32[4,1536,128]{2,1,0:T(8,128)}, bf16[4,1536,128]{2,1,0:T(8,128)(2,1)S(1)}) custom-call(s32[2]{0:T(128)S(1)} %pad_add_fusion.s, bf16[3,208,512]{2,1,0:T(8,128)(2,1)S(1)} %copy-done.14, bf16[3,208,512]{2,1,0:T(8,128)(2,1)S(1)} %pad.22.logit_own, bf16[3,208,512]{2,1,0:T(8,128)(2,1)S(1)} %copy-done.12, ...), custom_call_target="tpu_custom_call" | custom-call | flops 1887436800 | bytes 9830400 | tf_op jit(solution)/shard_map/late_grads/pallas_call | solution.py:325
  158.5 1.7 pad_maximum_fusion
  161.9 1.9 collective-permute-start.31
  165.8 4.7 %collective-permute-done.29 = bf16[1024,128]{1,0:T(8,128)(2,1)S(1)} collective-permute-done((bf16[1024,128]{1,0:T(8,128)(2,1)S(1)}, bf16[1024,128]{1,0:T(8,128)(2,1)S(1)}, u32[]{:S(2)}, u32[]{:S(2)}) %collective-permute-start.29) | collective-permute-done | bytes 262176 | tf_op jit(solution)/shard_map/ppermute | solution.py:377
  171.5 5.1 %collective-permute-done.31 = bf16[1024,128]{1,0:T(8,128)(2,1)S(1)} collective-permute-done((bf16[1024,128]{1,0:T(8,128)(2,1)S(1)}, bf16[1024,128]{1,0:T(8,128)(2,1)S(1)}, u32[]{:S(2)}, u32[]{:S(2)}) %collective-permute-start.31) | collective-permute-done | bytes 262176 | tf_op jit(solution)/shard_map/ppermute | solution.py:377
  178.3 3.5 %collective-permute-done.41 = bf16[1024,128]{1,0:T(8,128)(2,1)S(1)} collective-permute-done((bf16[1024,128]{1,0:T(8,128)(2,1)S(1)}, bf16[1024,128]{1,0:T(8,128)(2,1)S(1)}, u32[]{:S(2)}, u32[]{:S(2)}) %collective-permute-start.41) | collective-permute-done | bytes 262176 | tf_op jit(solution)/shard_map/ppermute | solution.py:377
  182.0 5.2 %collective-permute-done.43 = bf16[1024,128]{1,0:T(8,128)(2,1)S(1)} collective-permute-done((bf16[1024,128]{1,0:T(8,128)(2,1)S(1)}, bf16[1024,128]{1,0:T(8,128)(2,1)S(1)}, u32[]{:S(2)}, u32[]{:S(2)}) %collective-permute-start.43) | collective-permute-done | bytes 262176 | tf_op jit(solution)/shard_map/ppermute | solution.py:377
  187.6 1.6 collective-permute-done.42
  189.9 2.1 collective-permute-start.46
  192.9 5.2 %collective-permute-done.33 = bf16[256,128]{1,0:T(8,128)(2,1)S(1)} collective-permute-done((bf16[256,128]{1,0:T(8,128)(2,1)S(1)}, bf16[256,128]{1,0:T(8,128)(2,1)S(1)}, u32[]{:S(2)}, u32[]{:S(2)}) %collective-permute-start.33) | collective-permute-done | bytes 65568 | tf_op jit(solution)/shard_map/ppermute | solution.py:377
  198.3 4.3 %collective-permute-start.35 = (bf16[256,128]{1,0:T(8,128)(2,1)S(1)}, bf16[256,128]{1,0:T(8,128)(2,1)S(1)}, u32[]{:S(2)}, u32[]{:S(2)}) collective-permute-start(bf16[256,128]{1,0:T(8,128)(2,1)S(1)} %fusion.37), channel_id=1, source_target_pairs={{0,8},{2,10},{4,12},{6,14},{8,0},{10,2},{12,4},{14,6},{16,24},{18,... | collective-permute-start | bytes 196616 | tf_op jit(solution)/shard_map/ppermute | solution.py:377
  202.8 2.2 collective-permute-done.37
  205.0 1.9 collective-permute-done.36
  208.2 2.0 collective-permute-start.55
  212.0 1.6 collective-permute-start.50
  213.5 6.2 %collective-permute-done.53 = bf16[1536,128]{1,0:T(8,128)(2,1)S(1)} collective-permute-done((bf16[1536,128]{1,0:T(8,128)(2,1)S(1)}, bf16[1536,128]{1,0:T(8,128)(2,1)S(1)}, u32[]{:S(2)}, u32[]{:S(2)}) %collective-permute-start.53) | collective-permute-done | bytes 393248 | tf_op jit(solution)/shard_map/ppermute | solution.py:377
  219.8 8.7 %collective-permute-done.55 = bf16[1536,128]{1,0:T(8,128)(2,1)S(1)} collective-permute-done((bf16[1536,128]{1,0:T(8,128)(2,1)S(1)}, bf16[1536,128]{1,0:T(8,128)(2,1)S(1)}, u32[]{:S(2)}, u32[]{:S(2)}) %collective-permute-start.55) | collective-permute-done | bytes 393248 | tf_op jit(solution)/shard_map/ppermute | solution.py:377
  229.7 1.2 collective-permute-start.58
  230.9 1.3 collective-permute-start.57
  233.4 2.8 %collective-permute-done.58 = bf16[384,128]{1,0:T(8,128)(2,1)S(1)} collective-permute-done((bf16[384,128]{1,0:T(8,128)(2,1)S(1)}, bf16[384,128]{1,0:T(8,128)(2,1)S(1)}, u32[]{:S(2)}, u32[]{:S(2)}) %collective-permute-start.58) | collective-permute-done | bytes 98336 | tf_op jit(solution)/shard_map/ppermute | solution.py:377
  236.2 5.1 %collective-permute-done.57 = bf16[384,128]{1,0:T(8,128)(2,1)S(1)} collective-permute-done((bf16[384,128]{1,0:T(8,128)(2,1)S(1)}, bf16[384,128]{1,0:T(8,128)(2,1)S(1)}, u32[]{:S(2)}, u32[]{:S(2)}) %collective-permute-start.57) | collective-permute-done | bytes 98336 | tf_op jit(solution)/shard_map/ppermute | solution.py:377
  241.3 1.7 collective-permute-start.61
  243.0 2.8 collective-permute-start.59
  245.9 2.0 collective-permute-done.61
  247.9 2.0 collective-permute-done.60
  253.0 4.9 %collective-permute-done.62 = bf16[1536,128]{1,0:T(8,128)(2,1)S(1)} collective-permute-done((bf16[1536,128]{1,0:T(8,128)(2,1)S(1)}, bf16[1536,128]{1,0:T(8,128)(2,1)S(1)}, u32[]{:S(2)}, u32[]{:S(2)}) %collective-permute-start.62) | collective-permute-done | bytes 393248 | tf_op jit(solution)/shard_map/ppermute | solution.py:377
  259.9 2.4 reshape.258
  262.3 1.2 copy.50
  263.8 1.3 fusion.20
  265.7 1.5 convert_bitcast_fusion
  267.1 2.9 %reshape.260 = f32[512,1024]{1,0:T(8,128)} reshape(f32[512,4,2,128]{3,2,1,0:T(2,128)S(1)} %convert_bitcast_fusion) | data formatting | bytes 4194304 | tf_op jit(solution)/shard_map/convert_element_type | solution.py:655
  270.1 1.8 copy_bitcast_fusion.3
  274.7 1.5 copy.63
  (328 shorter events, 48.0 us)
Async XLA Ops:
  2.0 22.0 %collective-permute-start.9 = (f32[1536]{0:T(1024)}, f32[1536]{0:T(1024)}, u32[]{:S(2)}, u32[]{:S(2)}) collective-permute-start(f32[1536]{0:T(1024)} %pad_maximum_fusion.13), channel_id=1, source_target_pairs={{0,1},{1,0},{2,3},{3,2},{4,5},{5,4},{6,7},{7,6},{8,9},{9,8},{10,11... | collective-permute-start | bytes 18440 | tf_op jit(solution)/shard_map/ppermute | solution.py:377
  6.6 18.3 %collective-permute-start.3 = (bf16[128,512]{1,0:T(8,128)(2,1)}, bf16[128,512]{1,0:T(8,128)(2,1)S(1)}, u32[]{:S(2)}, u32[]{:S(2)}) collective-permute-start(bf16[128,512]{1,0:T(8,128)(2,1)} %constant_dynamic-slice_fusion.7), channel_id=1, source_target_pairs={{0,1},{1,0},{2,3},{3,2},{4,5},{5,4},{6,7},{7,6},{8,9},{9,8},{10,11... | collective-permute-start | bytes 393224 | tf_op jit(solution)/shard_map/ppermute | solution.py:377
  8.3 28.1 %collective-permute-start.10 = (bf16[256,512]{1,0:T(8,128)(2,1)}, bf16[256,512]{1,0:T(8,128)(2,1)S(1)}, u32[]{:S(2)}, u32[]{:S(2)}) collective-permute-start(bf16[256,512]{1,0:T(8,128)(2,1)} %constant_dynamic-slice_fusion.5), channel_id=1, source_target_pairs={{0,1},{1,0},{2,3},{3,2},{4,5},{5,4},{6,7},{7,6},{8,9},{9,8},{10,11... | collective-permute-start | bytes 786440 | tf_op jit(solution)/shard_map/ppermute | solution.py:377
  11.9 24.9 %collective-permute-start.5 = (bf16[512,256]{1,0:T(8,128)(2,1)}, bf16[512,256]{1,0:T(8,128)(2,1)S(1)}, u32[]{:S(2)}, u32[]{:S(2)}) collective-permute-start(bf16[512,256]{1,0:T(8,128)(2,1)} %constant_dynamic-slice_fusion.6), channel_id=1, source_target_pairs={{0,1},{1,0},{2,3},{3,2},{4,5},{5,4},{6,7},{7,6},{8,9},{9,8},{10,11... | collective-permute-start | bytes 786440 | tf_op jit(solution)/shard_map/ppermute | solution.py:377
  12.8 19.9 %collective-permute-start.1 = (bf16[3,512,128]{2,1,0:T(8,128)(2,1)}, bf16[3,512,128]{2,1,0:T(8,128)(2,1)}, u32[]{:S(2)}, u32[]{:S(2)}) collective-permute-start(bf16[3,512,128]{2,1,0:T(8,128)(2,1)} %constant_dynamic-slice_fusion.8), channel_id=1, source_target_pairs={{0,1},{1,0},{2,3},{3,2},{4,5},{5,4},{6,7},{7,6},{8,9},{9,8},{10,11... | collective-permute-start | bytes 1179656 | tf_op jit(solution)/shard_map/ppermute | solution.py:377
  24.1 10.1 %collective-permute-start.15 = (bf16[512,128]{1,0:T(8,128)(2,1)S(1)}, bf16[512,128]{1,0:T(8,128)(2,1)S(1)}, u32[]{:S(2)}, u32[]{:S(2)}) collective-permute-start(bf16[512,128]{1,0:T(8,128)(2,1)S(1)} %copy-done.70), channel_id=1, source_target_pairs={{0,1},{1,0},{2,3},{3,2},{4,5},{5,4},{6,7},{7,6},{8,9},{9,8},{10,11... | collective-permute-start | bytes 393224 | tf_op jit(solution)/shard_map/ppermute | solution.py:377
  24.9 10.0 %collective-permute-start.4 = (bf16[128,512]{1,0:T(8,128)(2,1)S(1)}, bf16[128,512]{1,0:T(8,128)(2,1)S(1)}, u32[]{:S(2)}, u32[]{:S(2)}) collective-permute-start(bf16[128,512]{1,0:T(8,128)(2,1)S(1)} %collective-permute-done.3), channel_id=1, source_target_pairs={{0,2},{2,0},{4,6},{6,4},{8,10},{10,8},{12,14},{14,12},{16,18},{18,... | collective-permute-start | bytes 393224 | tf_op jit(solution)/shard_map/ppermute | solution.py:377
  32.7 17.8 %collective-permute-start.2 = (bf16[3,512,128]{2,1,0:T(8,128)(2,1)}, bf16[3,512,128]{2,1,0:T(8,128)(2,1)S(1)}, u32[]{:S(2)}, u32[]{:S(2)}) collective-permute-start(bf16[3,512,128]{2,1,0:T(8,128)(2,1)} %collective-permute-done.1), channel_id=1, source_target_pairs={{0,2},{2,0},{4,6},{6,4},{8,10},{10,8},{12,14},{14,12},{16,18},{18,... | collective-permute-start | bytes 1179656 | tf_op jit(solution)/shard_map/ppermute | solution.py:377
  34.2 10.5 %collective-permute-start = (bf16[3,208,256]{2,1,0:T(8,128)(2,1)S(1)}, bf16[3,208,256]{2,1,0:T(8,128)(2,1)S(1)}, u32[]{:S(2)}, u32[]{:S(2)}) collective-permute-start(bf16[3,208,256]{2,1,0:T(8,128)(2,1)S(1)} %pad.21), channel_id=1, source_target_pairs={{0,1},{1,0},{2,3},{3,2},{4,5},{5,4},{6,7},{7,6},{8,9},{9,8},{10,11... | collective-permute-start | bytes 958472 | tf_op jit(solution)/shard_map/ppermute | solution.py:377
  34.8 6.4 %collective-permute-start.16 = (bf16[512,128]{1,0:T(8,128)(2,1)S(1)}, bf16[512,128]{1,0:T(8,128)(2,1)S(1)}, u32[]{:S(2)}, u32[]{:S(2)}) collective-permute-start(bf16[512,128]{1,0:T(8,128)(2,1)S(1)} %collective-permute-done.15.p0), channel_id=1, source_target_pairs={{0,4},{2,6},{4,0},{6,2},{8,12},{10,14},{12,8},{14,10},{16,20},{18,... | collective-permute-start | bytes 393224 | tf_op jit(solution)/shard_map/ppermute | solution.py:377
  36.3 10.6 %collective-permute-start.11 = (bf16[256,512]{1,0:T(8,128)(2,1)S(1)}, bf16[256,512]{1,0:T(8,128)(2,1)S(1)}, u32[]{:S(2)}, u32[]{:S(2)}) collective-permute-start(bf16[256,512]{1,0:T(8,128)(2,1)S(1)} %collective-permute-done.10.d0), channel_id=1, source_target_pairs={{0,4},{2,6},{4,0},{6,2},{8,12},{10,14},{12,8},{14,10},{16,20},{18,... | collective-permute-start | bytes 786440 | tf_op jit(solution)/shard_map/ppermute | solution.py:377
  36.9 13.6 %collective-permute-start.6 = (bf16[512,256]{1,0:T(8,128)(2,1)S(1)}, bf16[512,256]{1,0:T(8,128)(2,1)S(1)}, u32[]{:S(2)}, u32[]{:S(2)}) collective-permute-start(bf16[512,256]{1,0:T(8,128)(2,1)S(1)} %collective-permute-done.5.u0), channel_id=1, source_target_pairs={{0,4},{2,6},{4,0},{6,2},{8,12},{10,14},{12,8},{14,10},{16,20},{18,... | collective-permute-start | bytes 786440 | tf_op jit(solution)/shard_map/ppermute | solution.py:377
  41.3 32.6 %collective-permute-start.19 = (bf16[3,208,512]{2,1,0:T(8,128)(2,1)S(1)}, bf16[3,208,512]{2,1,0:T(8,128)(2,1)S(1)}, u32[]{:S(2)}, u32[]{:S(2)}) collective-permute-start(bf16[3,208,512]{2,1,0:T(8,128)(2,1)S(1)} %pad.23), channel_id=1, source_target_pairs={{0,1},{1,0},{2,3},{3,2},{4,5},{5,4},{6,7},{7,6},{8,9},{9,8},{10,11... | collective-permute-start | bytes 1916936 | tf_op jit(solution)/shard_map/ppermute | solution.py:377
  44.7 7.5 %collective-permute-start.12 = (bf16[256,512]{1,0:T(8,128)(2,1)S(1)}, bf16[256,512]{1,0:T(8,128)(2,1)S(1)}, u32[]{:S(2)}, u32[]{:S(2)}) collective-permute-start(bf16[256,512]{1,0:T(8,128)(2,1)S(1)} %collective-permute-done.10.d0), channel_id=1, source_target_pairs={{0,2},{2,0},{4,6},{6,4},{8,10},{10,8},{12,14},{14,12},{16,18},{18,... | collective-permute-start | bytes 786440 | tf_op jit(solution)/shard_map/ppermute | solution.py:377
  46.9 17.0 %collective-permute-start.7 = (bf16[512,256]{1,0:T(8,128)(2,1)S(1)}, bf16[512,256]{1,0:T(8,128)(2,1)S(1)}, u32[]{:S(2)}, u32[]{:S(2)}) collective-permute-start(bf16[512,256]{1,0:T(8,128)(2,1)S(1)} %collective-permute-done.5.u0), channel_id=1, source_target_pairs={{0,2},{2,0},{4,6},{6,4},{8,10},{10,8},{12,14},{14,12},{16,18},{18,... | collective-permute-start | bytes 786440 | tf_op jit(solution)/shard_map/ppermute | solution.py:377
  50.5 13.4 %collective-permute-start.13 = (bf16[256,512]{1,0:T(8,128)(2,1)S(1)}, bf16[256,512]{1,0:T(8,128)(2,1)S(1)}, u32[]{:S(2)}, u32[]{:S(2)}) collective-permute-start(bf16[256,512]{1,0:T(8,128)(2,1)S(1)} %collective-permute-done.11.d1), channel_id=1, source_target_pairs={{0,2},{2,0},{4,6},{6,4},{8,10},{10,8},{12,14},{14,12},{16,18},{18,... | collective-permute-start | bytes 786440 | tf_op jit(solution)/shard_map/ppermute | solution.py:377
  50.5 13.9 %collective-permute-start.8 = (bf16[512,256]{1,0:T(8,128)(2,1)S(1)}, bf16[512,256]{1,0:T(8,128)(2,1)S(1)}, u32[]{:S(2)}, u32[]{:S(2)}) collective-permute-start(bf16[512,256]{1,0:T(8,128)(2,1)S(1)} %collective-permute-done.6.u1), channel_id=1, source_target_pairs={{0,2},{2,0},{4,6},{6,4},{8,10},{10,8},{12,14},{14,12},{16,18},{18,... | collective-permute-start | bytes 786440 | tf_op jit(solution)/shard_map/ppermute | solution.py:377
  52.2 21.6 %collective-permute-start.20 = (bf16[3,208,256]{2,1,0:T(8,128)(2,1)S(1)}, bf16[3,208,256]{2,1,0:T(8,128)(2,1)S(1)}, u32[]{:S(2)}, u32[]{:S(2)}) collective-permute-start(bf16[3,208,256]{2,1,0:T(8,128)(2,1)S(1)} %pad.25), channel_id=1, source_target_pairs={{0,1},{1,0},{2,3},{3,2},{4,5},{5,4},{6,7},{7,6},{8,9},{9,8},{10,11... | collective-permute-start | bytes 958472 | tf_op jit(solution)/shard_map/ppermute | solution.py:377
  63.9 9.9 %collective-permute-start.17 = (bf16[512,128]{1,0:T(8,128)(2,1)S(1)}, bf16[512,128]{1,0:T(8,128)(2,1)S(1)}, u32[]{:S(2)}, u32[]{:S(2)}) collective-permute-start(bf16[512,128]{1,0:T(8,128)(2,1)S(1)} %collective-permute-done.15.p0), channel_id=1, source_target_pairs={{0,2},{2,0},{4,6},{6,4},{8,10},{10,8},{12,14},{14,12},{16,18},{18,... | collective-permute-start | bytes 393224 | tf_op jit(solution)/shard_map/ppermute | solution.py:377
  64.0 9.9 %collective-permute-start.18 = (bf16[512,128]{1,0:T(8,128)(2,1)S(1)}, bf16[512,128]{1,0:T(8,128)(2,1)S(1)}, u32[]{:S(2)}, u32[]{:S(2)}) collective-permute-start(bf16[512,128]{1,0:T(8,128)(2,1)S(1)} %collective-permute-done.16.p1), channel_id=1, source_target_pairs={{0,2},{2,0},{4,6},{6,4},{8,10},{10,8},{12,14},{14,12},{16,18},{18,... | collective-permute-start | bytes 393224 | tf_op jit(solution)/shard_map/ppermute | solution.py:377
  111.1 3.9 %collective-permute-start.23 = (f32[56,128]{1,0:T(8,128)S(1)}, f32[56,128]{1,0:T(8,128)S(1)}, u32[]{:S(2)}, u32[]{:S(2)}) collective-permute-start(f32[56,128]{1,0:T(8,128)S(1)} %bitcast.309), channel_id=1, source_target_pairs={{0,1},{1,0},{2,3},{3,2},{4,5},{5,4},{6,7},{7,6},{8,9},{9,8},{10,11... | collective-permute-start | bytes 86024 | tf_op jit(solution)/shard_map/ppermute | solution.py:377
  115.0 1.2 collective-permute-start.24
  115.1 41.0 %collective-permute-start.14 = (bf16[3,208,256]{2,1,0:T(8,128)(2,1)S(1)}, bf16[3,208,256]{2,1,0:T(8,128)(2,1)S(1)}, u32[]{:S(2)}, u32[]{:S(2)}) collective-permute-start(bf16[3,208,256]{2,1,0:T(8,128)(2,1)S(1)} %copy-done.39), channel_id=1, source_target_pairs={{0,1},{1,0},{2,3},{3,2},{4,5},{5,4},{6,7},{7,6},{8,9},{9,8},{10,11... | collective-permute-start | bytes 958472 | tf_op jit(solution)/shard_map/ppermute | solution.py:377
  116.2 12.2 %collective-permute-start.25 = (f32[56,128]{1,0:T(8,128)S(1)}, f32[56,128]{1,0:T(8,128)S(1)}, u32[]{:S(2)}, u32[]{:S(2)}) collective-permute-start(f32[56,128]{1,0:T(8,128)S(1)} %fusion.59), channel_id=1, source_target_pairs={{0,4},{2,6},{4,0},{6,2},{8,12},{10,14},{12,8},{14,10},{16,20},{18,... | collective-permute-start | bytes 86024 | tf_op jit(solution)/shard_map/ppermute | solution.py:377
  126.3 29.4 %collective-permute-start.22 = (bf16[3,208,256]{2,1,0:T(8,128)(2,1)S(1)}, bf16[3,208,256]{2,1,0:T(8,128)(2,1)S(1)}, u32[]{:S(2)}, u32[]{:S(2)}) collective-permute-start(bf16[3,208,256]{2,1,0:T(8,128)(2,1)S(1)} %copy-done.41), channel_id=1, source_target_pairs={{0,1},{1,0},{2,3},{3,2},{4,5},{5,4},{6,7},{7,6},{8,9},{9,8},{10,11... | collective-permute-start | bytes 958472 | tf_op jit(solution)/shard_map/ppermute | solution.py:377
  127.4 30.8 %collective-permute-start.21 = (bf16[3,208,512]{2,1,0:T(8,128)(2,1)S(1)}, bf16[3,208,512]{2,1,0:T(8,128)(2,1)S(1)}, u32[]{:S(2)}, u32[]{:S(2)}) collective-permute-start(bf16[3,208,512]{2,1,0:T(8,128)(2,1)S(1)} %copy-done.37), channel_id=1, source_target_pairs={{0,1},{1,0},{2,3},{3,2},{4,5},{5,4},{6,7},{7,6},{8,9},{9,8},{10,11... | collective-permute-start | bytes 1916936 | tf_op jit(solution)/shard_map/ppermute | solution.py:377
  128.4 11.1 %collective-permute-start.26 = (f32[56,128]{1,0:T(8,128)S(1)}, f32[56,128]{1,0:T(8,128)S(1)}, u32[]{:S(2)}, u32[]{:S(2)}) collective-permute-start(f32[56,128]{1,0:T(8,128)S(1)} %add.180), channel_id=1, source_target_pairs={{0,8},{2,10},{4,12},{6,14},{8,0},{10,2},{12,4},{14,6},{16,24},{18,... | collective-permute-start | bytes 86024 | tf_op jit(solution)/shard_map/ppermute | solution.py:377
  139.5 20.7 %collective-permute-start.28 = (bf16[4,1024,128]{2,1,0:T(8,128)(2,1)S(1)}, bf16[4,1024,128]{2,1,0:T(8,128)(2,1)S(1)}, u32[]{:S(2)}, u32[]{:S(2)}) collective-permute-start(bf16[4,1024,128]{2,1,0:T(8,128)(2,1)S(1)} %get-tuple-element.75), channel_id=1, source_target_pairs={{0,2},{2,0},{4,6},{6,4},{8,10},{10,8},{12,14},{14,12},{16,18},{18,... | collective-permute-start | bytes 3145736 | tf_op jit(solution)/shard_map/ppermute | solution.py:377
  139.5 14.1 %collective-permute-start.27 = (f32[56,128]{1,0:T(8,128)S(1)}, f32[56,128]{1,0:T(8,128)S(1)}, u32[]{:S(2)}, u32[]{:S(2)}) collective-permute-start(f32[56,128]{1,0:T(8,128)S(1)} %add.181), channel_id=1, source_target_pairs={{0,16},{2,18},{4,20},{6,22},{8,24},{10,26},{12,28},{14,30},{16,0},... | collective-permute-start | bytes 86024 | tf_op jit(solution)/shard_map/ppermute | solution.py:377
  153.6 11.3 %collective-permute-start.40 = (bf16[4,1024,128]{2,1,0:T(8,128)(2,1)S(1)}, bf16[4,1024,128]{2,1,0:T(8,128)(2,1)S(1)}, u32[]{:S(2)}, u32[]{:S(2)}) collective-permute-start(bf16[4,1024,128]{2,1,0:T(8,128)(2,1)S(1)} %get-tuple-element.78), channel_id=1, source_target_pairs={{0,2},{2,0},{4,6},{6,4},{8,10},{10,8},{12,14},{14,12},{16,18},{18,... | collective-permute-start | bytes 3145736 | tf_op jit(solution)/shard_map/ppermute | solution.py:377
  155.7 51.4 %collective-permute-start.52 = (bf16[4,1536,128]{2,1,0:T(8,128)(2,1)S(1)}, bf16[4,1536,128]{2,1,0:T(8,128)(2,1)S(1)}, u32[]{:S(2)}, u32[]{:S(2)}) collective-permute-start(bf16[4,1536,128]{2,1,0:T(8,128)(2,1)S(1)} %get-tuple-element.81), channel_id=1, source_target_pairs={{0,2},{2,0},{4,6},{6,4},{8,10},{10,8},{12,14},{14,12},{16,18},{18,... | collective-permute-start | bytes 4718600 | tf_op jit(solution)/shard_map/ppermute | solution.py:377
  161.3 9.2 %collective-permute-start.29 = (bf16[1024,128]{1,0:T(8,128)(2,1)S(1)}, bf16[1024,128]{1,0:T(8,128)(2,1)S(1)}, u32[]{:S(2)}, u32[]{:S(2)}) collective-permute-start(bf16[1024,128]{1,0:T(8,128)(2,1)S(1)} %get-tuple-element.110), channel_id=1, source_target_pairs={{0,4},{2,6},{4,0},{6,2},{8,12},{10,14},{12,8},{14,10},{16,20},{18,... | collective-permute-start | bytes 786440 | tf_op jit(solution)/shard_map/ppermute | solution.py:377
  161.9 14.7 %collective-permute-start.31 = (bf16[1024,128]{1,0:T(8,128)(2,1)S(1)}, bf16[1024,128]{1,0:T(8,128)(2,1)S(1)}, u32[]{:S(2)}, u32[]{:S(2)}) collective-permute-start(bf16[1024,128]{1,0:T(8,128)(2,1)S(1)} %get-tuple-element.111), channel_id=1, source_target_pairs={{0,5},{1,4},{2,7},{3,6},{4,1},{5,0},{6,3},{7,2},{8,13},{9,12},{10,... | collective-permute-start | bytes 786440 | tf_op jit(solution)/shard_map/ppermute | solution.py:377
  163.9 13.8 %collective-permute-start.30 = (bf16[1024,128]{1,0:T(8,128)(2,1)S(1)}, bf16[1024,128]{1,0:T(8,128)(2,1)S(1)}, u32[]{:S(2)}, u32[]{:S(2)}) collective-permute-start(bf16[1024,128]{1,0:T(8,128)(2,1)S(1)} %get-tuple-element.112), channel_id=1, source_target_pairs={{0,1},{1,0},{2,3},{3,2},{4,5},{5,4},{6,7},{7,6},{8,9},{9,8},{10,11... | collective-permute-start | bytes 786440 | tf_op jit(solution)/shard_map/ppermute | solution.py:377
  165.2 16.6 %collective-permute-start.41 = (bf16[1024,128]{1,0:T(8,128)(2,1)S(1)}, bf16[1024,128]{1,0:T(8,128)(2,1)S(1)}, u32[]{:S(2)}, u32[]{:S(2)}) collective-permute-start(bf16[1024,128]{1,0:T(8,128)(2,1)S(1)} %get-tuple-element.103), channel_id=1, source_target_pairs={{0,4},{2,6},{4,0},{6,2},{8,12},{10,14},{12,8},{14,10},{16,20},{18,... | collective-permute-start | bytes 786440 | tf_op jit(solution)/shard_map/ppermute | solution.py:377
  170.5 16.8 %collective-permute-start.43 = (bf16[1024,128]{1,0:T(8,128)(2,1)S(1)}, bf16[1024,128]{1,0:T(8,128)(2,1)S(1)}, u32[]{:S(2)}, u32[]{:S(2)}) collective-permute-start(bf16[1024,128]{1,0:T(8,128)(2,1)S(1)} %get-tuple-element.104), channel_id=1, source_target_pairs={{0,5},{1,4},{2,7},{3,6},{4,1},{5,0},{6,3},{7,2},{8,13},{9,12},{10,... | collective-permute-start | bytes 786440 | tf_op jit(solution)/shard_map/ppermute | solution.py:377
  176.6 12.5 %collective-permute-start.42 = (bf16[1024,128]{1,0:T(8,128)(2,1)S(1)}, bf16[1024,128]{1,0:T(8,128)(2,1)S(1)}, u32[]{:S(2)}, u32[]{:S(2)}) collective-permute-start(bf16[1024,128]{1,0:T(8,128)(2,1)S(1)} %get-tuple-element.105), channel_id=1, source_target_pairs={{0,1},{1,0},{2,3},{3,2},{4,5},{5,4},{6,7},{7,6},{8,9},{9,8},{10,11... | collective-permute-start | bytes 786440 | tf_op jit(solution)/shard_map/ppermute | solution.py:377
  177.8 12.0 %collective-permute-start.32 = (bf16[256,128]{1,0:T(8,128)(2,1)S(1)}, bf16[256,128]{1,0:T(8,128)(2,1)S(1)}, u32[]{:S(2)}, u32[]{:S(2)}) collective-permute-start(bf16[256,128]{1,0:T(8,128)(2,1)S(1)} %get-tuple-element.129), channel_id=1, source_target_pairs={{0,8},{2,10},{4,12},{6,14},{8,0},{10,2},{12,4},{14,6},{16,24},{18,... | collective-permute-start | bytes 196616 | tf_op jit(solution)/shard_map/ppermute | solution.py:377
  181.8 10.1 %collective-permute-start.34 = (bf16[256,128]{1,0:T(8,128)(2,1)S(1)}, bf16[256,128]{1,0:T(8,128)(2,1)S(1)}, u32[]{:S(2)}, u32[]{:S(2)}) collective-permute-start(bf16[256,128]{1,0:T(8,128)(2,1)S(1)} %get-tuple-element.130), channel_id=1, source_target_pairs={{0,24},{2,26},{4,28},{6,30},{8,16},{10,18},{12,20},{14,22},{16,8},... | collective-permute-start | bytes 196616 | tf_op jit(solution)/shard_map/ppermute | solution.py:377
  187.3 10.8 %collective-permute-start.33 = (bf16[256,128]{1,0:T(8,128)(2,1)S(1)}, bf16[256,128]{1,0:T(8,128)(2,1)S(1)}, u32[]{:S(2)}, u32[]{:S(2)}) collective-permute-start(bf16[256,128]{1,0:T(8,128)(2,1)S(1)} %get-tuple-element.131), channel_id=1, source_target_pairs={{0,16},{2,18},{4,20},{6,22},{8,24},{10,26},{12,28},{14,30},{16,0},... | collective-permute-start | bytes 196616 | tf_op jit(solution)/shard_map/ppermute | solution.py:377
  189.4 8.8 %collective-permute-start.44 = (bf16[256,128]{1,0:T(8,128)(2,1)S(1)}, bf16[256,128]{1,0:T(8,128)(2,1)S(1)}, u32[]{:S(2)}, u32[]{:S(2)}) collective-permute-start(bf16[256,128]{1,0:T(8,128)(2,1)S(1)} %get-tuple-element.126), channel_id=1, source_target_pairs={{0,8},{2,10},{4,12},{6,14},{8,0},{10,2},{12,4},{14,6},{16,24},{18,... | collective-permute-start | bytes 196616 | tf_op jit(solution)/shard_map/ppermute | solution.py:377
  189.9 8.4 %collective-permute-start.46 = (bf16[256,128]{1,0:T(8,128)(2,1)S(1)}, bf16[256,128]{1,0:T(8,128)(2,1)S(1)}, u32[]{:S(2)}, u32[]{:S(2)}) collective-permute-start(bf16[256,128]{1,0:T(8,128)(2,1)S(1)} %get-tuple-element.127), channel_id=1, source_target_pairs={{0,24},{2,26},{4,28},{6,30},{8,16},{10,18},{12,20},{14,22},{16,8},... | collective-permute-start | bytes 196616 | tf_op jit(solution)/shard_map/ppermute | solution.py:377
  191.9 10.7 %collective-permute-start.45 = (bf16[256,128]{1,0:T(8,128)(2,1)S(1)}, bf16[256,128]{1,0:T(8,128)(2,1)S(1)}, u32[]{:S(2)}, u32[]{:S(2)}) collective-permute-start(bf16[256,128]{1,0:T(8,128)(2,1)S(1)} %get-tuple-element.128), channel_id=1, source_target_pairs={{0,16},{2,18},{4,20},{6,22},{8,24},{10,26},{12,28},{14,30},{16,0},... | collective-permute-start | bytes 196616 | tf_op jit(solution)/shard_map/ppermute | solution.py:377
  198.1 6.8 %collective-permute-start.37 = (bf16[256,128]{1,0:T(8,128)(2,1)S(1)}, bf16[256,128]{1,0:T(8,128)(2,1)S(1)}, u32[]{:S(2)}, u32[]{:S(2)}) collective-permute-start(bf16[256,128]{1,0:T(8,128)(2,1)S(1)} %fusion.37), channel_id=1, source_target_pairs={{0,24},{2,26},{4,28},{6,30},{8,16},{10,18},{12,20},{14,22},{16,8},... | collective-permute-start | bytes 196616 | tf_op jit(solution)/shard_map/ppermute | solution.py:377
  198.2 8.7 %collective-permute-start.36 = (bf16[256,128]{1,0:T(8,128)(2,1)S(1)}, bf16[256,128]{1,0:T(8,128)(2,1)S(1)}, u32[]{:S(2)}, u32[]{:S(2)}) collective-permute-start(bf16[256,128]{1,0:T(8,128)(2,1)S(1)} %fusion.37), channel_id=1, source_target_pairs={{0,16},{2,18},{4,20},{6,22},{8,24},{10,26},{12,28},{14,30},{16,0},... | collective-permute-start | bytes 196616 | tf_op jit(solution)/shard_map/ppermute | solution.py:377
  198.3 8.8 %collective-permute-start.35 = (bf16[256,128]{1,0:T(8,128)(2,1)S(1)}, bf16[256,128]{1,0:T(8,128)(2,1)S(1)}, u32[]{:S(2)}, u32[]{:S(2)}) collective-permute-start(bf16[256,128]{1,0:T(8,128)(2,1)S(1)} %fusion.37), channel_id=1, source_target_pairs={{0,8},{2,10},{4,12},{6,14},{8,0},{10,2},{12,4},{14,6},{16,24},{18,... | collective-permute-start | bytes 196616 | tf_op jit(solution)/shard_map/ppermute | solution.py:377
  202.6 7.6 %collective-permute-start.49 = (bf16[256,128]{1,0:T(8,128)(2,1)S(1)}, bf16[256,128]{1,0:T(8,128)(2,1)S(1)}, u32[]{:S(2)}, u32[]{:S(2)}) collective-permute-start(bf16[256,128]{1,0:T(8,128)(2,1)S(1)} %fusion.34), channel_id=1, source_target_pairs={{0,24},{2,26},{4,28},{6,30},{8,16},{10,18},{12,20},{14,22},{16,8},... | collective-permute-start | bytes 196616 | tf_op jit(solution)/shard_map/ppermute | solution.py:377
  205.0 6.3 %collective-permute-start.48 = (bf16[256,128]{1,0:T(8,128)(2,1)S(1)}, bf16[256,128]{1,0:T(8,128)(2,1)S(1)}, u32[]{:S(2)}, u32[]{:S(2)}) collective-permute-start(bf16[256,128]{1,0:T(8,128)(2,1)S(1)} %fusion.34), channel_id=1, source_target_pairs={{0,16},{2,18},{4,20},{6,22},{8,24},{10,26},{12,28},{14,30},{16,0},... | collective-permute-start | bytes 196616 | tf_op jit(solution)/shard_map/ppermute | solution.py:377
  206.9 5.0 %collective-permute-start.47 = (bf16[256,128]{1,0:T(8,128)(2,1)S(1)}, bf16[256,128]{1,0:T(8,128)(2,1)S(1)}, u32[]{:S(2)}, u32[]{:S(2)}) collective-permute-start(bf16[256,128]{1,0:T(8,128)(2,1)S(1)} %fusion.34), channel_id=1, source_target_pairs={{0,8},{2,10},{4,12},{6,14},{8,0},{10,2},{12,4},{14,6},{16,24},{18,... | collective-permute-start | bytes 196616 | tf_op jit(solution)/shard_map/ppermute | solution.py:377
  207.7 12.1 %collective-permute-start.53 = (bf16[1536,128]{1,0:T(8,128)(2,1)S(1)}, bf16[1536,128]{1,0:T(8,128)(2,1)S(1)}, u32[]{:S(2)}, u32[]{:S(2)}) collective-permute-start(bf16[1536,128]{1,0:T(8,128)(2,1)S(1)} %get-tuple-element.94), channel_id=1, source_target_pairs={{0,4},{2,6},{4,0},{6,2},{8,12},{10,14},{12,8},{14,10},{16,20},{18,... | collective-permute-start | bytes 1179656 | tf_op jit(solution)/shard_map/ppermute | solution.py:377
  208.2 20.2 %collective-permute-start.55 = (bf16[1536,128]{1,0:T(8,128)(2,1)S(1)}, bf16[1536,128]{1,0:T(8,128)(2,1)S(1)}, u32[]{:S(2)}, u32[]{:S(2)}) collective-permute-start(bf16[1536,128]{1,0:T(8,128)(2,1)S(1)} %get-tuple-element.95), channel_id=1, source_target_pairs={{0,5},{1,4},{2,7},{3,6},{4,1},{5,0},{6,3},{7,2},{8,13},{9,12},{10,... | collective-permute-start | bytes 1179656 | tf_op jit(solution)/shard_map/ppermute | solution.py:377
  210.2 18.3 %collective-permute-start.54 = (bf16[1536,128]{1,0:T(8,128)(2,1)S(1)}, bf16[1536,128]{1,0:T(8,128)(2,1)S(1)}, u32[]{:S(2)}, u32[]{:S(2)}) collective-permute-start(bf16[1536,128]{1,0:T(8,128)(2,1)S(1)} %get-tuple-element.96), channel_id=1, source_target_pairs={{0,1},{1,0},{2,3},{3,2},{4,5},{5,4},{6,7},{7,6},{8,9},{9,8},{10,11... | collective-permute-start | bytes 1179656 | tf_op jit(solution)/shard_map/ppermute | solution.py:377
  211.3 21.0 %collective-permute-start.38 = (bf16[1024,128]{1,0:T(8,128)(2,1)S(1)}, bf16[1024,128]{1,0:T(8,128)(2,1)S(1)}, u32[]{:S(2)}, u32[]{:S(2)}) collective-permute-start(bf16[1024,128]{1,0:T(8,128)(2,1)S(1)} %get-tuple-element.145), channel_id=1, source_target_pairs={{0,4},{2,6},{4,0},{6,2},{8,12},{10,14},{12,8},{14,10},{16,20},{18,... | collective-permute-start | bytes 786440 | tf_op jit(solution)/shard_map/ppermute | solution.py:377
  212.0 33.8 %collective-permute-start.50 = (bf16[1024,128]{1,0:T(8,128)(2,1)S(1)}, bf16[1024,128]{1,0:T(8,128)(2,1)S(1)}, u32[]{:S(2)}, u32[]{:S(2)}) collective-permute-start(bf16[1024,128]{1,0:T(8,128)(2,1)S(1)} %get-tuple-element.139), channel_id=1, source_target_pairs={{0,4},{2,6},{4,0},{6,2},{8,12},{10,14},{12,8},{14,10},{16,20},{18,... | collective-permute-start | bytes 786440 | tf_op jit(solution)/shard_map/ppermute | solution.py:377
  228.7 4.7 %collective-permute-start.56 = (bf16[384,128]{1,0:T(8,128)(2,1)S(1)}, bf16[384,128]{1,0:T(8,128)(2,1)S(1)}, u32[]{:S(2)}, u32[]{:S(2)}) collective-permute-start(bf16[384,128]{1,0:T(8,128)(2,1)S(1)} %get-tuple-element.115), channel_id=1, source_target_pairs={{0,8},{2,10},{4,12},{6,14},{8,0},{10,2},{12,4},{14,6},{16,24},{18,... | collective-permute-start | bytes 294920 | tf_op jit(solution)/shard_map/ppermute | solution.py:377
  229.7 6.5 %collective-permute-start.58 = (bf16[384,128]{1,0:T(8,128)(2,1)S(1)}, bf16[384,128]{1,0:T(8,128)(2,1)S(1)}, u32[]{:S(2)}, u32[]{:S(2)}) collective-permute-start(bf16[384,128]{1,0:T(8,128)(2,1)S(1)} %get-tuple-element.116), channel_id=1, source_target_pairs={{0,24},{2,26},{4,28},{6,30},{8,16},{10,18},{12,20},{14,22},{16,8},... | collective-permute-start | bytes 294920 | tf_op jit(solution)/shard_map/ppermute | solution.py:377
  230.9 10.3 %collective-permute-start.57 = (bf16[384,128]{1,0:T(8,128)(2,1)S(1)}, bf16[384,128]{1,0:T(8,128)(2,1)S(1)}, u32[]{:S(2)}, u32[]{:S(2)}) collective-permute-start(bf16[384,128]{1,0:T(8,128)(2,1)S(1)} %get-tuple-element.117), channel_id=1, source_target_pairs={{0,16},{2,18},{4,20},{6,22},{8,24},{10,26},{12,28},{14,30},{16,0},... | collective-permute-start | bytes 294920 | tf_op jit(solution)/shard_map/ppermute | solution.py:377
  232.3 18.3 %collective-permute-start.39 = (bf16[2,1024,128]{2,1,0:T(8,128)(2,1)S(1)}, bf16[2,1024,128]{2,1,0:T(8,128)(2,1)S(1)}, u32[]{:S(2)}, u32[]{:S(2)}) collective-permute-start(bf16[2,1024,128]{2,1,0:T(8,128)(2,1)S(1)} %pad_maximum_fusion.7), channel_id=1, source_target_pairs={{0,2},{2,0},{4,6},{6,4},{8,10},{10,8},{12,14},{14,12},{16,18},{18,... | collective-permute-start | bytes 1572872 | tf_op jit(solution)/shard_map/ppermute | solution.py:377
  241.3 6.6 %collective-permute-start.61 = (bf16[384,128]{1,0:T(8,128)(2,1)S(1)}, bf16[384,128]{1,0:T(8,128)(2,1)S(1)}, u32[]{:S(2)}, u32[]{:S(2)}) collective-permute-start(bf16[384,128]{1,0:T(8,128)(2,1)S(1)} %fusion.31), channel_id=1, source_target_pairs={{0,24},{2,26},{4,28},{6,30},{8,16},{10,18},{12,20},{14,22},{16,8},... | collective-permute-start | bytes 294920 | tf_op jit(solution)/shard_map/ppermute | solution.py:377
  243.0 6.9 %collective-permute-start.60 = (bf16[384,128]{1,0:T(8,128)(2,1)S(1)}, bf16[384,128]{1,0:T(8,128)(2,1)S(1)}, u32[]{:S(2)}, u32[]{:S(2)}) collective-permute-start(bf16[384,128]{1,0:T(8,128)(2,1)S(1)} %fusion.31), channel_id=1, source_target_pairs={{0,16},{2,18},{4,20},{6,22},{8,24},{10,26},{12,28},{14,30},{16,0},... | collective-permute-start | bytes 294920 | tf_op jit(solution)/shard_map/ppermute | solution.py:377
  243.0 6.9 %collective-permute-start.59 = (bf16[384,128]{1,0:T(8,128)(2,1)S(1)}, bf16[384,128]{1,0:T(8,128)(2,1)S(1)}, u32[]{:S(2)}, u32[]{:S(2)}) collective-permute-start(bf16[384,128]{1,0:T(8,128)(2,1)S(1)} %fusion.31), channel_id=1, source_target_pairs={{0,8},{2,10},{4,12},{6,14},{8,0},{10,2},{12,4},{14,6},{16,24},{18,... | collective-permute-start | bytes 294920 | tf_op jit(solution)/shard_map/ppermute | solution.py:377
  245.8 5.1 %collective-permute-start.51 = (bf16[2,1024,128]{2,1,0:T(8,128)(2,1)S(1)}, bf16[2,1024,128]{2,1,0:T(8,128)(2,1)S(1)}, u32[]{:S(2)}, u32[]{:S(2)}) collective-permute-start(bf16[2,1024,128]{2,1,0:T(8,128)(2,1)S(1)} %pad_maximum_fusion.8), channel_id=1, source_target_pairs={{0,2},{2,0},{4,6},{6,4},{8,10},{10,8},{12,14},{14,12},{16,18},{18,... | collective-permute-start | bytes 1572872 | tf_op jit(solution)/shard_map/ppermute | solution.py:377
  250.1 7.8 %collective-permute-start.62 = (bf16[1536,128]{1,0:T(8,128)(2,1)S(1)}, bf16[1536,128]{1,0:T(8,128)(2,1)S(1)}, u32[]{:S(2)}, u32[]{:S(2)}) collective-permute-start(bf16[1536,128]{1,0:T(8,128)(2,1)S(1)} %get-tuple-element.133), channel_id=1, source_target_pairs={{0,4},{2,6},{4,0},{6,2},{8,12},{10,14},{12,8},{14,10},{16,20},{18,... | collective-permute-start | bytes 1179656 | tf_op jit(solution)/shard_map/ppermute | solution.py:377
  258.9 13.0 %collective-permute-start.63 = (bf16[2,1536,128]{2,1,0:T(8,128)(2,1)}, bf16[2,1536,128]{2,1,0:T(8,128)(2,1)S(1)}, u32[]{:S(2)}, u32[]{:S(2)}) collective-permute-start(bf16[2,1536,128]{2,1,0:T(8,128)(2,1)} %pad_maximum_fusion.5), channel_id=1, source_target_pairs={{0,2},{2,0},{4,6},{6,4},{8,10},{10,8},{12,14},{14,12},{16,18},{18,... | collective-permute-start | bytes 2359304 | tf_op jit(solution)/shard_map/ppermute | solution.py:377
  (74 other events, 770.1 us)

commit v3 on v1

v3 whole, which is shorter than its diff:
```python
import functools
import math

import jax
import jax.numpy as jnp
from jax import lax
from jax.experimental import pallas as pl
from jax.experimental.pallas import tpu as pltpu
from jax.sharding import PartitionSpec as P

HEAD_DIM = 64
SEQ_LEN = 50
BLOCK = 4 * SEQ_LEN
PAD = -(-BLOCK // 16) * 16
EPS = 1e-05
NEG = -1e30
GELU_C = 0.7978845608028654
GELU_A = 0.044715
SPILL = 8 * 1024 * 1024
BF = jnp.bfloat16
F32 = jnp.float32
FIRST_GAIN, FIRST_SHIFT, OUT_BIAS, SECOND_GAIN, SECOND_SHIFT, DOWN_BIAS, PRIOR_GAIN, PRIOR_SHIFT, UP_BIAS, PRIOR_BIAS = range(10)


def mm(a, b):
    return lax.dot_general(a, b, (((1,), (0,)), ((), ())), preferred_element_type=F32)


def mm_bt(a, b):
    return lax.dot_general(a, b, (((1,), (1,)), ((), ())), preferred_element_type=F32)


def mm_at(a, b):
    return lax.dot_general(a, b, (((0,), (0,)), ((), ())), preferred_element_type=F32)


def norm_of(value):
    centre = value - jnp.mean(value, axis=-1, keepdims=True)
    factor = lax.rsqrt(jnp.mean(centre * centre, axis=-1, keepdims=True) + EPS)
    return centre * factor, factor


def norm_back(grad, unit, factor, gain):
    scaled = grad * gain
    first = jnp.mean(scaled, axis=-1, keepdims=True)
    second = jnp.mean(scaled * unit, axis=-1, keepdims=True)
    return factor * (scaled - first - unit * second)


def col_sum(value):
    return jnp.sum(value, axis=0, keepdims=True)


def whole_rows(here, own, other):
    low = jnp.where(here == 0, own[...], other[...])
    high = jnp.where(here == 0, other[...], own[...])
    return jnp.concatenate([low, high], axis=1).astype(F32)


def in_order(core, got, near, axis):
    low = jnp.where(core == 0, got, near)
    high = jnp.where(core == 0, near, got)
    return jnp.concatenate([low, high], axis=axis)


def allowed_pairs(seg):
    seg2 = jnp.concatenate([seg, seg], axis=0)
    row = lax.broadcasted_iota(jnp.int32, (2 * PAD, PAD), 0)
    row = jnp.where(row >= PAD, row - PAD, row)
    col = lax.broadcasted_iota(jnp.int32, (2 * PAD, PAD), 1)
    return (col <= row) & (col >= seg2)


def two_heads(value):
    first = lax.broadcasted_iota(jnp.int32, value.shape, 1) < HEAD_DIM
    none = jnp.zeros_like(value)
    return jnp.concatenate([jnp.where(first, value, none), jnp.where(first, none, value)], axis=0)


def one_pair(value):
    first = lax.broadcasted_iota(jnp.int32, (PAD, 2 * HEAD_DIM), 1) < HEAD_DIM
    return jnp.where(first, value[:PAD], value[PAD:])


def softmax_of(query2, key, allowed):
    scores = jnp.where(allowed, mm_bt(query2, key), NEG)
    expo = jnp.exp(scores - jnp.max(scores, axis=-1, keepdims=True))
    return expo * (1.0 / jnp.sum(expo, axis=-1, keepdims=True))


def vector(small, index, n):
    return small[index : index + 1, :n]


def blocks_in(ref):
    return [slice(i * PAD, i * PAD + PAD) for i in range(ref.shape[0] // PAD)]


def add_up(sums, values):
    return [v if s is None else s + v for s, v in zip(sums, values, strict=True)]


def split_rows(half, source, own, sent, wide_rows):
    rows, n = source.shape
    wide_rows[0:rows, 0:n] = source[...].astype(F32)
    for which, target in ((half, own), (1 - half, sent)):
        for block, at in enumerate(blocks_in(target)):
            start = pl.multiple_of(which * (rows // 2) + block * BLOCK, 8)
            part = wide_rows[pl.ds(start, PAD), 0:n]
            inside = lax.broadcasted_iota(jnp.int32, part.shape, 0) < BLOCK
            target[at, :] = jnp.where(inside, part, 0.0).astype(BF)


def first_kernel(s, frames, qkv, up, prior, down, out, *refs):
    smalls, (qkv_ref, sent_ref, wide_ref, tall_ref, bias_ref, own_ref, small_ref, wide_rows) = refs[:-8], refs[-8:]
    qkv_ref[...] = qkv[...]
    split_rows(s[0], frames, own_ref, sent_ref, wide_rows)
    n, m = up.shape[1], down.shape[0]
    wide_ref[:, :n] = up[...]
    wide_ref[:, n:] = prior[...]
    tall_ref[:m, :] = down[...]
    tall_ref[m:, :] = out[...]
    for i, ref in enumerate(smalls):
        small_ref[i : i + 1, : ref.shape[1]] = ref[...]
    n = smalls[UP_BIAS].shape[1]
    bias_ref[:, :n] = smalls[UP_BIAS][...]
    bias_ref[:, n:] = smalls[PRIOR_BIAS][...]


def cotangents_kernel(s, logit, out, logit_sent, out_sent, logit_own, out_own, wide_rows):
    split_rows(s[0], logit, logit_own, logit_sent, wide_rows)
    split_rows(s[0], out, out_own, out_sent, wide_rows)


def gate(values, after, name=None):
    def run(*refs):
        pass

    near = pl.BlockSpec(memory_space=pltpu.VMEM)
    return pl.pallas_call(
        run,
        in_specs=[near] * (len(values) + len(after)),
        out_specs=[near] * len(values),
        out_shape=[pltpu.VMEM(v.shape, v.dtype) for v in values],
        input_output_aliases={i: i for i in range(len(values))},
        name=name,
    )(*[pin(v) for v in values], *[pin(v) for v in after])


def attend_kernel(
    s, own, other, seg, small, qkv, got, near,
    first_ref, triple_ref, mixed_ref, qkv_other_ref,
):
    unit, _ = norm_of(whole_rows(s[0], own, other))
    n = first_ref.shape[1]
    first_ref[...] = (unit * vector(small, FIRST_GAIN, n) + vector(small, FIRST_SHIFT, n)).astype(BF)
    for c in range(3):
        qkv_other_ref[c] = in_order(s[2], got[c], near[c], 1)
        for half, weight in enumerate((qkv, qkv_other_ref)):
            value = mm(first_ref[...], weight[c]).astype(BF)
            triple_ref[:, (half * 3 + c) * 256 : (half * 3 + c + 1) * 256] = value
    for at in blocks_in(own):
        allowed = allowed_pairs(seg[at, :])
        for pair in range(4):
            start = (pair // 2) * 768 + (pair % 2) * 128
            query, key, value = (
                triple_ref[at, start + c * 256 : start + c * 256 + 128] for c in range(3)
            )
            query2 = two_heads(query * HEAD_DIM ** (-0.5))
            weights = softmax_of(query2, key, allowed).astype(BF)
            mixed_ref[at, pair * 128 : pair * 128 + 128] = one_pair(mm(weights, value)).astype(BF)


def feed_kernel(
    s, own, other, mixed, small, out, t0, t1, t2, t3, up, down, w0, w1, w2, w3, bias_other,
    block_other_ref, block_own_ref, middle_ref, second_ref, act_ref, slope_ref, ending_ref, prior_in_ref,
    out_other_ref,
):
    n, half = out.shape[0], up.shape[1]
    for j, piece in enumerate((t0, t1, t2, t3)):
        size = n // 4
        out_other_ref[pl.ds(pl.multiple_of((s[1] ^ j) * size, 16), size), :] = piece[256:, :]
    middle_ref[...] = (
        whole_rows(s[0], own, other)
        + vector(small, OUT_BIAS, middle_ref.shape[1])
        + mm(mixed[:, :n], out[...])
        + mm(mixed[:, n:], out_other_ref[...])
    )
    unit, _ = norm_of(middle_ref[...])
    wide = middle_ref.shape[1]
    second_ref[...] = (unit * vector(small, SECOND_GAIN, wide) + vector(small, SECOND_SHIFT, wide)).astype(BF)
    ending_ref[...] = middle_ref[...] + vector(small, DOWN_BIAS, wide)
    for i in range(8):
        if i < 4:
            at = slice(i * 256, i * 256 + 256)
            w_up, w_down, bias = up[:, at], down[at, :], small[UP_BIAS : UP_BIAS + 1, at]
        else:
            place = pl.multiple_of((s[1] ^ (i - 4)) * 256, 256)
            at = pl.ds(pl.multiple_of(half + place, 256), 256)
            w_up, w_down = (w0, w1, w2, w3)[i - 4][:, :256], (t0, t1, t2, t3)[i - 4][:256, :]
            bias = bias_other[:, pl.ds(place, 256)]
        for rows in blocks_in(own):
            hidden = mm(second_ref[rows, :], w_up) + bias
            square = hidden * hidden
            bent = jnp.tanh(GELU_C * (hidden + GELU_A * hidden * square))
            act = (0.5 * hidden * (1.0 + bent)).astype(BF)
            slope = 0.5 * (1.0 + bent) + (0.5 * GELU_C) * hidden * (1.0 - bent * bent) * (
                1.0 + (3.0 * GELU_A) * square
            )
            act_ref[rows, at] = act
            slope_ref[rows, at] = slope
            ending_ref[rows, :] += mm(act, w_down)
    total = ending_ref[...]
    unit, _ = norm_of(total)
    prior_in_ref[...] = (unit * vector(small, PRIOR_GAIN, wide) + vector(small, PRIOR_SHIFT, wide)).astype(BF)
    low, high = total[:, :256].astype(BF), total[:, 256:].astype(BF)
    block_own_ref[...] = jnp.where(s[0] == 0, low, high)
    block_other_ref[...] = jnp.where(s[0] == 0, high, low)


def prior_kernel(
    s, prior_in, ending, small, logit_own, out_own, prior, w0, w1, w2, w3, logit_other, out_other, bias_other,
    logits_other_ref, logits_ref, grad_ending_ref, ending_grad_ref, vec_ref, bias_ref, weight,
):
    half = prior.shape[1]
    for j, piece in enumerate((w0, w1, w2, w3)):
        weight[:, pl.ds(pl.multiple_of((s[1] ^ j) * 128, 128), 128)] = piece[:, 256:]
    logits_other_ref[...] = (mm(prior_in[...], weight[...]) + bias_other[:, -half:]).astype(BF)
    logits_ref[...] = mm(prior_in[...], prior[...]) + vector(small, PRIOR_BIAS, half)
    logits_ref.send()
    back = mm_bt(logit_own[...], prior[...]) + mm_bt(logit_other[...], weight[...])
    unit, factor = norm_of(ending[...])
    gain = vector(small, PRIOR_GAIN, unit.shape[1])
    grad = whole_rows(s[0], out_own, out_other) + norm_back(back, unit, factor, gain)
    grad_ending_ref[...] = grad
    ending_grad_ref[...] = grad.astype(BF)
    vec_ref[...] = jnp.concatenate([col_sum(back * unit), col_sum(back), col_sum(grad)], axis=0)
    bias_ref[:, :half] = col_sum(logit_own[...].astype(F32))
    bias_ref[:, half:] = col_sum(logit_other[...].astype(F32))


def store_piece(keep, send, h, j, start, value):
    at = slice(start, start + value.shape[0])
    if j < 2:
        keep[h * 2 + j, at, :] = value
    else:
        send[h * 2 + j - 2, at, :] = value.astype(BF)


def late_grads_kernel(s, prior_in, logit_own, logit_other, act, ending_grad, keep, send, wide):
    half = act.shape[1] // 2
    n = prior_in.shape[1]
    for h in range(2):
        wide[...] = mm_at(prior_in[...], (logit_own, logit_other)[h][...])
        for j in (2, 3, 0, 1):
            place = s[1] ^ j
            store_piece(keep, send, h, j, 0, wide[:, pl.ds(pl.multiple_of(place * 128, 128), 128)])
            part = act[:, pl.ds(pl.multiple_of(h * half + place * 256, 256), 256)]
            value = mm_at(part, ending_grad[...])
            for t in range(n // 128):
                store_piece(keep, send, h, j, n + t * 256, value[:, t * 128 : t * 128 + 128])


def up_grads_kernel(s, second, hidden_grad, keep, send, turned):
    turned[...] = second[...].T
    half = hidden_grad.shape[1] // 2
    n = second.shape[1]
    for h in range(2):
        for j in (2, 3, 0, 1):
            at = pl.ds(pl.multiple_of(h * half + (s[1] ^ j) * 256, 256), 256)
            value = mm(turned[...], hidden_grad[:, at])
            for t in range(2):
                store_piece(keep, send, h, j, t * n, value[:, t * 128 : t * 128 + 128])


def early_grads_kernel(
    s, mixed, middle_grad, first, triple_grad, vec_one, vec_two, vec_three, bias_up, bias_prior,
    keep, send, wide, vectors,
):
    row = 0
    for ref in (vec_one, vec_two, vec_three):
        for i in range(ref.shape[0]):
            for t in range(ref.shape[1] // 128):
                vectors[row : row + 1, :] = ref[i : i + 1, t * 128 : t * 128 + 128]
                row += 1
    for ref in (bias_up, bias_prior):
        tiles = ref.shape[1] // 128
        for t in range(tiles):
            place = row + lax.rem(t + s[0] * (tiles // 2), tiles)
            vectors[pl.ds(place, 1), :] = ref[:, t * 128 : t * 128 + 128]
        row += tiles
    vectors[row:, :] = jnp.zeros((vectors.shape[0] - row, 128), F32)
    m = mixed.shape[1] // 2
    for h in range(2):
        wide[...] = mm_at(mixed[:, h * m : h * m + m], middle_grad[...])
        for j in (2, 3, 0, 1):
            place = pl.multiple_of((s[1] ^ j) * 128, 128)
            store_piece(keep, send, h, j, 0, wide[:, pl.ds(place, 128)])
            value = mm_at(first[:, pl.ds(place, 128)], triple_grad[:, h * 768 : h * 768 + 768])
            for c in range(3):
                for t in range(2):
                    at = slice(c * 256 + t * 128, c * 256 + t * 128 + 128)
                    store_piece(keep, send, h, j, m + (t * 3 + c) * 128, value[:, at])
            part = vectors[(h * 2 + j % 2) * 16 : (h * 2 + j % 2) * 16 + 16, :]
            store_piece(keep, send, h, j, m + 768, part)


def feed_back_kernel(
    s, ending_grad, slope, middle, grad_ending, small, down, up, t0, w0, t1, w1, t2, w2, t3, w3,
    hidden_grad_ref, grad_middle_ref, middle_grad_ref, vec_ref, bias_ref, back,
):
    half = up.shape[1]
    for i in range(8):
        if i < 4:
            at = slice(i * 256, i * 256 + 256)
            w_up, w_down = up[:, at], down[at, :]
        else:
            at = pl.ds(pl.multiple_of(half + (s[1] ^ (i - 4)) * 256, 256), 256)
            w_up, w_down = (w0, w1, w2, w3)[i - 4][:, :256], (t0, t1, t2, t3)[i - 4][:256, :]
        sums = [None]
        for rows in blocks_in(ending_grad):
            low = (mm_bt(ending_grad[rows, :], w_down) * slope[rows, at]).astype(BF)
            hidden_grad_ref[rows, at] = low
            sums = add_up(sums, [col_sum(low.astype(F32))])
            value = mm_bt(low, w_up)
            if i == 0:
                back[rows, :] = value
            else:
                back[rows, :] += value
        bias_ref[:, at] = sums[0]
    unit, factor = norm_of(middle[...])
    value = back[...]
    gain = vector(small, SECOND_GAIN, unit.shape[1])
    total = grad_ending[...] + norm_back(value, unit, factor, gain)
    grad_middle_ref[...] = total
    middle_grad_ref[...] = total.astype(BF)
    vec_ref[...] = jnp.concatenate([col_sum(value * unit), col_sum(value), col_sum(total)], axis=0)


def attend_back_kernel(
    s, middle_grad, grad_middle, own, triple, qkv_other, out_other, small, out, seg, other, qkv,
    triple_grad_ref, frames_other_ref, frames_own_ref, vec_ref, mixed_grad,
):
    n = out.shape[0]
    mixed_grad[:, :n] = mm_bt(middle_grad[...], out[...]).astype(BF)
    mixed_grad[:, n:] = mm_bt(middle_grad[...], out_other[...]).astype(BF)
    factor = HEAD_DIM ** (-0.5)
    for at in blocks_in(own):
        allowed = allowed_pairs(seg[at, :])
        for pair in range(4):
            start = (pair // 2) * 768 + (pair % 2) * 128
            query, key, value = (triple[at, start + c * 256 : start + c * 256 + 128] for c in range(3))
            query2 = two_heads(query * factor)
            mixed2 = two_heads(mixed_grad[at, pair * 128 : pair * 128 + 128])
            again = softmax_of(query2, key, allowed)
            weight_grad = mm_bt(mixed2, value)
            inner = jnp.sum(again * weight_grad, axis=-1, keepdims=True)
            score_grad = (again * (weight_grad - inner)).astype(BF)
            thirds = (
                (one_pair(mm(score_grad, key)) * factor).astype(BF),
                mm_at(score_grad, query2).astype(BF),
                mm_at(again.astype(BF), mixed2).astype(BF),
            )
            for c in range(3):
                triple_grad_ref[at, start + c * 256 : start + c * 256 + 128] = thirds[c]
    back = None
    for half, weight in enumerate((qkv, qkv_other)):
        for c in range(3):
            value = mm_bt(triple_grad_ref[:, (half * 3 + c) * 256 : (half * 3 + c + 1) * 256], weight[c])
            back = value if back is None else back + value
    unit, scale = norm_of(whole_rows(s[0], own, other))
    total = grad_middle[...] + norm_back(back, unit, scale, vector(small, FIRST_GAIN, unit.shape[1]))
    low, high = total[:, :256], total[:, 256:]
    frames_own_ref[...] = jnp.where(s[0] == 0, low, high)
    frames_other_ref[...] = jnp.where(s[0] == 0, high, low).astype(BF)
    vec_ref[...] = jnp.concatenate([col_sum(back * unit), col_sum(back)], axis=0)


def late_place_kernel(s, mine, near, far, farther, prior_ref, down_ref):
    n = prior_ref.shape[0]
    for j, piece in enumerate((mine, near, far, farther)):
        place = s[1] ^ j
        prior_ref[:, pl.ds(pl.multiple_of(place * 128, 128), 128)] = piece[:n, :].astype(F32)
        rows = pl.ds(pl.multiple_of(place * 256, 256), 256)
        for t in range(down_ref.shape[1] // 128):
            down_ref[rows, t * 128 : t * 128 + 128] = piece[n + t * 256 : n + t * 256 + 256, :].astype(F32)


def up_place_kernel(s, mine, near, far, farther, up_ref):
    n = up_ref.shape[0]
    for j, piece in enumerate((mine, near, far, farther)):
        for t in range(2):
            start = pl.multiple_of((s[1] ^ j) * 256 + t * 128, 128)
            up_ref[:, pl.ds(start, 128)] = piece[t * n : t * n + n, :].astype(F32)


def early_place_kernel(s, mine, near, far, farther, sums, out_ref, qkv_ref, *vecs):
    n = out_ref.shape[0]
    for j, piece in enumerate((mine, near, far, farther)):
        at = pl.ds(pl.multiple_of((s[1] ^ j) * 128, 128), 128)
        out_ref[:, at] = piece[0:n, :].astype(F32)
        for c in range(3):
            for t in range(2):
                start = n + (t * 3 + c) * 128
                qkv_ref[c, at, t * 128 : t * 128 + 128] = piece[start : start + 128, :].astype(F32)
    row = 0
    for ref in vecs[:8]:
        for t in range(ref.shape[1] // 128):
            ref[:, t * 128 : t * 128 + 128] = sums[row : row + 1, :]
            row += 1
    for ref in vecs[8:]:
        tiles = ref.shape[1] // 128
        for t in range(tiles):
            ref[:, t * 128 : t * 128 + 128] = sums[pl.ds(row + s[0] * tiles + t, 1), :]
        row += 2 * tiles


def core_kernel(lows, rests, s, keep, got, *outs):
    for places, low in zip(lows, outs):
        for k, i in enumerate(places):
            value = (keep[i] + got[i].astype(F32)).astype(BF)
            if len(places) == 1:
                low[...] = value
            else:
                low[k] = value
    for k, i in enumerate(rests):
        outs[-1][k] = keep[i] + got[i].astype(F32)


def early_core_kernel(extra, s, keep, got, *outs):
    n = keep.shape[1] - extra // 4
    for i in (3, 2, 1, 0):
        out = outs[i - 1] if i else outs[3]
        dtype = BF if i else F32
        out[:n, :] = (keep[i, :n] + got[i, :n].astype(F32)).astype(dtype)
        for k in range(4):
            start = n + k * (extra // 4)
            out[start : start + extra // 4, :] = (keep[k, n:] + got[k, n:].astype(F32)).astype(dtype)


def fold_two_kernel(s, rest, got, low, out):
    low[...] = (rest[1] + got[1].astype(F32)).astype(BF)
    out[...] = rest[0] + got[0].astype(F32)


def fold_kernel(size, which, extra, n_got, s, rest, *refs):
    got, outs, total = refs[:n_got], refs[n_got:-1], refs[-1]
    total[...] = functools.reduce(lambda x, y: x + y[...].astype(F32), got, rest[...])
    n = (total.shape[0] - extra) // size
    for k in list(range(1, size)) + [0]:
        target = outs[k]
        start = pl.multiple_of((s[which] ^ k) * n if size > 1 else 0, 16)
        target[:n, :] = total[pl.ds(start, n), :].astype(BF if k else F32)
        if extra:
            target[n:, :] = total[n * size :, :].astype(BF if k else F32)


def last_fold_kernel(extra, n_got, s, rest, *refs):
    got, outs = refs[:n_got], refs[n_got:]
    total = functools.reduce(lambda x, y: x + y[...].astype(F32), got, rest[...])
    n = total.shape[0] - extra
    outs[0][...] = total[:n].astype(BF)
    if extra:
        outs[1][...] = total[n:]


def join_kernel(which, s, *refs):
    parts, out = refs[:-1], refs[-1]
    n = parts[0].shape[0]
    for k, part in enumerate(parts):
        out[pl.ds(pl.multiple_of((s[which] ^ k) * n, 16), n), :] = part[...]


class Loaded:
    def __init__(self, ref, copy):
        self.ref, self.copy, self.shape = ref, copy, ref.shape

    def get(self):
        if self.copy is not None:
            self.copy.wait()
            self.copy = None
        return self.ref

    def __getitem__(self, index):
        return self.get()[index]


class Leaving:
    def __init__(self, ref, copy):
        self.ref, self.copy, self.shape, self.sent = ref, copy, ref.shape, False

    def __getitem__(self, index):
        return self.ref[index]

    def __setitem__(self, index, value):
        self.ref[index] = value

    def send(self):
        if not self.sent:
            self.copy.start()
            self.sent = True


class Far:
    def __init__(self, value, shape=None, cut=None):
        self.value, self.shape, self.cut = value, shape or value.shape, cut or (lambda s, ref: ref)


def call(kernel, scalars, ins, outs, scratch=(), name=None, after=()):
    n_in, n_out, n_after = len(ins), len(outs), len(after)
    far_in = [i for i, v in enumerate(ins) if isinstance(v, Far)]
    far_out = [i for i, o in enumerate(outs) if not o[2]]
    room = [pltpu.VMEM(ins[i].shape, ins[i].value.dtype) for i in far_in]
    room += [pltpu.VMEM(outs[i][0], outs[i][1]) for i in far_out]
    need = sum(math.prod(r.shape) * jnp.dtype(r.dtype).itemsize for r in room + list(scratch))

    def run(s, *refs):
        given, refs = list(refs[:n_in]), refs[n_in + n_after :]
        made, refs = list(refs[:n_out]), refs[n_out:]
        own, refs = refs[: len(scratch)], refs[len(scratch) :]
        rooms, sems = refs[:-1], refs[-1]
        for k, i in enumerate(far_in):
            copy = pltpu.make_async_copy(ins[i].cut(s, given[i]), rooms[k], sems.at[k])
            copy.start()
            given[i] = Loaded(rooms[k], copy)
        leaving = []
        for k, i in enumerate(far_out, len(far_in)):
            made[i] = Leaving(rooms[k], pltpu.make_async_copy(rooms[k], made[i], sems.at[k]))
            leaving.append(made[i])
        kernel(s, *given, *made, *own)
        for value in given:
            if isinstance(value, Loaded):
                value.get()
        for value in leaving:
            value.send()
        for value in leaving:
            value.copy.wait()

    near, far = pl.BlockSpec(memory_space=pltpu.VMEM), pl.BlockSpec(memory_space=pltpu.HBM)
    return pl.pallas_call(
        run,
        in_specs=[pl.BlockSpec(memory_space=pltpu.SMEM)]
        + [far if isinstance(v, Far) else near for v in ins]
        + [near] * n_after,
        out_specs=[near if stays else far for _, _, stays in outs],
        out_shape=[(pltpu.VMEM if stays else pltpu.HBM)(shape, dtype) for shape, dtype, stays in outs],
        scratch_shapes=list(scratch) + room + [pltpu.SemaphoreType.DMA((max(1, len(room)),))],
        compiler_params=pltpu.CompilerParams(vmem_limit_bytes=need + SPILL),
        cost_estimate=pl.CostEstimate(flops=0, bytes_accessed=0, transcendentals=0),
        name=name,
    )(scalars, *[pin(v) for v in ins], *[pin(v) for v in after])


def pin(value):
    if isinstance(value, Far):
        return pltpu.with_memory_space_constraint(value.value, pltpu.HBM)
    return pltpu.with_memory_space_constraint(value, pltpu.VMEM)


def swap(value, axes, sizes, mask):
    count = 1
    for size in sizes:
        count *= size
    return lax.ppermute(value, axes, [(i, i ^ mask) for i in range(count)])


class Moves:
    def __init__(self, n_dp, n_tensor):
        self.n_dp, self.n_tensor = n_dp, n_tensor
        self.dp = lax.axis_index("dp")
        self.here = lax.axis_index("tensor")

    def along(self, value, mask):
        return swap(value, "dp", (self.n_dp,), mask)

    def core(self, value):
        return self.along(value, 1)

    def side(self, value):
        return self.along(value, 2)

    def over(self, value):
        return swap(value, "tensor", (self.n_tensor,), 1)

    def cross(self, value):
        return swap(value, ("dp", "tensor"), (self.n_dp, self.n_tensor), 5)

    def groups(self):
        shift, rest = 2, self.n_dp // 4
        while rest > 1:
            size = 4 if rest % 4 == 0 else 2
            yield shift, size
            shift, rest = shift + (2 if size == 4 else 1), rest // size


    def reduce_core(self, scalars, keep, sent, lows, rests, name, after=()):
        n = sent.shape[1]
        outs = [(((len(p), n, 128) if len(p) > 1 else (n, 128)), BF, True) for p in lows]
        got = self.core(sent)
        return call(
            functools.partial(core_kernel, lows, rests),
            scalars,
            [keep, got],
            outs + [((len(rests), n, 128), F32, True)],
            name=name,
            after=after,
        )

    def fold_two(self, scalars, rest, got, name, after=()):
        n = got.shape[1]
        return call(
            fold_two_kernel, scalars, [rest, got], [((n, 128), BF, True), ((n, 128), F32, True)], name=name, after=after
        )

    def fold_rest(self, scalars, rest, got, name, extra=0, after=()):
        n = got[0].shape[0] - extra
        which = 3
        for shift, size in self.groups():
            m = n // size + extra
            outs = [((m, 128), F32, True)] + [((m, 128), BF, True)] * (size - 1)
            rest, *sent = call(
                functools.partial(fold_kernel, size, which, extra, len(got)),
                scalars,
                [rest, *got],
                outs,
                [pltpu.VMEM((n + extra, 128), F32)],
                name=name + "_fold",
                after=after,
            )
            got = [self.along(v, k << shift) for k, v in enumerate(sent, 1)]
            n, which, after = n // size, which + 1, ()
        outs = [((n, 128), BF, True)] + ([((extra, 128), F32, True)] if extra else [])
        return call(functools.partial(last_fold_kernel, extra, len(got)), scalars, [rest, *got], outs, name=name + "_last")

    def gather(self, scalars, total, name):
        groups = list(self.groups())
        for i in reversed(range(len(groups))):
            shift, size = groups[i]
            parts = [total] + [self.along(total, k << shift) for k in range(1, size)]
            (total,) = call(
                functools.partial(join_kernel, 3 + i),
                scalars,
                parts,
                [((total.shape[0] * size, 128), BF, True)],
                name=name + "_join",
            )
        near = self.side(total)
        return total, near, self.core(total), self.core(near)


def rows_of(here, own, other):
    cut = [
        v.reshape(-1, PAD, v.shape[1])[:, :BLOCK].reshape(-1, v.shape[1]) for v in (own, other.astype(own.dtype))
    ]
    return jnp.concatenate(
        [jnp.where(here == 0, cut[0], cut[1]), jnp.where(here == 0, cut[1], cut[0])], axis=0
    )


def episode_starts(resets):
    rows = resets.shape[0]
    inside = lax.broadcasted_iota(jnp.int32, (rows // SEQ_LEN, SEQ_LEN), 1)
    starts = jnp.where((inside == 0) | (resets.reshape(-1, SEQ_LEN) == 1), inside, 0)
    starts = lax.cummax(starts, axis=1).reshape(rows // BLOCK, BLOCK // SEQ_LEN, SEQ_LEN)
    starts = starts + SEQ_LEN * jnp.arange(BLOCK // SEQ_LEN, dtype=jnp.int32)[None, :, None]
    starts = starts.reshape(rows // BLOCK, BLOCK)
    tail = jnp.broadcast_to(jnp.arange(BLOCK, PAD, dtype=jnp.int32), (rows // BLOCK, PAD - BLOCK))
    return jnp.concatenate([starts, tail], axis=1)


def local(
    n_dp, n_tensor, frames, resets, first_gain, first_shift, qkv_weight, out_weight, out_bias, second_gain,
    second_shift, up_weight, up_bias, down_weight, down_bias, prior_gain, prior_shift, prior_weight,
    prior_bias, out_cotangent, logit_cotangent,
):
    move = Moves(n_dp, n_tensor)
    rows, half = frames.shape
    width = 2 * half
    mine = rows // 2
    blocks = mine // BLOCK
    hidden_width, n_logits = up_bias.shape[0], prior_bias.shape[0]
    row = lambda v: v.reshape(1, -1)
    core, side = move.dp & 1, (move.dp >> 1) & 1
    groups = [(move.dp >> shift) & (size - 1) for shift, size in move.groups()]
    scalars = jnp.stack([move.here, core * 2 + side, core, *groups]).astype(jnp.int32)
    here = move.here
    total_rows = blocks * PAD
    quarter = hidden_width // 4

    def near_rows(*entries):
        return [((total_rows, n), dtype, True) for n, dtype in entries]

    def pieces(n):
        return [((4, n, 128), F32, True), ((4, n, 128), BF, True)]

    def columns(value, size, which):
        cut = lambda s, ref: ref.at[..., pl.ds(pl.multiple_of(s[which] * size, 128), size)]
        return Far(value, (*value.shape[:-1], size), cut)

    def some_rows(value, size, which):
        cut = lambda s, ref: ref.at[pl.ds(pl.multiple_of(s[which] * size, 16), size), :]
        return Far(value, (size, value.shape[1]), cut)

    vectors = [first_gain, first_shift, out_bias, second_gain, second_shift, down_bias, prior_gain, prior_shift]
    vectors = [row(v) for v in vectors + [up_bias, prior_bias]]
    qkv_part, frames_sent, wide_part, tall_part, bias_sent, frames_own, small = call(
        first_kernel,
        scalars,
        [
            Far(frames),
            columns(qkv_weight, half // 2, 2),
            columns(up_weight, quarter, 1),
            columns(prior_weight, n_logits // 4, 1),
            some_rows(down_weight, quarter, 1),
            some_rows(out_weight, half // 4, 1),
            *[Far(v) for v in vectors],
        ],
        [((3, width, half // 2), BF, True)]
        + near_rows((half, BF))
        + [((width, quarter + n_logits // 4), BF, True), ((quarter + half // 4, width), BF, True)]
        + [((1, hidden_width + n_logits), F32, True)]
        + near_rows((half, BF))
        + [((16, hidden_width), F32, True)],
        [pltpu.VMEM((rows + 16, half), F32)],
        "first_parts",
    )
    qkv_got = move.over(qkv_part)
    frames_other = move.over(frames_sent)
    qkv_near = move.core(qkv_got)
    wide_part, tall_part, bias_sent = gate([wide_part, tall_part, bias_sent], [qkv_got], "after_first")
    wide_got = move.over(wide_part)
    tall_got = move.over(tall_part)
    bias_other = move.over(bias_sent)
    seg = lax.dynamic_slice_in_dim(episode_starts(resets), here * blocks, blocks, 0).reshape(-1, 1)
    first, triple, mixed, qkv_other = call(
        attend_kernel,
        scalars,
        [frames_own, frames_other, seg, small, Far(qkv_weight), qkv_got, qkv_near],
        near_rows((width, BF), (3 * width, BF), (width, BF)) + [(qkv_weight.shape, BF, True)],
        name="attend",
    )
    wide_got, tall_got = gate([wide_got, tall_got], [mixed], "after_attend")

    def all_quarters(got):
        beside = move.side(got)
        return [got, beside, move.core(got), move.core(beside)]

    wide_pieces = all_quarters(wide_got)
    tall_pieces = all_quarters(tall_got)
    logit_sent, out_sent, logit_own, out_own = call(
        cotangents_kernel,
        scalars,
        [Far(logit_cotangent), Far(out_cotangent)],
        near_rows((n_logits, BF), (half, BF)) + near_rows((n_logits, BF), (half, BF)),
        [pltpu.VMEM((rows + 16, n_logits), F32)],
        name="cotangents",
        after=(tall_got,),
    )
    logit_other = move.over(logit_sent)
    out_other = move.over(out_sent)
    block_send, block_own, middle, second, act, slope, ending, prior_in, out_weight_other = call(
        feed_kernel,
        scalars,
        [frames_own, frames_other, mixed, small, Far(out_weight), *tall_pieces, Far(up_weight), Far(down_weight)]
        + [*wide_pieces, bias_other],
        near_rows((half, BF), (half, BF))
        + near_rows((width, F32), (width, BF), (2 * hidden_width, BF), (2 * hidden_width, F32))
        + near_rows((width, F32), (width, BF))
        + [(out_weight.shape, BF, True)],
        name="feed",
    )
    block_got = move.over(block_send)
    logits_send, logits_own, grad_ending, ending_grad, vec_three, prior_bias_sum = call(
        prior_kernel,
        scalars,
        [prior_in, ending, small, logit_own, out_own, Far(prior_weight), *wide_pieces, logit_other, out_other, bias_other],
        near_rows((n_logits, BF)) + [((total_rows, n_logits), F32, False)]
        + near_rows((width, F32), (width, BF))
        + [((3, width), F32, True), ((1, 2 * n_logits), F32, True)],
        [pltpu.VMEM(prior_weight.shape, BF)],
        name="prior",
    )
    logits_got = move.over(logits_send)
    late_keep, late_send = call(
        late_grads_kernel,
        scalars,
        [prior_in, logit_own, logit_other, act, ending_grad],
        pieces(width + hidden_width),
        [pltpu.VMEM((width, n_logits), F32)],
        name="late_grads",
        after=(block_got,),
    )
    late_low, late_rest = move.reduce_core(scalars, late_keep, late_send, ((2, 3),), (0, 1), "late_core")
    hidden_grad, grad_middle, middle_grad, vec_two, up_bias_sum = call(
        feed_back_kernel,
        scalars,
        [ending_grad, slope, middle, grad_ending, small, Far(down_weight), Far(up_weight)]
        + [v for both in zip(tall_pieces, wide_pieces) for v in both],
        near_rows((2 * hidden_width, BF), (width, F32), (width, BF))
        + [((3, width), F32, True), ((1, 2 * hidden_width), F32, True)],
        [pltpu.VMEM((total_rows, width), F32)],
        name="feed_back",
        after=(late_send,),
    )
    up_keep, up_send = call(
        up_grads_kernel,
        scalars,
        [second, hidden_grad],
        pieces(width * hidden_width // 512),
        [pltpu.VMEM((width, total_rows), BF)],
        name="up_grads",
        after=(late_low,),
    )
    up_low, up_rest = move.reduce_core(scalars, up_keep, up_send, ((1, 3),), (0, 2), "up_core")
    late_low2, late_rest = move.fold_two(scalars, late_rest, move.over(late_low), "late_over")
    triple_grad, frames_send, frames_grad, vec_one = call(
        attend_back_kernel,
        scalars,
        [middle_grad, grad_middle, frames_own, triple, qkv_other, out_weight_other, small, Far(out_weight), seg, frames_other]
        + [Far(qkv_weight)],
        near_rows((3 * width, BF), (half, BF)) + [((total_rows, half), F32, False)] + [((2, width), F32, True)],
        [pltpu.VMEM((total_rows, width), BF)],
        name="attend_back",
        after=(up_send, logits_got),
    )
    spare = 64
    keep, send = call(
        early_grads_kernel,
        scalars,
        [mixed, middle_grad, first, triple_grad, vec_one, vec_two, vec_three, up_bias_sum, prior_bias_sum],
        pieces(half + 768 + spare // 4),
        [pltpu.VMEM((half, width), F32), pltpu.VMEM((spare, 128), F32)],
        name="early_grads",
        after=(up_low,),
    )
    up_low2, up_rest = move.fold_two(scalars, up_rest, move.side(up_low), "up_side")
    (late,) = move.fold_rest(scalars, late_rest, [move.side(late_low2)], "late")
    (up_sums,) = move.fold_rest(scalars, up_rest, [move.over(up_low2)], "up")
    late = move.gather(scalars, late, "late")
    up_sums = move.gather(scalars, up_sums, "up")
    frames_got = move.over(frames_send)
    *lows, rest = call(
        functools.partial(early_core_kernel, spare),
        scalars,
        [keep, move.core(send)],
        [((half + 768 + spare, 128), BF, True)] * 3 + [((half + 768 + spare, 128), F32, True)],
        name="early_core",
    )
    total, sums = move.fold_rest(
        scalars, rest, [move.side(lows[0]), move.over(lows[1]), move.cross(lows[2])], "early", spare
    )
    placed = call(
        early_place_kernel,
        scalars,
        [*move.gather(scalars, total, "early"), sums],
        [((half, width), F32, False), ((3, width, half), F32, False)]
        + [((1, n), F32, False) for n in [width] * 8 + [hidden_width, n_logits]],
        name="early_place",
    )
    out_grad, qkv_grad = placed[:2]
    named = [v.reshape(-1) for v in placed[2:]]
    prior_grad, down_grad = call(
        late_place_kernel,
        scalars,
        list(late),
        [((width, n_logits), F32, False), ((hidden_width, width), F32, False)],
        name="late_place",
    )
    (up_grad,) = call(
        up_place_kernel, scalars, list(up_sums), [((width, hidden_width), F32, False)], name="up_place"
    )
    return (
        rows_of(here, block_own, block_got),
        rows_of(here, logits_own, logits_got),
        rows_of(here, frames_grad, frames_got),
        named[0],
        named[1],
        qkv_grad,
        out_grad,
        named[4],
        named[2],
        named[3],
        up_grad,
        named[8],
        down_grad,
        named[7],
        named[5],
        named[6],
        prior_grad,
        named[9],
    )


def solution(mesh):
    rows, cols = P("dp", "tensor"), P(None, "tensor")
    placed = (
        rows, P("dp"), P(), P(), P(None, None, "tensor"), P("tensor", None), P(), P(), P(), cols, P("tensor"),
        P("tensor", None), P(), P(), P(), cols, P("tensor"), rows, rows,
    )
    given = (
        rows, rows, rows, P(), P(), P(None, None, "tensor"), P("tensor", None), P(), P(), P(), cols,
        P("tensor"), P("tensor", None), P(), P(), P(), cols, P("tensor"),
    )
    return jax.shard_map(
        functools.partial(local, mesh.shape["dp"], mesh.shape["tensor"]),
        mesh=mesh,
        in_specs=placed,
        out_specs=given,
        check_vma=False,
    )
```

time: 327 us -> 260 us (0.80)
  Pallas kernels: 103 us -> 75.7 us
  local copies, waits for them, and re-layouts: 32 us -> 9.25 us
  starting transfers between devices: 70.6 us -> 53.2 us
  other arithmetic: 17.4 us -> 4.42 us
  waiting for transfers between devices: 98.5 us -> 111 us
    pallas_call x6 -> x29, Pallas kernels: 103 us -> 75.7 us  [the longest x27 75.7 us: call(): pl.pallas_call(run, in_specs=[pl.BlockSpec(memory_space=pltpu.SMEM)] + [f...]
    ppermute x64 -> x54, starting transfers between devices: 70.6 us -> 53.2 us  [swap(): return lax.ppermute(value, axes, [(i, i ^ mask) for i in range(count)])]
    ppermute x64 -> x54, waiting for transfers between devices: 98.5 us -> 111 us  [swap(): return lax.ppermute(value, axes, [(i, i ^ mask) for i in range(count)])]
    dynamic_slice x10 -> x0, local copies, waits for them, and re-layouts: 11.1 us -> none  [the longest x5 7.45 us: part(): return lax.dynamic_slice_in_dim(value, index * size, size, dim)]
    convert_element_type x10 -> x0, local copies, waits for them, and re-layouts: 7.24 us -> none  [the longest x2 3.21 us: local(): early[:, 256:].reshape(4, 2, 3, 128, 128).transpose(2, 0, 3, 1, 4)]
    another operation x16 -> x1, other arithmetic: 6.55 us -> 0.08 us  [local(): jnp.stack([move.here, core * 2 + side, core, *groups]).astype(jnp.int32)]
    convert_element_type x6 -> x0, other arithmetic: 4.33 us -> none  [the longest x1 1.72 us: local(): early[:, :256].transpose(1, 0, 2).reshape(half, width).astype(F32)]
    unnamed x141 -> x34, local copies, waits for them, and re-layouts: 9.55 us -> 8.63 us
  transfers between devices with their start and end apart: 64 -> 54, of which waited for: 27 -> 21; matrix products, arithmetic and copies ran while one was open for 11% -> 2% of each run, Pallas kernels for 12% -> 25%
where the time goes in v3:
time: 260 us; the launch traced here: 256 us
  waiting for transfers between devices  111 us (43%)
  Pallas kernels  75.7 us (29%)
  starting transfers between devices  53.2 us (20%)
  local copies, waits for them, and re-layouts  9.25 us (4%)
  other arithmetic  4.42 us (2%)
    ppermute x54, waiting for transfers between devices, swap(): return lax.ppermute(value, axes, [(i, i ^ mask) for i in range(count)])  111 us
    pallas_call x27, Pallas kernels, call(): pl.pallas_call(run, in_specs=[pl.BlockSpec(memory_space=pltpu.SMEM)] + [f...  75.7 us
    ppermute x54, starting transfers between devices, swap(): return lax.ppermute(value, axes, [(i, i ^ mask) for i in range(count)])  53.2 us
    unnamed x34, local copies, waits for them, and re-layouts  8.63 us
  transfers between devices with their start and end apart: 54, of which 21 were waited for; matrix products, arithmetic and copies ran while one was open for 2% of the time, Pallas kernels for 25%

profile of v3, /device:TPU:0, one launch (start us, length us, event | category | flops | bytes accessed | tf_op | source)
XLA Modules:
  0.0 255.5 jit_solution(1711305344655447028)
XLA Ops:
  0.7 2.9 %first_parts.1 = (bf16[3,512,128]{2,1,0:T(8,128)(2,1)S(1)}, bf16[624,256]{1,0:T(8,128)(2,1)}, bf16[512,384]{1,0:T(8,128)(2,1)S(1)}, bf16[320,512]{1,0:T(8,128)(2...) custom-call(s32[4]{0:T(128)S(1)} %pad_add_fusion.s, ...), custom_call_target="tpu_custom_call" | custom-call | tf_op jit(solution)/shard_map/first_parts/pallas_call | solution.py:540
  3.6 3.0 %collective-permute-start = (bf16[624,256]{1,0:T(8,128)(2,1)}, bf16[624,256]{1,0:T(8,128)(2,1)S(1)}, u32[]{:S(2)}, u32[]{:S(2)}) collective-permute-start(bf16[624,256]{1,0:T(8,128)(2,1)} %get-tuple-element.109), channel_id=1, source_target_pairs={{0,1},{1,0},{2,3},{3,2},{4,5},{5,4},{6,7},{7,6},{8,9},{9,8},{10,11... | collective-permute-start | bytes 958472 | tf_op jit(solution)/shard_map/ppermute | solution.py:564
  7.3 15.5 %collective-permute-done.1.refs_5_.refs_3_ = bf16[3,512,128]{2,1,0:T(8,128)(2,1)S(1)} collective-permute-done((bf16[3,512,128]{2,1,0:T(8,128)(2,1)S(1)}, bf16[3,512,128]{2,1,0:T(8,128)(2,1)S(1)}, u32[]{:S(2)}, u32[]{:S(2)}) %collective-permute-start.1) | collective-permute-done | bytes 393248 | tf_op jit(solution)/shard_map/ppermute | solution.py:564
  22.8 1.7 collective-permute-start.3
  25.2 1.1 collective-permute-done.2.refs_6_
  27.0 1.0 copy-done.9
  28.0 5.3 %attend.1 = (bf16[624,512]{1,0:T(8,128)(2,1)S(1)}, bf16[624,1536]{1,0:T(8,128)(2,1)S(1)}, bf16[624,512]{1,0:T(8,128)(2,1)S(1)}, bf16[3,512,256]{2,1,0:T(8,128)(2,1)S(1)}) custom-call(s32[4]{0:T(128)S(1)} %pad_add_fusion.s, bf16[624,256]{1,0:T(8,128)(2,1)S(1)} %get-tuple-element.108.refs_0_.refs_2_, ...), custom_call_target="tpu_custom_call" | custom-call | tf_op jit(solution)/shard_map/attend/pallas_call | solution.py:540
  33.4 1.2 copy-done
  36.3 3.8 %collective-permute-done.4.refs_1_ = bf16[320,512]{1,0:T(8,128)(2,1)S(1)} collective-permute-done((bf16[320,512]{1,0:T(8,128)(2,1)S(1)}, bf16[320,512]{1,0:T(8,128)(2,1)S(1)}, u32[]{:S(2)}, u32[]{:S(2)}) %collective-permute-start.4) | collective-permute-done | bytes 327712 | tf_op jit(solution)/shard_map/ppermute | solution.py:564
  40.1 1.4 collective-permute-start.8
  42.2 10.0 %collective-permute-done.8.refs_12_.refs_7_.refs_10_ = bf16[512,384]{1,0:T(8,128)(2,1)S(1)} collective-permute-done((bf16[512,384]{1,0:T(8,128)(2,1)S(1)}, bf16[512,384]{1,0:T(8,128)(2,1)S(1)}, u32[]{:S(2)}, u32[]{:S(2)}) %collective-permute-start.8) | collective-permute-done | bytes 393248 | tf_op jit(solution)/shard_map/ppermute | solution.py:564
  52.7 3.8 %collective-permute-done.5.refs_6_.refs_9_ = bf16[320,512]{1,0:T(8,128)(2,1)S(1)} collective-permute-done((bf16[320,512]{1,0:T(8,128)(2,1)S(1)}, bf16[320,512]{1,0:T(8,128)(2,1)S(1)}, u32[]{:S(2)}, u32[]{:S(2)}) %collective-permute-start.5) | collective-permute-done | bytes 327712 | tf_op jit(solution)/shard_map/ppermute | solution.py:564
  56.5 1.1 collective-permute-start.11
  57.6 2.3 cotangents.1
  60.2 1.1 collective-permute-start.13
  61.3 0.9 collective-permute-start.14
  62.2 7.2 %feed.1 = (bf16[624,256]{1,0:T(8,128)(2,1)S(1)}, bf16[624,256]{1,0:T(8,128)(2,1)S(1)}, f32[624,512]{1,0:T(8,128)S(1)}, bf16[624,512]{1,0:T(8,128)(2,1)S(1)}, bf1...) custom-call(s32[4]{0:T(128)S(1)} %pad_add_fusion.s, ...), custom_call_target="tpu_custom_call" | custom-call | tf_op jit(solution)/shard_map/feed/pallas_call | solution.py:540
  69.5 1.2 collective-permute-start.12
  70.6 13.6 %collective-permute-done.14.refs_11_ = bf16[624,256]{1,0:T(8,128)(2,1)S(1)} collective-permute-done((bf16[624,256]{1,0:T(8,128)(2,1)S(1)}, bf16[624,256]{1,0:T(8,128)(2,1)S(1)}, u32[]{:S(2)}, u32[]{:S(2)}) %collective-permute-start.14) | collective-permute-done | bytes 319520 | tf_op jit(solution)/shard_map/ppermute | solution.py:564
  84.3 3.8 %prior.1 = (bf16[624,512]{1,0:T(8,128)(2,1)S(1)}, f32[624,512]{1,0:T(8,128)}, f32[624,512]{1,0:T(8,128)S(1)}, bf16[624,512]{1,0:T(8,128)(2,1)S(1)}, f32[3,512]{1,0:T(4,128)S(1)}, /*index=5*/f32[1,1024]{1,0:T(1,128)S(1)}) custom-call(s32[4]{0:T(128)S(1)} %pad_add_fusion.s, bf16[624,512]{1,0:T(8,128)(2,1)S(1)} %get-tuple-element.123.refs_0_, ...), custom_call_target="tpu_custom_call" | custom-call | tf_op jit(solution)/shard_map/prior/pallas_call | solution.py:540
  88.1 2.2 collective-permute-done.12.refs_5_
  90.2 3.5 %late_grads.1 = (f32[4,1536,128]{2,1,0:T(8,128)S(1)}, bf16[4,1536,128]{2,1,0:T(8,128)(2,1)S(1)}) custom-call(s32[4]{0:T(128)S(1)} %pad_add_fusion.s, bf16[624,512]{1,0:T(8,128)(2,1)S(1)} %get-tuple-element.123.refs_0_, bf16[624,512]{1,0:T(8,128)(2,1)S(1)} %get-tuple-element.125.refs_3_.refs_1_, ...), custom_call_target="tpu_custom_call" | custom-call | tf_op jit(solution)/shard_map/late_grads/pallas_call | solution.py:540
  93.8 6.6 %feed_back.1 = (bf16[624,2048]{1,0:T(8,128)(2,1)S(1)}, f32[624,512]{1,0:T(8,128)S(1)}, bf16[624,512]{1,0:T(8,128)(2,1)S(1)}, f32[3,512]{1,0:T(4,128)S(1)}, f32[1,2048]{1,0:T(1,128)S(1)}) custom-call(s32[4]{0:T(128)S(1)} %pad_add_fusion.s, bf16[624,512]{1,0:T(8,128)(2,1)S(1)} %get-tuple-element.131.refs_4_.refs_0_, ...), custom_call_target="tpu_custom_call" | custom-call | tf_op jit(solution)/shard_map/feed_back/pallas_call | solution.py:540
  101.2 2.4 up_grads.1
  104.2 0.9 collective-permute-start.15
  105.1 1.1 collective-permute-start.43
  106.2 15.2 %collective-permute-done.15.refs_12_ = bf16[624,512]{1,0:T(8,128)(2,1)S(1)} collective-permute-done((bf16[624,512]{1,0:T(8,128)(2,1)S(1)}, bf16[624,512]{1,0:T(8,128)(2,1)S(1)}, u32[]{:S(2)}, u32[]{:S(2)}) %collective-permute-start.15) | collective-permute-done | bytes 639008 | tf_op jit(solution)/shard_map/ppermute | solution.py:564
  121.4 21.9 %attend_back.1 = (bf16[624,1536]{1,0:T(8,128)(2,1)S(1)}, bf16[624,256]{1,0:T(8,128)(2,1)S(1)}, f32[624,256]{1,0:T(8,128)}, f32[2,512]{1,0:T(2,128)S(1)}) custom-call(s32[4]{0:T(128)S(1)} %pad_add_fusion.s, bf16[624,512]{1,0:T(8,128)(2,1)S(1)} %get-tuple-element.137.refs_0_.refs_1_, f32[624,512]{1,0:T(8,128)S(1)} %get-tuple-element.138.refs_1_, ...), custom_call_target="tpu_custom_call" | custom-call | tf_op jit(solution)/shard_map/attend_back/pallas_call | solution.py:540
  144.6 2.5 early_grads.1
  147.2 1.5 collective-permute-start.32
  150.1 11.9 %collective-permute-done.32.refs_1_ = bf16[2,1024,128]{2,1,0:T(8,128)(2,1)S(1)} collective-permute-done((bf16[2,1024,128]{2,1,0:T(8,128)(2,1)S(1)}, bf16[2,1024,128]{2,1,0:T(8,128)(2,1)S(1)}, u32[]{:S(2)}, u32[]{:S(2)}) %collective-permute-start.32) | collective-permute-done | bytes 524320 | tf_op jit(solution)/shard_map/ppermute | solution.py:564
  164.3 5.6 %collective-permute-done.44.refs_1_ = bf16[1536,128]{1,0:T(8,128)(2,1)S(1)} collective-permute-done((bf16[1536,128]{1,0:T(8,128)(2,1)S(1)}, bf16[1536,128]{1,0:T(8,128)(2,1)S(1)}, u32[]{:S(2)}, u32[]{:S(2)}) %collective-permute-start.44) | collective-permute-done | bytes 393248 | tf_op jit(solution)/shard_map/ppermute | solution.py:564
  170.7 1.6 collective-permute-start.45
  172.3 2.6 %collective-permute-start.46 = (bf16[384,128]{1,0:T(8,128)(2,1)S(1)}, bf16[384,128]{1,0:T(8,128)(2,1)S(1)}, u32[]{:S(2)}, u32[]{:S(2)}) collective-permute-start(bf16[384,128]{1,0:T(8,128)(2,1)S(1)} %get-tuple-element.190), channel_id=1, source_target_pairs={{0,16},{2,18},{4,20},{6,22},{8,24},{10,26},{12,28},{14,30},{16,0},... | collective-permute-start | bytes 294920 | tf_op jit(solution)/shard_map/ppermute | solution.py:564
  175.1 1.2 collective-permute-done.45.refs_1_
  176.3 6.2 %collective-permute-done.46.refs_2_ = bf16[384,128]{1,0:T(8,128)(2,1)S(1)} collective-permute-done((bf16[384,128]{1,0:T(8,128)(2,1)S(1)}, bf16[384,128]{1,0:T(8,128)(2,1)S(1)}, u32[]{:S(2)}, u32[]{:S(2)}) %collective-permute-start.46) | collective-permute-done | bytes 98336 | tf_op jit(solution)/shard_map/ppermute | solution.py:564
  183.2 2.5 collective-permute-start.50
  186.3 1.6 early_core.1
  187.9 1.5 collective-permute-start.20
  190.6 1.5 collective-permute-start.22
  192.2 1.0 copy-done.7
  193.2 0.9 copy-done.11
  194.8 1.4 collective-permute-start.48
  197.0 2.5 collective-permute-done.48.refs_1_
  199.5 1.0 late_join.1.refs_0_
  200.5 1.5 collective-permute-start.51
  202.0 3.0 %collective-permute-start.35 = (bf16[256,128]{1,0:T(8,128)(2,1)S(1)}, bf16[256,128]{1,0:T(8,128)(2,1)S(1)}, u32[]{:S(2)}, u32[]{:S(2)}) collective-permute-start(bf16[256,128]{1,0:T(8,128)(2,1)S(1)} %get-tuple-element.182), channel_id=1, source_target_pairs={{0,16},{2,18},{4,20},{6,22},{8,24},{10,26},{12,28},{14,30},{16,0},... | collective-permute-start | bytes 196616 | tf_op jit(solution)/shard_map/ppermute | solution.py:564
  206.5 3.7 %collective-permute-start.24 = (bf16[320,128]{1,0:T(8,128)(2,1)S(1)}, bf16[320,128]{1,0:T(8,128)(2,1)S(1)}, u32[]{:S(2)}, u32[]{:S(2)}) collective-permute-start(bf16[320,128]{1,0:T(8,128)(2,1)S(1)} %get-tuple-element.166), channel_id=1, source_target_pairs={{0,16},{2,18},{4,20},{6,22},{8,24},{10,26},{12,28},{14,30},{16,0},... | collective-permute-start | bytes 245768 | tf_op jit(solution)/shard_map/ppermute | solution.py:564
  212.4 1.1 collective-permute-start.39
  213.5 1.0 collective-permute-start.38
  214.7 2.2 collective-permute-start.37
  216.9 1.2 collective-permute-start.25
  218.5 4.7 %collective-permute-done.25.refs_3_ = bf16[320,128]{1,0:T(8,128)(2,1)S(1)} collective-permute-done((bf16[320,128]{1,0:T(8,128)(2,1)S(1)}, bf16[320,128]{1,0:T(8,128)(2,1)S(1)}, u32[]{:S(2)}, u32[]{:S(2)}) %collective-permute-start.25) | collective-permute-done | bytes 81952 | tf_op jit(solution)/shard_map/ppermute | solution.py:564
  224.3 1.3 collective-permute-start.28
  225.6 3.1 %collective-permute-start.26 = (bf16[256,128]{1,0:T(8,128)(2,1)S(1)}, bf16[256,128]{1,0:T(8,128)(2,1)S(1)}, u32[]{:S(2)}, u32[]{:S(2)}) collective-permute-start(bf16[256,128]{1,0:T(8,128)(2,1)S(1)} %get-tuple-element.168.refs_0_), channel_id=1, source_target_pairs={{0,8},{2,10},{4,12},{6,14},{8,0},{10,2},{12,4},{14,6},{16,24},{18,... | collective-permute-start | bytes 196616 | tf_op jit(solution)/shard_map/ppermute | solution.py:564
  228.8 1.7 pad_maximum_fusion
  231.2 2.2 collective-permute-done.27.refs_2_
  234.1 2.0 collective-permute-start.29
  236.3 6.3 %collective-permute-done.40.refs_1_ = bf16[1024,128]{1,0:T(8,128)(2,1)S(1)} collective-permute-done((bf16[1024,128]{1,0:T(8,128)(2,1)S(1)}, bf16[1024,128]{1,0:T(8,128)(2,1)S(1)}, u32[]{:S(2)}, u32[]{:S(2)}) %collective-permute-start.40) | collective-permute-done | bytes 262176 | tf_op jit(solution)/shard_map/ppermute | solution.py:564
  243.1 4.2 %collective-permute-done.29.refs_1_ = bf16[1024,128]{1,0:T(8,128)(2,1)S(1)} collective-permute-done((bf16[1024,128]{1,0:T(8,128)(2,1)S(1)}, bf16[1024,128]{1,0:T(8,128)(2,1)S(1)}, u32[]{:S(2)}, u32[]{:S(2)}) %collective-permute-start.29) | collective-permute-done | bytes 262176 | tf_op jit(solution)/shard_map/ppermute | solution.py:564
  247.3 1.1 pad_maximum_fusion.1
  248.4 2.5 late_place.1
  251.0 2.1 up_place.1
  253.2 2.1 early_place.1
  (128 shorter events, 23.6 us)
Async XLA Ops:
  0.7 6.0 %copy-start.16 = (s32[1200]{0:T(1024)S(1)}, s32[1200]{0:T(1024)}, u32[]{:S(2)}) copy-start(s32[1200]{0:T(1024)} %param.20) | copy-start | bytes 14404
  3.6 21.5 %collective-permute-start = (bf16[624,256]{1,0:T(8,128)(2,1)}, bf16[624,256]{1,0:T(8,128)(2,1)S(1)}, u32[]{:S(2)}, u32[]{:S(2)}) collective-permute-start(bf16[624,256]{1,0:T(8,128)(2,1)} %get-tuple-element.109), channel_id=1, source_target_pairs={{0,1},{1,0},{2,3},{3,2},{4,5},{5,4},{6,7},{7,6},{8,9},{9,8},{10,11... | collective-permute-start | bytes 958472 | tf_op jit(solution)/shard_map/ppermute | solution.py:564
  6.6 16.2 %collective-permute-start.1 = (bf16[3,512,128]{2,1,0:T(8,128)(2,1)S(1)}, bf16[3,512,128]{2,1,0:T(8,128)(2,1)S(1)}, u32[]{:S(2)}, u32[]{:S(2)}) collective-permute-start(bf16[3,512,128]{2,1,0:T(8,128)(2,1)S(1)} %get-tuple-element.111), channel_id=1, source_target_pairs={{0,1},{1,0},{2,3},{3,2},{4,5},{5,4},{6,7},{7,6},{8,9},{9,8},{10,11... | collective-permute-start | bytes 1179656 | tf_op jit(solution)/shard_map/ppermute | solution.py:564
  22.8 17.3 %collective-permute-start.3 = (bf16[512,384]{1,0:T(8,128)(2,1)S(1)}, bf16[512,384]{1,0:T(8,128)(2,1)S(1)}, u32[]{:S(2)}, u32[]{:S(2)}) collective-permute-start(bf16[512,384]{1,0:T(8,128)(2,1)S(1)} %get-tuple-element.116), channel_id=1, source_target_pairs={{0,1},{1,0},{2,3},{3,2},{4,5},{5,4},{6,7},{7,6},{8,9},{9,8},{10,11... | collective-permute-start | bytes 1179656 | tf_op jit(solution)/shard_map/ppermute | solution.py:564
  24.6 1.7 collective-permute-start.2
  24.6 15.6 %collective-permute-start.4 = (bf16[320,512]{1,0:T(8,128)(2,1)S(1)}, bf16[320,512]{1,0:T(8,128)(2,1)S(1)}, u32[]{:S(2)}, u32[]{:S(2)}) collective-permute-start(bf16[320,512]{1,0:T(8,128)(2,1)S(1)} %get-tuple-element.117), channel_id=1, source_target_pairs={{0,1},{1,0},{2,3},{3,2},{4,5},{5,4},{6,7},{7,6},{8,9},{9,8},{10,11... | collective-permute-start | bytes 983048 | tf_op jit(solution)/shard_map/ppermute | solution.py:564
  27.0 1.0 copy-start.9
  33.3 1.3 copy-start
  40.1 12.1 %collective-permute-start.8 = (bf16[512,384]{1,0:T(8,128)(2,1)S(1)}, bf16[512,384]{1,0:T(8,128)(2,1)S(1)}, u32[]{:S(2)}, u32[]{:S(2)}) collective-permute-start(bf16[512,384]{1,0:T(8,128)(2,1)S(1)} %get-tuple-element.119.refs_11_.refs_6_.refs_8_), channel_id=1, source_target_pairs={{0,4},{2,6},{4,0},{6,2},{8,12},{10,14},{12,8},{14,10},{16,20},{18,... | collective-permute-start | bytes 1179656 | tf_op jit(solution)/shard_map/ppermute | solution.py:564
  41.5 15.0 %collective-permute-start.5 = (bf16[320,512]{1,0:T(8,128)(2,1)S(1)}, bf16[320,512]{1,0:T(8,128)(2,1)S(1)}, u32[]{:S(2)}, u32[]{:S(2)}) collective-permute-start(bf16[320,512]{1,0:T(8,128)(2,1)S(1)} %get-tuple-element.118.refs_5_.refs_2_.refs_7_), channel_id=1, source_target_pairs={{0,4},{2,6},{4,0},{6,2},{8,12},{10,14},{12,8},{14,10},{16,20},{18,... | collective-permute-start | bytes 983048 | tf_op jit(solution)/shard_map/ppermute | solution.py:564
  42.2 20.0 %collective-permute-start.9 = (bf16[512,384]{1,0:T(8,128)(2,1)S(1)}, bf16[512,384]{1,0:T(8,128)(2,1)S(1)}, u32[]{:S(2)}, u32[]{:S(2)}) collective-permute-start(bf16[512,384]{1,0:T(8,128)(2,1)S(1)} %get-tuple-element.119.refs_11_.refs_6_.refs_8_), channel_id=1, source_target_pairs={{0,2},{2,0},{4,6},{6,4},{8,10},{10,8},{12,14},{14,12},{16,18},{18,... | collective-permute-start | bytes 1179656 | tf_op jit(solution)/shard_map/ppermute | solution.py:564
  52.2 10.0 %collective-permute-start.10 = (bf16[512,384]{1,0:T(8,128)(2,1)S(1)}, bf16[512,384]{1,0:T(8,128)(2,1)S(1)}, u32[]{:S(2)}, u32[]{:S(2)}) collective-permute-start(bf16[512,384]{1,0:T(8,128)(2,1)S(1)} %collective-permute-done.8.refs_12_.refs_7_.refs_10_), channel_id=1, source_target_pairs={{0,2},{2,0},{4,6},{6,4},{8,10},{10,8},{12,14},{14,12},{16,18},{18,... | collective-permute-start | bytes 1179656 | tf_op jit(solution)/shard_map/ppermute | solution.py:564
  52.2 9.1 %collective-permute-start.6 = (bf16[320,512]{1,0:T(8,128)(2,1)S(1)}, bf16[320,512]{1,0:T(8,128)(2,1)S(1)}, u32[]{:S(2)}, u32[]{:S(2)}) collective-permute-start(bf16[320,512]{1,0:T(8,128)(2,1)S(1)} %get-tuple-element.118.refs_5_.refs_2_.refs_7_), channel_id=1, source_target_pairs={{0,2},{2,0},{4,6},{6,4},{8,10},{10,8},{12,14},{14,12},{16,18},{18,... | collective-permute-start | bytes 983048 | tf_op jit(solution)/shard_map/ppermute | solution.py:564
  56.5 5.7 %collective-permute-start.7 = (bf16[320,512]{1,0:T(8,128)(2,1)S(1)}, bf16[320,512]{1,0:T(8,128)(2,1)S(1)}, u32[]{:S(2)}, u32[]{:S(2)}) collective-permute-start(bf16[320,512]{1,0:T(8,128)(2,1)S(1)} %collective-permute-done.5.refs_6_.refs_9_), channel_id=1, source_target_pairs={{0,2},{2,0},{4,6},{6,4},{8,10},{10,8},{12,14},{14,12},{16,18},{18,... | collective-permute-start | bytes 983048 | tf_op jit(solution)/shard_map/ppermute | solution.py:564
  56.5 3.6 %collective-permute-start.11 = (f32[1,1536]{1,0:T(1,128)S(1)}, f32[1,1536]{1,0:T(1,128)S(1)}, u32[]{:S(2)}, u32[]{:S(2)}) collective-permute-start(f32[1,1536]{1,0:T(1,128)S(1)} %get-tuple-element.120), channel_id=1, source_target_pairs={{0,1},{1,0},{2,3},{3,2},{4,5},{5,4},{6,7},{7,6},{8,9},{9,8},{10,11... | collective-permute-start | bytes 18440 | tf_op jit(solution)/shard_map/ppermute | solution.py:564
  60.2 24.1 %collective-permute-start.13 = (bf16[624,512]{1,0:T(8,128)(2,1)S(1)}, bf16[624,512]{1,0:T(8,128)(2,1)S(1)}, u32[]{:S(2)}, u32[]{:S(2)}) collective-permute-start(bf16[624,512]{1,0:T(8,128)(2,1)S(1)} %get-tuple-element.127), channel_id=1, source_target_pairs={{0,1},{1,0},{2,3},{3,2},{4,5},{5,4},{6,7},{7,6},{8,9},{9,8},{10,11... | collective-permute-start | bytes 1916936 | tf_op jit(solution)/shard_map/ppermute | solution.py:564
  61.3 23.0 %collective-permute-start.14 = (bf16[624,256]{1,0:T(8,128)(2,1)S(1)}, bf16[624,256]{1,0:T(8,128)(2,1)S(1)}, u32[]{:S(2)}, u32[]{:S(2)}) collective-permute-start(bf16[624,256]{1,0:T(8,128)(2,1)S(1)} %get-tuple-element.128), channel_id=1, source_target_pairs={{0,1},{1,0},{2,3},{3,2},{4,5},{5,4},{6,7},{7,6},{8,9},{9,8},{10,11... | collective-permute-start | bytes 958472 | tf_op jit(solution)/shard_map/ppermute | solution.py:564
  69.5 20.8 %collective-permute-start.12 = (bf16[624,256]{1,0:T(8,128)(2,1)S(1)}, bf16[624,256]{1,0:T(8,128)(2,1)S(1)}, u32[]{:S(2)}, u32[]{:S(2)}) collective-permute-start(bf16[624,256]{1,0:T(8,128)(2,1)S(1)} %get-tuple-element.122), channel_id=1, source_target_pairs={{0,1},{1,0},{2,3},{3,2},{4,5},{5,4},{6,7},{7,6},{8,9},{9,8},{10,11... | collective-permute-start | bytes 958472 | tf_op jit(solution)/shard_map/ppermute | solution.py:564
  93.7 6.7 %collective-permute-start.16 = (bf16[4,1536,128]{2,1,0:T(8,128)(2,1)S(1)}, bf16[4,1536,128]{2,1,0:T(8,128)(2,1)S(1)}, u32[]{:S(2)}, u32[]{:S(2)}) collective-permute-start(bf16[4,1536,128]{2,1,0:T(8,128)(2,1)S(1)} %get-tuple-element.136.refs_15_), channel_id=1, source_target_pairs={{0,2},{2,0},{4,6},{6,4},{8,10},{10,8},{12,14},{14,12},{16,18},{18,... | collective-permute-start | bytes 4718600 | tf_op jit(solution)/shard_map/ppermute | solution.py:564
  101.2 20.2 %copy-start.1 = (bf16[624,1536]{1,0:T(8,128)(2,1)S(1)}, bf16[624,1536]{1,0:T(8,128)(2,1)}, u32[]{:S(2)}) copy-start(bf16[624,1536]{1,0:T(8,128)(2,1)} %copy-done) | copy-start | bytes 5750788
  101.2 20.2 %copy-start.3 = (bf16[3,512,256]{2,1,0:T(8,128)(2,1)S(1)}, bf16[3,512,256]{2,1,0:T(8,128)(2,1)}, u32[]{:S(2)}) copy-start(bf16[3,512,256]{2,1,0:T(8,128)(2,1)} %copy-done.2) | copy-start | bytes 2359300
  103.7 39.7 %collective-permute-start.18 = (bf16[4,1024,128]{2,1,0:T(8,128)(2,1)S(1)}, bf16[4,1024,128]{2,1,0:T(8,128)(2,1)S(1)}, u32[]{:S(2)}, u32[]{:S(2)}) collective-permute-start(bf16[4,1024,128]{2,1,0:T(8,128)(2,1)S(1)} %get-tuple-element.146.refs_11_), channel_id=1, source_target_pairs={{0,2},{2,0},{4,6},{6,4},{8,10},{10,8},{12,14},{14,12},{16,18},{18,... | collective-permute-start | bytes 3145736 | tf_op jit(solution)/shard_map/ppermute | solution.py:564
  104.2 17.2 %collective-permute-start.15 = (bf16[624,512]{1,0:T(8,128)(2,1)S(1)}, bf16[624,512]{1,0:T(8,128)(2,1)S(1)}, u32[]{:S(2)}, u32[]{:S(2)}) collective-permute-start(bf16[624,512]{1,0:T(8,128)(2,1)S(1)} %get-tuple-element.130), channel_id=1, source_target_pairs={{0,1},{1,0},{2,3},{3,2},{4,5},{5,4},{6,7},{7,6},{8,9},{9,8},{10,11... | collective-permute-start | bytes 1916936 | tf_op jit(solution)/shard_map/ppermute | solution.py:564
  105.1 43.6 %collective-permute-start.43 = (bf16[2,1536,128]{2,1,0:T(8,128)(2,1)S(1)}, bf16[2,1536,128]{2,1,0:T(8,128)(2,1)S(1)}, u32[]{:S(2)}, u32[]{:S(2)}) collective-permute-start(bf16[2,1536,128]{2,1,0:T(8,128)(2,1)S(1)} %get-tuple-element.145.refs_2_), channel_id=1, source_target_pairs={{0,1},{1,0},{2,3},{3,2},{4,5},{5,4},{6,7},{7,6},{8,9},{9,8},{10,11... | collective-permute-start | bytes 2359304 | tf_op jit(solution)/shard_map/ppermute | solution.py:564
  143.4 1.2 copy-start.5
  147.1 39.2 %collective-permute-start.19 = (bf16[4,1040,128]{2,1,0:T(8,128)(2,1)S(1)}, bf16[4,1040,128]{2,1,0:T(8,128)(2,1)S(1)}, u32[]{:S(2)}, u32[]{:S(2)}) collective-permute-start(bf16[4,1040,128]{2,1,0:T(8,128)(2,1)S(1)} %get-tuple-element.159), channel_id=1, source_target_pairs={{0,2},{2,0},{4,6},{6,4},{8,10},{10,8},{12,14},{14,12},{16,18},{18,... | collective-permute-start | bytes 3194888 | tf_op jit(solution)/shard_map/ppermute | solution.py:564
  147.2 14.8 %collective-permute-start.32 = (bf16[2,1024,128]{2,1,0:T(8,128)(2,1)S(1)}, bf16[2,1024,128]{2,1,0:T(8,128)(2,1)S(1)}, u32[]{:S(2)}, u32[]{:S(2)}) collective-permute-start(bf16[2,1024,128]{2,1,0:T(8,128)(2,1)S(1)} %get-tuple-element.157.refs_9_), channel_id=1, source_target_pairs={{0,4},{2,6},{4,0},{6,2},{8,12},{10,14},{12,8},{14,10},{16,20},{18,... | collective-permute-start | bytes 1572872 | tf_op jit(solution)/shard_map/ppermute | solution.py:564
  149.5 20.5 %collective-permute-start.44 = (bf16[1536,128]{1,0:T(8,128)(2,1)S(1)}, bf16[1536,128]{1,0:T(8,128)(2,1)S(1)}, u32[]{:S(2)}, u32[]{:S(2)}) collective-permute-start(bf16[1536,128]{1,0:T(8,128)(2,1)S(1)} %get-tuple-element.187), channel_id=1, source_target_pairs={{0,4},{2,6},{4,0},{6,2},{8,12},{10,14},{12,8},{14,10},{16,20},{18,... | collective-permute-start | bytes 1179656 | tf_op jit(solution)/shard_map/ppermute | solution.py:564
  163.4 26.5 %collective-permute-start.33 = (bf16[1024,128]{1,0:T(8,128)(2,1)S(1)}, bf16[1024,128]{1,0:T(8,128)(2,1)S(1)}, u32[]{:S(2)}, u32[]{:S(2)}) collective-permute-start(bf16[1024,128]{1,0:T(8,128)(2,1)S(1)} %get-tuple-element.179), channel_id=1, source_target_pairs={{0,1},{1,0},{2,3},{3,2},{4,5},{5,4},{6,7},{7,6},{8,9},{9,8},{10,11... | collective-permute-start | bytes 786440 | tf_op jit(solution)/shard_map/ppermute | solution.py:564
  170.7 5.7 %collective-permute-start.45 = (bf16[384,128]{1,0:T(8,128)(2,1)S(1)}, bf16[384,128]{1,0:T(8,128)(2,1)S(1)}, u32[]{:S(2)}, u32[]{:S(2)}) collective-permute-start(bf16[384,128]{1,0:T(8,128)(2,1)S(1)} %get-tuple-element.189), channel_id=1, source_target_pairs={{0,8},{2,10},{4,12},{6,14},{8,0},{10,2},{12,4},{14,6},{16,24},{18,... | collective-permute-start | bytes 294920 | tf_op jit(solution)/shard_map/ppermute | solution.py:564
  172.3 10.2 %collective-permute-start.46 = (bf16[384,128]{1,0:T(8,128)(2,1)S(1)}, bf16[384,128]{1,0:T(8,128)(2,1)S(1)}, u32[]{:S(2)}, u32[]{:S(2)}) collective-permute-start(bf16[384,128]{1,0:T(8,128)(2,1)S(1)} %get-tuple-element.190), channel_id=1, source_target_pairs={{0,16},{2,18},{4,20},{6,22},{8,24},{10,26},{12,28},{14,30},{16,0},... | collective-permute-start | bytes 294920 | tf_op jit(solution)/shard_map/ppermute | solution.py:564
  174.9 7.6 %collective-permute-start.47 = (bf16[384,128]{1,0:T(8,128)(2,1)S(1)}, bf16[384,128]{1,0:T(8,128)(2,1)S(1)}, u32[]{:S(2)}, u32[]{:S(2)}) collective-permute-start(bf16[384,128]{1,0:T(8,128)(2,1)S(1)} %get-tuple-element.191), channel_id=1, source_target_pairs={{0,24},{2,26},{4,28},{6,30},{8,16},{10,18},{12,20},{14,22},{16,8},... | collective-permute-start | bytes 294920 | tf_op jit(solution)/shard_map/ppermute | solution.py:564
  183.2 11.6 %collective-permute-start.50 = (bf16[384,128]{1,0:T(8,128)(2,1)S(1)}, bf16[384,128]{1,0:T(8,128)(2,1)}, u32[]{:S(2)}, u32[]{:S(2)}) collective-permute-start(bf16[384,128]{1,0:T(8,128)(2,1)S(1)} %late_last.1.refs_0_), channel_id=1, source_target_pairs={{0,24},{2,26},{4,28},{6,30},{8,16},{10,18},{12,20},{14,22},{16,8},... | collective-permute-start | bytes 294920 | tf_op jit(solution)/shard_map/ppermute | solution.py:564
  185.7 10.5 %collective-permute-start.49 = (bf16[384,128]{1,0:T(8,128)(2,1)S(1)}, bf16[384,128]{1,0:T(8,128)(2,1)}, u32[]{:S(2)}, u32[]{:S(2)}) collective-permute-start(bf16[384,128]{1,0:T(8,128)(2,1)S(1)} %late_last.1.refs_0_), channel_id=1, source_target_pairs={{0,16},{2,18},{4,20},{6,22},{8,24},{10,26},{12,28},{14,30},{16,0},... | collective-permute-start | bytes 294920 | tf_op jit(solution)/shard_map/ppermute | solution.py:564
  187.9 14.1 %collective-permute-start.20 = (bf16[1088,128]{1,0:T(8,128)(2,1)}, bf16[1088,128]{1,0:T(8,128)(2,1)S(1)}, u32[]{:S(2)}, u32[]{:S(2)}) collective-permute-start(bf16[1088,128]{1,0:T(8,128)(2,1)} %get-tuple-element.161), channel_id=1, source_target_pairs={{0,4},{2,6},{4,0},{6,2},{8,12},{10,14},{12,8},{14,10},{16,20},{18,... | collective-permute-start | bytes 835592 | tf_op jit(solution)/shard_map/ppermute | solution.py:564
  189.4 15.6 %collective-permute-start.21 = (bf16[1088,128]{1,0:T(8,128)(2,1)}, bf16[1088,128]{1,0:T(8,128)(2,1)S(1)}, u32[]{:S(2)}, u32[]{:S(2)}) collective-permute-start(bf16[1088,128]{1,0:T(8,128)(2,1)} %get-tuple-element.162), channel_id=1, source_target_pairs={{0,1},{1,0},{2,3},{3,2},{4,5},{5,4},{6,7},{7,6},{8,9},{9,8},{10,11... | collective-permute-start | bytes 835592 | tf_op jit(solution)/shard_map/ppermute | solution.py:564
  190.6 15.1 %collective-permute-start.22 = (bf16[1088,128]{1,0:T(8,128)(2,1)}, bf16[1088,128]{1,0:T(8,128)(2,1)S(1)}, u32[]{:S(2)}, u32[]{:S(2)}) collective-permute-start(bf16[1088,128]{1,0:T(8,128)(2,1)} %get-tuple-element.163), channel_id=1, source_target_pairs={{0,5},{1,4},{2,7},{3,6},{4,1},{5,0},{6,3},{7,2},{8,13},{9,12},{10,... | collective-permute-start | bytes 835592 | tf_op jit(solution)/shard_map/ppermute | solution.py:564
  192.2 1.0 copy-start.7
  194.8 4.7 %collective-permute-start.48 = (bf16[384,128]{1,0:T(8,128)(2,1)S(1)}, bf16[384,128]{1,0:T(8,128)(2,1)S(1)}, u32[]{:S(2)}, u32[]{:S(2)}) collective-permute-start(bf16[384,128]{1,0:T(8,128)(2,1)S(1)} %late_last.1.refs_0_), channel_id=1, source_target_pairs={{0,8},{2,10},{4,12},{6,14},{8,0},{10,2},{12,4},{14,6},{16,24},{18,... | collective-permute-start | bytes 294920 | tf_op jit(solution)/shard_map/ppermute | solution.py:564
  196.2 10.3 %collective-permute-start.34 = (bf16[256,128]{1,0:T(8,128)(2,1)S(1)}, bf16[256,128]{1,0:T(8,128)(2,1)S(1)}, u32[]{:S(2)}, u32[]{:S(2)}) collective-permute-start(bf16[256,128]{1,0:T(8,128)(2,1)S(1)} %get-tuple-element.181), channel_id=1, source_target_pairs={{0,8},{2,10},{4,12},{6,14},{8,0},{10,2},{12,4},{14,6},{16,24},{18,... | collective-permute-start | bytes 196616 | tf_op jit(solution)/shard_map/ppermute | solution.py:564
  200.5 23.7 %collective-permute-start.51 = (bf16[1536,128]{1,0:T(8,128)(2,1)S(1)}, bf16[1536,128]{1,0:T(8,128)(2,1)S(1)}, u32[]{:S(2)}, u32[]{:S(2)}) collective-permute-start(bf16[1536,128]{1,0:T(8,128)(2,1)S(1)} %late_join.1.refs_0_), channel_id=1, source_target_pairs={{0,4},{2,6},{4,0},{6,2},{8,12},{10,14},{12,8},{14,10},{16,20},{18,... | collective-permute-start | bytes 1179656 | tf_op jit(solution)/shard_map/ppermute | solution.py:564
  202.0 9.1 %collective-permute-start.35 = (bf16[256,128]{1,0:T(8,128)(2,1)S(1)}, bf16[256,128]{1,0:T(8,128)(2,1)S(1)}, u32[]{:S(2)}, u32[]{:S(2)}) collective-permute-start(bf16[256,128]{1,0:T(8,128)(2,1)S(1)} %get-tuple-element.182), channel_id=1, source_target_pairs={{0,16},{2,18},{4,20},{6,22},{8,24},{10,26},{12,28},{14,30},{16,0},... | collective-permute-start | bytes 196616 | tf_op jit(solution)/shard_map/ppermute | solution.py:564
  205.0 6.8 %collective-permute-start.36 = (bf16[256,128]{1,0:T(8,128)(2,1)S(1)}, bf16[256,128]{1,0:T(8,128)(2,1)S(1)}, u32[]{:S(2)}, u32[]{:S(2)}) collective-permute-start(bf16[256,128]{1,0:T(8,128)(2,1)S(1)} %get-tuple-element.183), channel_id=1, source_target_pairs={{0,24},{2,26},{4,28},{6,30},{8,16},{10,18},{12,20},{14,22},{16,8},... | collective-permute-start | bytes 196616 | tf_op jit(solution)/shard_map/ppermute | solution.py:564
  205.7 12.4 %copy-start.14 = (f32[624,512]{1,0:T(8,128)S(1)}, f32[624,512]{1,0:T(8,128)}, u32[]{:S(2)}) copy-start(f32[624,512]{1,0:T(8,128)} %get-tuple-element.129) | copy-start | bytes 3833860
  206.5 8.2 %collective-permute-start.23 = (bf16[320,128]{1,0:T(8,128)(2,1)S(1)}, bf16[320,128]{1,0:T(8,128)(2,1)S(1)}, u32[]{:S(2)}, u32[]{:S(2)}) collective-permute-start(bf16[320,128]{1,0:T(8,128)(2,1)S(1)} %get-tuple-element.165), channel_id=1, source_target_pairs={{0,8},{2,10},{4,12},{6,14},{8,0},{10,2},{12,4},{14,6},{16,24},{18,... | collective-permute-start | bytes 245768 | tf_op jit(solution)/shard_map/ppermute | solution.py:564
  206.5 10.3 %collective-permute-start.24 = (bf16[320,128]{1,0:T(8,128)(2,1)S(1)}, bf16[320,128]{1,0:T(8,128)(2,1)S(1)}, u32[]{:S(2)}, u32[]{:S(2)}) collective-permute-start(bf16[320,128]{1,0:T(8,128)(2,1)S(1)} %get-tuple-element.166), channel_id=1, source_target_pairs={{0,16},{2,18},{4,20},{6,22},{8,24},{10,26},{12,28},{14,30},{16,0},... | collective-permute-start | bytes 245768 | tf_op jit(solution)/shard_map/ppermute | solution.py:564
  212.4 11.9 %collective-permute-start.39 = (bf16[256,128]{1,0:T(8,128)(2,1)S(1)}, bf16[256,128]{1,0:T(8,128)(2,1)S(1)}, u32[]{:S(2)}, u32[]{:S(2)}) collective-permute-start(bf16[256,128]{1,0:T(8,128)(2,1)S(1)} %up_last.1.refs_0_), channel_id=1, source_target_pairs={{0,24},{2,26},{4,28},{6,30},{8,16},{10,18},{12,20},{14,22},{16,8},... | collective-permute-start | bytes 196616 | tf_op jit(solution)/shard_map/ppermute | solution.py:564
  213.5 12.1 %collective-permute-start.38 = (bf16[256,128]{1,0:T(8,128)(2,1)S(1)}, bf16[256,128]{1,0:T(8,128)(2,1)S(1)}, u32[]{:S(2)}, u32[]{:S(2)}) collective-permute-start(bf16[256,128]{1,0:T(8,128)(2,1)S(1)} %up_last.1.refs_0_), channel_id=1, source_target_pairs={{0,16},{2,18},{4,20},{6,22},{8,24},{10,26},{12,28},{14,30},{16,0},... | collective-permute-start | bytes 196616 | tf_op jit(solution)/shard_map/ppermute | solution.py:564
  214.7 11.0 %collective-permute-start.37 = (bf16[256,128]{1,0:T(8,128)(2,1)S(1)}, bf16[256,128]{1,0:T(8,128)(2,1)S(1)}, u32[]{:S(2)}, u32[]{:S(2)}) collective-permute-start(bf16[256,128]{1,0:T(8,128)(2,1)S(1)} %up_last.1.refs_0_), channel_id=1, source_target_pairs={{0,8},{2,10},{4,12},{6,14},{8,0},{10,2},{12,4},{14,6},{16,24},{18,... | collective-permute-start | bytes 196616 | tf_op jit(solution)/shard_map/ppermute | solution.py:564
  216.9 6.2 %collective-permute-start.25 = (bf16[320,128]{1,0:T(8,128)(2,1)S(1)}, bf16[320,128]{1,0:T(8,128)(2,1)S(1)}, u32[]{:S(2)}, u32[]{:S(2)}) collective-permute-start(bf16[320,128]{1,0:T(8,128)(2,1)S(1)} %get-tuple-element.167), channel_id=1, source_target_pairs={{0,24},{2,26},{4,28},{6,30},{8,16},{10,18},{12,20},{14,22},{16,8},... | collective-permute-start | bytes 245768 | tf_op jit(solution)/shard_map/ppermute | solution.py:564
  218.1 5.0 %copy-start.13 = (bf16[624,256]{1,0:T(8,128)(2,1)S(1)}, bf16[624,256]{1,0:T(8,128)(2,1)}, u32[]{:S(2)}) copy-start(bf16[624,256]{1,0:T(8,128)(2,1)} %copy-done.12) | copy-start | bytes 958468
  223.1 13.0 %collective-permute-start.17 = (bf16[624,256]{1,0:T(8,128)(2,1)S(1)}, bf16[624,256]{1,0:T(8,128)(2,1)S(1)}, u32[]{:S(2)}, u32[]{:S(2)}) collective-permute-start(bf16[624,256]{1,0:T(8,128)(2,1)S(1)} %copy-done.13), channel_id=1, source_target_pairs={{0,1},{1,0},{2,3},{3,2},{4,5},{5,4},{6,7},{7,6},{8,9},{9,8},{10,11... | collective-permute-start | bytes 958472 | tf_op jit(solution)/shard_map/ppermute | solution.py:564
  224.2 18.4 %collective-permute-start.52 = (bf16[1536,128]{1,0:T(8,128)(2,1)S(1)}, bf16[1536,128]{1,0:T(8,128)(2,1)S(1)}, u32[]{:S(2)}, u32[]{:S(2)}) collective-permute-start(bf16[1536,128]{1,0:T(8,128)(2,1)S(1)} %late_join.1.refs_0_), channel_id=1, source_target_pairs={{0,2},{2,0},{4,6},{6,4},{8,10},{10,8},{12,14},{14,12},{16,18},{18,... | collective-permute-start | bytes 1179656 | tf_op jit(solution)/shard_map/ppermute | solution.py:564
  224.3 6.9 %collective-permute-start.28 = (bf16[256,128]{1,0:T(8,128)(2,1)S(1)}, bf16[256,128]{1,0:T(8,128)(2,1)S(1)}, u32[]{:S(2)}, u32[]{:S(2)}) collective-permute-start(bf16[256,128]{1,0:T(8,128)(2,1)S(1)} %get-tuple-element.168.refs_0_), channel_id=1, source_target_pairs={{0,24},{2,26},{4,28},{6,30},{8,16},{10,18},{12,20},{14,22},{16,8},... | collective-permute-start | bytes 196616 | tf_op jit(solution)/shard_map/ppermute | solution.py:564
  225.6 7.8 %collective-permute-start.27 = (bf16[256,128]{1,0:T(8,128)(2,1)S(1)}, bf16[256,128]{1,0:T(8,128)(2,1)S(1)}, u32[]{:S(2)}, u32[]{:S(2)}) collective-permute-start(bf16[256,128]{1,0:T(8,128)(2,1)S(1)} %get-tuple-element.168.refs_0_), channel_id=1, source_target_pairs={{0,16},{2,18},{4,20},{6,22},{8,24},{10,26},{12,28},{14,30},{16,0},... | collective-permute-start | bytes 196616 | tf_op jit(solution)/shard_map/ppermute | solution.py:564
  225.6 7.9 %collective-permute-start.26 = (bf16[256,128]{1,0:T(8,128)(2,1)S(1)}, bf16[256,128]{1,0:T(8,128)(2,1)S(1)}, u32[]{:S(2)}, u32[]{:S(2)}) collective-permute-start(bf16[256,128]{1,0:T(8,128)(2,1)S(1)} %get-tuple-element.168.refs_0_), channel_id=1, source_target_pairs={{0,8},{2,10},{4,12},{6,14},{8,0},{10,2},{12,4},{14,6},{16,24},{18,... | collective-permute-start | bytes 196616 | tf_op jit(solution)/shard_map/ppermute | solution.py:564
  230.4 5.7 %copy-start.15 = (f32[624,256]{1,0:T(8,128)S(1)}, f32[624,256]{1,0:T(8,128)}, u32[]{:S(2)}) copy-start(f32[624,256]{1,0:T(8,128)} %get-tuple-element.147) | copy-start | bytes 1916932
  231.2 17.2 %collective-permute-start.53 = (bf16[1536,128]{1,0:T(8,128)(2,1)S(1)}, bf16[1536,128]{1,0:T(8,128)(2,1)S(1)}, u32[]{:S(2)}, u32[]{:S(2)}) collective-permute-start(bf16[1536,128]{1,0:T(8,128)(2,1)S(1)} %collective-permute-done.51.refs_1_), channel_id=1, source_target_pairs={{0,2},{2,0},{4,6},{6,4},{8,10},{10,8},{12,14},{14,12},{16,18},{18,... | collective-permute-start | bytes 1179656 | tf_op jit(solution)/shard_map/ppermute | solution.py:564
  233.4 9.2 %collective-permute-start.40 = (bf16[1024,128]{1,0:T(8,128)(2,1)S(1)}, bf16[1024,128]{1,0:T(8,128)(2,1)S(1)}, u32[]{:S(2)}, u32[]{:S(2)}) collective-permute-start(bf16[1024,128]{1,0:T(8,128)(2,1)S(1)} %up_join.1.refs_0_), channel_id=1, source_target_pairs={{0,4},{2,6},{4,0},{6,2},{8,12},{10,14},{12,8},{14,10},{16,20},{18,... | collective-permute-start | bytes 786440 | tf_op jit(solution)/shard_map/ppermute | solution.py:564
  234.1 13.2 %collective-permute-start.29 = (bf16[1024,128]{1,0:T(8,128)(2,1)S(1)}, bf16[1024,128]{1,0:T(8,128)(2,1)S(1)}, u32[]{:S(2)}, u32[]{:S(2)}) collective-permute-start(bf16[1024,128]{1,0:T(8,128)(2,1)S(1)} %early_join.1.refs_0_), channel_id=1, source_target_pairs={{0,4},{2,6},{4,0},{6,2},{8,12},{10,14},{12,8},{14,10},{16,20},{18,... | collective-permute-start | bytes 786440 | tf_op jit(solution)/shard_map/ppermute | solution.py:564
  236.2 14.8 %collective-permute-start.41 = (bf16[1024,128]{1,0:T(8,128)(2,1)S(1)}, bf16[1024,128]{1,0:T(8,128)(2,1)S(1)}, u32[]{:S(2)}, u32[]{:S(2)}) collective-permute-start(bf16[1024,128]{1,0:T(8,128)(2,1)S(1)} %up_join.1.refs_0_), channel_id=1, source_target_pairs={{0,2},{2,0},{4,6},{6,4},{8,10},{10,8},{12,14},{14,12},{16,18},{18,... | collective-permute-start | bytes 786440 | tf_op jit(solution)/shard_map/ppermute | solution.py:564
  242.6 8.4 %collective-permute-start.42 = (bf16[1024,128]{1,0:T(8,128)(2,1)S(1)}, bf16[1024,128]{1,0:T(8,128)(2,1)S(1)}, u32[]{:S(2)}, u32[]{:S(2)}) collective-permute-start(bf16[1024,128]{1,0:T(8,128)(2,1)S(1)} %collective-permute-done.40.refs_1_), channel_id=1, source_target_pairs={{0,2},{2,0},{4,6},{6,4},{8,10},{10,8},{12,14},{14,12},{16,18},{18,... | collective-permute-start | bytes 786440 | tf_op jit(solution)/shard_map/ppermute | solution.py:564
  242.6 10.5 %collective-permute-start.30 = (bf16[1024,128]{1,0:T(8,128)(2,1)S(1)}, bf16[1024,128]{1,0:T(8,128)(2,1)S(1)}, u32[]{:S(2)}, u32[]{:S(2)}) collective-permute-start(bf16[1024,128]{1,0:T(8,128)(2,1)S(1)} %early_join.1.refs_0_), channel_id=1, source_target_pairs={{0,2},{2,0},{4,6},{6,4},{8,10},{10,8},{12,14},{14,12},{16,18},{18,... | collective-permute-start | bytes 786440 | tf_op jit(solution)/shard_map/ppermute | solution.py:564
  247.3 5.9 %collective-permute-start.31 = (bf16[1024,128]{1,0:T(8,128)(2,1)S(1)}, bf16[1024,128]{1,0:T(8,128)(2,1)S(1)}, u32[]{:S(2)}, u32[]{:S(2)}) collective-permute-start(bf16[1024,128]{1,0:T(8,128)(2,1)S(1)} %collective-permute-done.29.refs_1_), channel_id=1, source_target_pairs={{0,2},{2,0},{4,6},{6,4},{8,10},{10,8},{12,14},{14,12},{16,18},{18,... | collective-permute-start | bytes 786440 | tf_op jit(solution)/shard_map/ppermute | solution.py:564
  (7 other events, 5.7 us)
